TPU v7x, 256 devices: a whole 4x4x8 slice. The times are simulated.
256 devices in a mesh: rep: 8 (over x_lo, y), blk: 32 (over z, x_hi, core).
Axes of the slice: x: 4 (x_hi: 2, x_lo: 2; x = x_hi * 2 + x_lo), y: 4, z: 8, core: 2. Of those that a mesh axis runs over, the one named last changes fastest.
Arguments:
- features: bfloat16 [32, 4096, 128], P('blk', 'rep'), may hold values from -6 to 6
- weight: bfloat16 [128, 256], replicated, may hold values from -0.5 to 0.5
- cotangent: bfloat16 [32, 4096, 256], P('blk', 'rep'), may hold values from -6 to 6
- self_weight: float32 [32, 4096], P('blk', 'rep'), may hold values from 0.3 to 1.5
- block_rows: int32 [8, 32, 384], P('rep', 'blk'), may hold values from 0 to 127, as said below
- block_cols: int32 [8, 32, 384], P('rep', 'blk'), may hold values from 0 to 31, as said below
- block_counts: int32 [8, 32], P('rep', 'blk'), may hold values from 1 to 384, as said below
- block_values: bfloat16 [8, 32, 384, 128, 128], P('rep', 'blk'), as said below
Outputs:
- activated: bfloat16 [32, 4096, 256], P('blk', 'rep')
- feature_grad: bfloat16 [32, 4096, 128], P('blk', 'rep')
- weight_grad: float32 [128, 256], P('rep')
Inputs may be any that keep to these rules, and one draw needn't show every extreme that they name: `block_counts`: one device of every draw has all 384 slots live. `block_rows`: the live slots of one device name distinct (row tile, column tile) pairs; slots past the count hold 0. `block_cols`: slots past the count hold 0. `block_values`: slots at or past a device's count hold zeros.
All inputs are finite; a program needn't handle non-finite values.
Results may differ from a plain program's by a relative error of at most 0.024.
Values may be sent and summed in bfloat16 or wider, within the bound.
No kernel may reach another device: no remote copies, remote signals or barrier semaphores. Data moves between devices by JAX's collectives and lax.ppermute only.
A program may use at most 128 MiB of HBM per device.

v0:
```python
import math

import jax
import jax.numpy as jnp
from jax import lax
from jax.sharding import PartitionSpec as P

group_slots = 32


def silu_slope(pre_act):
    sigma = jax.nn.sigmoid(pre_act)
    return sigma * (1.0 + pre_act * (1.0 - sigma))


def tile_products(tile_values, row_index, col_index, live_count, source, targets, flipped):
    feat_width = source.shape[-1]
    tile_side = tile_values.shape[-1]
    start_sums = jnp.zeros((targets, tile_side, feat_width), jnp.float32)
    turn_count = (live_count + group_slots - 1) // group_slots

    def one_group(step_index, summed):
        first_slot = step_index * group_slots
        tile_block = lax.dynamic_slice_in_dim(tile_values, first_slot, group_slots, 0)
        rows_here = lax.dynamic_slice_in_dim(row_index, first_slot, group_slots, 0)
        cols_here = lax.dynamic_slice_in_dim(col_index, first_slot, group_slots, 0)
        is_live = (first_slot + jnp.arange(group_slots, dtype=jnp.int32) < live_count).astype(
            jnp.float32
        )
        if flipped:
            picked = source[rows_here]
            products = jnp.einsum(
                "gji,gjf->gif", tile_block, picked, preferred_element_type=jnp.float32
            )
            landing = cols_here
        else:
            picked = source[cols_here]
            products = jnp.einsum(
                "gij,gjf->gif", tile_block, picked, preferred_element_type=jnp.float32
            )
            landing = rows_here
        return summed.at[landing].add(products * is_live[:, None, None])

    return lax.fori_loop(0, turn_count, one_group, start_sums)


def on_device(
    features, weight, cotangent, self_weight, block_rows, block_cols, block_counts, block_values
):
    rows_dev = features.shape[1]
    feat_width = features.shape[2]
    tile_side = block_values.shape[-1]
    blk_count = lax.axis_size("blk")
    rep_count = lax.axis_size("rep")
    tile_values = block_values[0, 0]
    row_index = block_rows[0, 0]
    col_index = block_cols[0, 0]
    live_count = block_counts[0, 0]
    row_tiles = blk_count * rows_dev // tile_side
    col_tiles = rep_count * rows_dev // tile_side
    panel = lax.all_gather(features, "rep", axis=1, tiled=True)
    panel_tiles = panel.reshape(col_tiles, tile_side, feat_width)
    own_scale = self_weight[0][:, None]
    forward_terms = tile_products(
        tile_values, row_index, col_index, live_count, panel_tiles, row_tiles, False
    )
    forward_terms = forward_terms.reshape(blk_count, rows_dev, feat_width)
    summed_rows = lax.psum_scatter(
        forward_terms.astype(jnp.bfloat16), "blk", scatter_dimension=0, tiled=True
    ).astype(jnp.float32)[0]
    aggregated = (summed_rows + own_scale * features[0].astype(jnp.float32)).astype(jnp.bfloat16)
    pre_act = jnp.dot(aggregated, weight, preferred_element_type=jnp.float32)
    activated = jax.nn.silu(pre_act).astype(jnp.bfloat16)
    slope = (cotangent[0].astype(jnp.float32) * silu_slope(pre_act)).astype(jnp.bfloat16)
    node_total = blk_count * rep_count * rows_dev
    weight_part = jnp.einsum(
        "nf,nh->fh", aggregated, slope, preferred_element_type=jnp.float32
    ) / math.sqrt(node_total)
    row_grad = lax.dot_general(
        slope, weight, (((1,), (1,)), ((), ())), preferred_element_type=jnp.float32
    ).astype(jnp.bfloat16)
    all_grads = lax.all_gather(row_grad[None], "blk", axis=0, tiled=True)
    grad_tiles = all_grads.reshape(row_tiles, tile_side, feat_width)
    backward_terms = tile_products(
        tile_values, row_index, col_index, live_count, grad_tiles, col_tiles, True
    )
    backward_terms = backward_terms.reshape(1, rep_count * rows_dev, feat_width)
    own_grad = own_scale * row_grad.astype(jnp.float32)
    column_part = lax.psum_scatter(
        backward_terms.astype(jnp.bfloat16), "rep", scatter_dimension=1, tiled=True
    ).astype(jnp.float32)
    weight_full = lax.psum(weight_part, ("rep", "blk"))
    share_rows = weight_full.shape[0] // rep_count
    weight_grad = lax.dynamic_slice_in_dim(
        weight_full, lax.axis_index("rep") * share_rows, share_rows, 0
    )
    feature_grad = (column_part[0] + own_grad).astype(jnp.bfloat16)
    return (activated[None], feature_grad[None], weight_grad)


def solution(mesh):
    placed = (
        P("blk", "rep", None),
        P(),
        P("blk", "rep", None),
        P("blk", "rep"),
        P("rep", "blk", None),
        P("rep", "blk", None),
        P("rep", "blk"),
        P("rep", "blk", None, None, None),
    )
    return jax.shard_map(
        on_device,
        mesh=mesh,
        in_specs=placed,
        out_specs=(P("blk", "rep", None), P("blk", "rep", None), P("rep", None)),
        check_vma=False,
    )
```

profile of v0, /device:TPU:1, one launch (start us, length us, event | category | flops | bytes accessed | tf_op | source)
XLA Modules:
  0.0 693.2 jit_solution(6397314962938212612)
XLA Ops:
  7.2 0.7 all-gather.4.cloned.1.call-update
  7.9 0.0 reduce-scatter.3.cloned.1.call-start
  8.6 0.7 reduce
  9.3 0.7 reduce.1
  10.0 40.2 %all-gather.4.cloned.1.call-done = bf16[1,4096,128]{2,1,0:T(8,128)(2,1)} async-done(((bf16[1,512,128]{2,1,0:T(8,128)(2,1)}), bf16[1,4096,128]{2,1,0:T(8,128)(2,1)}) %all-gather.4.cloned.1.call-update) | async-done | bytes 1048592 | tf_op jit(solution)/shard_map/all_gather | solution.py:61
  50.2 4.3 broadcast_in_dim.29
  54.5 43.3 %while.20 = (s32[]{:T(128)}, f32[128,128,128]{2,1,0:T(8,128)}, s32[]{:T(128)}, s32[384]{0:T(512)S(1)}, bf16[384,128,128]{2,1,0:T(8,128)(2,1)}, /*index=5*/s32[38...) while((s32[]{:T(128)}, f32[128,128,128]{2,1,0:T(8,128)}, ...), condition=%wide.region_2.3_spmd, body=%wide.region_0.2_spmd.sunk | while | flops 135267616 | bytes 12588339 | solution.py:44
  54.5 0.6 compare_convert_fusion.4
  55.1 0.1 compare_select_fusion.6
  55.2 2.0 gather_fusion
  57.2 1.7 convolution_multiply_fusion.5
  58.9 6.2 scatter_fusion
  65.1 0.6 compare_convert_fusion.4
  65.8 0.1 compare_select_fusion.6
  65.9 2.0 gather_fusion
  67.8 1.7 convolution_multiply_fusion.5
  69.5 6.3 scatter_fusion
  75.8 0.6 compare_convert_fusion.4
  76.4 0.1 compare_select_fusion.6
  76.5 2.0 gather_fusion
  78.5 1.7 convolution_multiply_fusion.5
  80.2 6.2 scatter_fusion
  86.4 0.6 compare_convert_fusion.4
  87.1 0.1 compare_select_fusion.6
  87.2 2.0 gather_fusion
  89.1 1.7 convolution_multiply_fusion.5
  90.8 7.0 %scatter_fusion = f32[128,128,128]{2,1,0:T(8,128)} fusion(f32[128,128,128]{2,1,0:T(8,128)} %get-tuple-element.258, s32[32]{0:T(128)S(1)} %get-tuple-element.233, f32[32,128,128]{2,1,0:T(8,128)S(1)} %convolution_multiply_fusion.5), kind=kCustom, calls=%fused_computation.2.clone.1 | custom fusion | flops 524288 | bytes 6291584 | tf_op jit(solution)/shard_map/while/body/scatter-add | solution.py:42
  97.8 6.3 convert_element_type.66
  104.1 0.0 all-gather.6.cloned.1.call-start
  104.2 206.5 %reduce-scatter.3.cloned.1.call-done = bf16[1,512,128]{2,1,0:T(8,128)(2,1)} async-done(((bf16[32,512,128]{2,1,0:T(8,128)(2,1)}), bf16[1,512,128]{2,1,0:T(8,128)(2,1)}) %reduce-scatter.3.cloned.1.call-update) | async-done | bytes 131088 | tf_op jit(solution)/shard_map/reduce_scatter | solution.py:68
  310.6 2.1 fusion.4
  312.7 0.9 convolution_convert_fusion
  313.6 0.0 all-reduce.2.cloned.1.call-start
  313.7 16.7 %copy.11 = bf16[1,1,384,128,128]{3,4,2,1,0:T(8,128)(2,1)} copy(bf16[1,1,384,128,128]{4,3,2,1,0:T(8,128)(2,1)} %bitcast.44) | data formatting | bytes 25165824 | tf_op args[7]
  330.3 1.0 convolution_multiply_fusion.2
  331.3 0.0 reduce-scatter.5.cloned.1.call-start
  331.4 73.3 %all-gather.6.cloned.1.call-done = bf16[16384,128]{1,0:T(8,128)(2,1)} async-done(((bf16[512,128]{1,0:T(8,128)(2,1)}), bf16[16384,128]{1,0:T(8,128)(2,1)}) %all-gather.6.cloned.1.call-update) | async-done | bytes 4194320 | tf_op jit(solution)/shard_map/all_gather | solution.py:82
  404.7 1.6 broadcast_in_dim.31
  406.2 46.8 %while.21 = (s32[]{:T(128)}, f32[32,128,128]{2,1,0:T(8,128)}, s32[]{:T(128)}, s32[384]{0:T(512)S(1)}, bf16[384,128,128]{1,2,0:T(8,128)(2,1)}, /*index=5*/s32[384...) while((s32[]{:T(128)}, f32[32,128,128]{2,1,0:T(8,128)}, ...), condition=%wide.region_6.7_spmd, body=%wide.region_4.6_spmd.sunk | while | flops 135267616 | bytes 12588339 | solution.py:44
  406.3 0.6 compare_convert_fusion.5
  406.9 0.1 compare_select_fusion.7
  407.0 2.9 gather_fusion.1
  409.9 1.7 convolution_multiply_fusion.6
  411.6 6.1 scatter_fusion.1
  417.7 0.6 compare_convert_fusion.5
  418.4 0.1 compare_select_fusion.7
  418.5 2.9 gather_fusion.1
  421.4 1.7 convolution_multiply_fusion.6
  423.1 6.2 scatter_fusion.1
  429.3 0.6 compare_convert_fusion.5
  429.9 0.1 compare_select_fusion.7
  430.0 2.9 gather_fusion.1
  433.0 1.7 convolution_multiply_fusion.6
  434.6 6.1 scatter_fusion.1
  440.7 0.6 compare_convert_fusion.5
  441.4 0.1 compare_select_fusion.7
  441.5 3.0 gather_fusion.1
  444.4 1.7 convolution_multiply_fusion.6
  446.1 7.0 %scatter_fusion.1 = f32[32,128,128]{2,1,0:T(8,128)} fusion(f32[32,128,128]{2,1,0:T(8,128)} %get-tuple-element.294, s32[32]{0:T(128)S(1)} %get-tuple-element.243, f32[32,128,128]{2,1,0:T(8,128)S(1)} %convolution_multiply_fusion.6), kind=kCustom, calls=%fused_computation.3.clone.1 | custom fusion | flops 524288 | bytes 6291584 | tf_op jit(solution)/shard_map/while/body/scatter-add | solution.py:42
  453.1 2.8 convert_element_type.76
  455.9 192.1 %all-reduce.2.cloned.1.call-done = f32[128,256]{1,0:T(8,128)} async-done(((f32[128,256]{1,0:T(8,128)}), f32[128,256]{1,0:T(8,128)}) %all-reduce.2.cloned.1.call-update) | async-done | bytes 131088 | tf_op jit(solution)/shard_map/psum | solution.py:92
  648.0 1.3 constant_dynamic-slice_fusion
  649.3 35.6 %reduce-scatter.5.cloned.1.call-done = bf16[1,512,128]{2,1,0:T(8,128)(2,1)} async-done(((bf16[1,4096,128]{2,1,0:T(8,128)(2,1)}), bf16[1,512,128]{2,1,0:T(8,128)(2,1)}) %reduce-scatter.5.cloned.1.call-update) | async-done | bytes 131088 | tf_op jit(solution)/shard_map/reduce_scatter | solution.py:89
  684.9 1.7 fusion.9
  (25 shorter events, 0.2 us)
Async XLA Ops:
  7.2 303.5 %copy-start = (bf16[128,256]{1,0:T(8,128)(2,1)S(1)}, bf16[128,256]{1,0:T(8,128)(2,1)}, u32[]{:S(2)}) copy-start(bf16[128,256]{1,0:T(8,128)(2,1)} %param.13) | copy-start | bytes 196612
  7.2 43.0 %all-gather.4.cloned.1.call-start = ((), (), s32[]{:S(2)}) async-start(), calls=%async_computation.2 | async-start | bytes 1179648 | tf_op jit(solution)/shard_map/all_gather | solution.py:61
  7.9 302.7 %reduce-scatter.3.cloned.1.call-start = ((), (), s32[]{:S(2)}) async-start(), calls=%async_computation.3 | async-start | bytes 4325376 | tf_op jit(solution)/shard_map/reduce_scatter | solution.py:68
  104.1 206.6 %copy-start.2 = (bf16[1,512,128]{2,1,0:T(8,128)(2,1)S(1)}, bf16[1,512,128]{2,1,0:T(8,128)(2,1)}, u32[]{:S(2)}) copy-start(bf16[1,512,128]{2,1,0:T(8,128)(2,1)} %param.12) | copy-start | bytes 393220
  104.1 206.6 %copy-start.4 = (f32[1,512]{1,0:T(1,128)S(1)}, f32[1,512]{1,0:T(1,128)}, u32[]{:S(2)}) copy-start(f32[1,512]{1,0:T(1,128)} %param.15) | copy-start | bytes 6148
  104.1 206.6 %copy-start.5 = (bf16[1,512,256]{2,1,0:T(8,128)(2,1)S(1)}, bf16[1,512,256]{2,1,0:T(8,128)(2,1)}, u32[]{:S(2)}) copy-start(bf16[1,512,256]{2,1,0:T(8,128)(2,1)} %param.14) | copy-start | bytes 786436
  104.1 300.6 %all-gather.6.cloned.1.call-start = ((), (), s32[]{:S(2)}) async-start(), calls=%async_computation.6 | async-start | bytes 4325376 | tf_op jit(solution)/shard_map/all_gather | solution.py:82
  313.6 334.4 %all-reduce.2.cloned.1.call-start = ((), (), s32[]{:S(2)}) async-start(), calls=%async_computation.5 | async-start | bytes 262144 | tf_op jit(solution)/shard_map/psum | solution.py:92
  313.6 16.7 %copy-start.3 = (bf16[1,512,128]{2,1,0:T(8,128)(2,1)S(1)}, bf16[1,512,128]{2,1,0:T(8,128)(2,1)}, u32[]{:S(2)}) copy-start(bf16[1,512,128]{2,1,0:T(8,128)(2,1)} %reduce-scatter.3.cloned.1.call-done) | copy-start | bytes 393220
  331.3 353.6 %reduce-scatter.5.cloned.1.call-start = ((), (), s32[]{:S(2)}) async-start(), calls=%async_computation.4 | async-start | bytes 1179648 | tf_op jit(solution)/shard_map/reduce_scatter | solution.py:89
  453.1 231.8 %copy-start.1 = (bf16[512,128]{1,0:T(8,128)(2,1)S(1)}, bf16[512,128]{1,0:T(8,128)(2,1)}, u32[]{:S(2)}) copy-start(bf16[512,128]{1,0:T(8,128)(2,1)} %convolution_convert_fusion) | copy-start | bytes 393220
Sparse Core Ops, SparseCore 0:
  9.8 40.3 all-gather.3
  104.2 206.3 reduce-scatter.2
  314.4 90.2 all-gather.5
  410.9 237.0 all-reduce.1
  650.5 34.3 reduce-scatter.4
where the time goes:
time: 703 us; the launch traced here: 693 us
  waiting for transfers between devices  548 us (78%)
  other arithmetic  69.2 us (10%)
  local copies, waits for them, and re-layouts  43.5 us (6%)
  matrix products  17.2 us (2%)
  between operations  14.5 us (2%)
    reduce_scatter x1, waiting for transfers between devices, on_device(): lax.psum_scatter(forward_terms.astype(jnp.bfloat16), 'blk', scatter_dimen...  206 us
    psum x1, waiting for transfers between devices, on_device(): weight_full = lax.psum(weight_part, ('rep', 'blk'))  192 us
    all_gather x1, waiting for transfers between devices, on_device(): all_grads = lax.all_gather(row_grad[None], 'blk', axis=0, tiled=True)  73.3 us
    scatter-add x8, other arithmetic, one_group(): return summed.at[landing].add(products * is_live[:, None, None])  51.1 us
    all_gather x1, waiting for transfers between devices, on_device(): panel = lax.all_gather(features, 'rep', axis=1, tiled=True)  40.2 us
    reduce_scatter x1, waiting for transfers between devices, on_device(): lax.psum_scatter(backward_terms.astype(jnp.bfloat16), 'rep', scatter_dime...  35.6 us
    unnamed x13, local copies, waits for them, and re-layouts  16.7 us
  transfers between devices with their start and end apart: 5, of which 5 were waited for; matrix products, arithmetic and copies ran while one was open for 10% of the time, Pallas kernels for 0%

commit v1 on v0

v1 whole, which is shorter than its diff:
```python
import math

import jax
import jax.numpy as jnp
from jax import lax
from jax.experimental import pallas as pl
from jax.experimental.pallas import tpu as pltpu
from jax.sharding import Mesh
from jax.sharding import PartitionSpec as P

AXES = ("xl", "y", "z", "xh", "c")
SIZES = (2, 4, 8, 2, 2)
REP = ("xl", "y")
BLK = ("z", "xh", "c")
NZ = 8
BS = 128
GROUP = 32
BUFFERS = 4


def _pairs(move):
    pairs = []
    for xl in range(2):
        for y in range(4):
            for z in range(8):
                for xh in range(2):
                    for c in range(2):
                        src = (xl, y, z, xh, c)
                        flat = []
                        for at in (src, move(*src)):
                            index = 0
                            for size, value in zip(SIZES, at):
                                index = index * size + value
                            flat.append(index)
                        pairs.append(tuple(flat))
    return pairs


def z_shift(k):
    return _pairs(lambda xl, y, z, xh, c: (xl, y, (z + k) % 8, xh, c))


def z_flip(k):
    return _pairs(lambda xl, y, z, xh, c: (xl, y, z ^ k, xh, c))


CORE_SWAP = _pairs(lambda xl, y, z, xh, c: (xl, y, z, xh, 1 - c))
X_SWAP = _pairs(lambda xl, y, z, xh, c: (xl, y, z, 1 - xh, c))


def send(value, pairs):
    return lax.ppermute(value, AXES, pairs)


def stream_tiles(count, tiles_ref, buf, sems, use):
    groups = (count + GROUP - 1) // GROUP

    def copy(group, slot):
        return pltpu.make_async_copy(
            tiles_ref.at[pl.ds(group * GROUP, GROUP)], buf.at[slot], sems.at[slot]
        )

    for first in range(BUFFERS - 1):

        @pl.when(first < groups)
        def _():
            copy(first, first).start()

    def one_group(group, carry):
        slot = lax.rem(group, BUFFERS)
        copy(group, slot).wait()

        @pl.when(group + BUFFERS - 1 < groups)
        def _():
            copy(group + BUFFERS - 1, lax.rem(group + BUFFERS - 1, BUFFERS)).start()

        for j in range(GROUP):
            use(group * GROUP + j, slot, j)
        return carry

    return lambda: lax.fori_loop(0, groups, one_group, 0)


def forward_kernel(
    land_ref, cols_ref, count_ref, panel_ref, tiles_ref, keep_ref, away_ref, acc, buf, sems
):
    def use(s, slot, j):
        acc[land_ref[s]] += jnp.dot(
            buf[slot, j], panel_ref[cols_ref[s]], preferred_element_type=jnp.float32
        )

    run = stream_tiles(count_ref[0], tiles_ref, buf, sems, use)
    acc[...] = jnp.zeros_like(acc)
    run()
    half = acc.shape[0] // 2
    keep_ref[...] = acc[:half].astype(jnp.bfloat16)
    away_ref[...] = acc[half:].astype(jnp.bfloat16)


def forward_products(land, cols, count, panel, tiles):
    smem = pl.BlockSpec(memory_space=pltpu.SMEM)
    vmem = pl.BlockSpec(memory_space=pltpu.VMEM)
    half = jax.ShapeDtypeStruct((64, BS, BS), jnp.bfloat16)
    return pl.pallas_call(
        forward_kernel,
        out_shape=(half, half),
        in_specs=[smem, smem, smem, vmem, pl.BlockSpec(memory_space=pl.ANY)],
        out_specs=(vmem, vmem),
        scratch_shapes=[
            pltpu.VMEM((128, BS, BS), jnp.float32),
            pltpu.VMEM((BUFFERS, GROUP, BS, BS), jnp.bfloat16),
            pltpu.SemaphoreType.DMA((BUFFERS,)),
        ],
        compiler_params=pltpu.CompilerParams(vmem_limit_bytes=40 << 20),
        cost_estimate=pl.CostEstimate(
            flops=384 * 2 * BS**3, bytes_accessed=18 << 20, transcendentals=0
        ),
        name="forward_products",
    )(land, cols, count, panel, tiles)


def backward_kernel(
    land_ref, cols_ref, count_ref, *refs
):
    piece_refs = refs[:-6]
    tiles_ref, out_ref, acc, buf, grads, sems = refs[-6:]

    def use(s, slot, j):
        acc[cols_ref[s]] += lax.dot_general(
            buf[slot, j],
            grads[land_ref[s]],
            (((0,), (0,)), ((), ())),
            preferred_element_type=jnp.float32,
        )

    copies = []
    at = 0
    for i, ref in enumerate(piece_refs):
        size = ref.shape[0]
        copies.append(
            pltpu.make_async_copy(ref, grads.at[pl.ds(at, size)], sems.at[BUFFERS + i])
        )
        at += size
    for one in copies:
        one.start()
    run = stream_tiles(count_ref[0], tiles_ref, buf, sems, use)
    acc[...] = jnp.zeros_like(acc)
    for one in copies:
        one.wait()
    run()
    out_ref[...] = acc[...].astype(jnp.bfloat16)


def backward_products(land, cols, count, pieces, tiles):
    smem = pl.BlockSpec(memory_space=pltpu.SMEM)
    vmem = pl.BlockSpec(memory_space=pltpu.VMEM)
    hbm = pl.BlockSpec(memory_space=pl.ANY)
    return pl.pallas_call(
        backward_kernel,
        out_shape=jax.ShapeDtypeStruct((32, BS, BS), jnp.bfloat16),
        in_specs=[smem, smem, smem] + [hbm] * (len(pieces) + 1),
        out_specs=vmem,
        scratch_shapes=[
            pltpu.VMEM((32, BS, BS), jnp.float32),
            pltpu.VMEM((BUFFERS, GROUP, BS, BS), jnp.bfloat16),
            pltpu.VMEM((128, BS, BS), jnp.bfloat16),
            pltpu.SemaphoreType.DMA((BUFFERS + len(pieces),)),
        ],
        compiler_params=pltpu.CompilerParams(vmem_limit_bytes=40 << 20),
        cost_estimate=pl.CostEstimate(
            flops=384 * 2 * BS**3, bytes_accessed=18 << 20, transcendentals=0
        ),
        name="backward_products",
    )(land, cols, count, *pieces, tiles)


def add_pair(a, b):
    return (a.astype(jnp.float32) + b.astype(jnp.float32)).astype(jnp.bfloat16)


def dense(summed, scale, features, weight, cotangent):
    aggregated = (summed + scale * features.astype(jnp.float32)).astype(jnp.bfloat16)
    pre_act = jnp.dot(aggregated, weight, preferred_element_type=jnp.float32)
    sigma = jax.nn.sigmoid(pre_act)
    activated = (pre_act * sigma).astype(jnp.bfloat16)
    slope = (
        cotangent.astype(jnp.float32) * (sigma * (1.0 + pre_act * (1.0 - sigma)))
    ).astype(jnp.bfloat16)
    weight_part = lax.dot_general(
        aggregated, slope, (((0,), (0,)), ((), ())), preferred_element_type=jnp.float32
    )
    row_grad = lax.dot_general(
        slope, weight, (((1,), (1,)), ((), ())), preferred_element_type=jnp.float32
    ).astype(jnp.bfloat16)
    return activated, weight_part, row_grad


def on_device(
    features, weight, cotangent, self_weight, block_rows, block_cols, block_counts, block_values
):
    tiles = block_values[0, 0]
    rows = block_rows[0, 0]
    cols = block_cols[0, 0]
    count = block_counts[0]
    z = lax.axis_index("z")
    xh = lax.axis_index("xh")
    c = lax.axis_index("c")
    panel_at = rows // 4
    q = rows % 4
    half, low = q // 2, q % 2
    row_z, row_x, row_c = panel_at // 4, (panel_at // 2) % 2, panel_at % 2
    rel_c, rel_x = row_c ^ c, row_x ^ xh
    rel_out = (row_z - z) % NZ
    rel_in = (z - row_z) % NZ
    land_fwd = (((rel_c * 2 + half) * 2 + rel_x) * NZ + rel_out) * 2 + low
    land_bwd = (
        rel_c * 64
        + half * 32
        + jnp.where(half == 0, rel_in * 4 + rel_x * 2, rel_x * 16 + rel_in * 2)
        + low
    )

    panel = lax.all_to_all(jnp.broadcast_to(features, (8, 512, BS)), REP, 0, 0)
    keep, away = forward_products(land_fwd, cols, count, panel.reshape(32, BS, BS), tiles)
    summed = add_pair(keep, send(away, CORE_SWAP)).reshape(2, 2, NZ, 256, BS)

    first = add_pair(summed[0, 0], send(summed[0, 1], X_SWAP))
    total_a = first[0].astype(jnp.float32)
    for k in range(1, NZ):
        total_a = total_a + send(first[k], z_shift(k)).astype(jnp.float32)
    second = summed[1]
    total_b = second[:, 0].astype(jnp.float32)
    for k in range(1, NZ):
        total_b = total_b + send(second[:, k], z_shift(k)).astype(jnp.float32)
    total_b = total_b[0] + send(total_b[1].astype(jnp.bfloat16), X_SWAP).astype(jnp.float32)

    scale = self_weight[0][:, None]
    act_a, weight_a, grad_a = dense(
        total_a, scale[:256], features[0, :256], weight, cotangent[0, :256]
    )
    act_b, weight_b, grad_b = dense(
        total_b, scale[256:], features[0, 256:], weight, cotangent[0, 256:]
    )
    activated = jnp.concatenate([act_a, act_b], 0)[None]

    pair = jnp.stack([grad_a, send(grad_a, X_SWAP)])
    got_a = jnp.stack([pair] + [send(pair, z_shift(k)) for k in range(1, NZ)])
    got_b = jnp.stack([grad_b] + [send(grad_b, z_shift(k)) for k in range(1, NZ)])
    got_bx = send(got_b, X_SWAP)
    pieces = [got_a, got_b, got_bx]
    pieces = pieces + [send(piece, CORE_SWAP) for piece in pieces]
    pieces = [piece.reshape(-1, BS, BS) for piece in pieces]
    columns = backward_products(land_bwd, cols, count, pieces, tiles)
    parts = lax.all_to_all(columns.reshape(8, 512, BS), REP, 0, 0)
    row_grad = jnp.concatenate([grad_a, grad_b], 0)
    feature_grad = (
        jnp.sum(parts.astype(jnp.float32), 0) + scale * row_grad.astype(jnp.float32)
    ).astype(jnp.bfloat16)[None]

    node_total = 32 * 8 * 512
    weight_sum = (weight_a + weight_b) * (1.0 / math.sqrt(node_total))
    weight_sum = jnp.sum(lax.all_to_all(weight_sum.reshape(8, 16, 256), REP, 0, 0), 0)
    for move in (CORE_SWAP, X_SWAP, z_flip(1), z_flip(2), z_flip(4)):
        weight_sum = weight_sum + send(weight_sum, move)
    return activated, feature_grad, weight_sum


def solution(mesh):
    fine = Mesh(mesh.devices.reshape(SIZES), AXES)
    placed = (
        P(BLK, REP, None),
        P(),
        P(BLK, REP, None),
        P(BLK, REP),
        P(REP, BLK, None),
        P(REP, BLK, None),
        P(REP, BLK),
        P(REP, BLK, None, None, None),
    )
    return jax.shard_map(
        on_device,
        mesh=fine,
        in_specs=placed,
        out_specs=(P(BLK, REP, None), P(BLK, REP, None), P(REP, None)),
        check_vma=False,
    )
```

time: 703 us -> 201 us (0.29)
  waiting for transfers between devices: 548 us -> 79.7 us
  starting transfers between devices: 0.2 us -> 97 us
  other arithmetic: 69.2 us -> 3.65 us
  local copies, waits for them, and re-layouts: 43.5 us -> 2.58 us
  matrix products: 17.2 us -> 2.62 us
  between operations: 14.5 us -> 1.68 us
  Pallas kernels: 0 us -> 10.7 us
    reduce_scatter x2 -> x0, waiting for transfers between devices: 242 us -> none  [the longest x1 206 us: on_device(): lax.psum_scatter(forward_terms.astype(jnp.bfloat16), 'blk', scatter_dimen...]
    psum x1 -> x0, waiting for transfers between devices: 192 us -> none  [on_device(): weight_full = lax.psum(weight_part, ('rep', 'blk'))]
    all_gather x2 -> x0, waiting for transfers between devices: 113 us -> none  [the longest x1 73.3 us: on_device(): all_grads = lax.all_gather(row_grad[None], 'blk', axis=0, tiled=True)]
    ppermute x0 -> x41, starting transfers between devices: none -> 81.8 us  [send(): return lax.ppermute(value, AXES, pairs)]
    ppermute x0 -> x41, waiting for transfers between devices: none -> 65.5 us  [send(): return lax.ppermute(value, AXES, pairs)]
    scatter-add x8 -> x0, other arithmetic: 51.1 us -> none  [one_group(): return summed.at[landing].add(products * is_live[:, None, None])]
    gather x8 -> x0, local copies, waits for them, and re-layouts: 19.7 us -> none  [the longest x4 11.8 us: one_group(): picked = source[rows_here]]
    unnamed x13 -> x28, local copies, waits for them, and re-layouts: 16.7 us -> 0.25 us
  transfers between devices with their start and end apart: 5 -> 44, of which waited for: 5 -> 19; matrix products, arithmetic and copies ran while one was open for 10% -> 2% of each run, Pallas kernels for 0% -> 3%
where the time goes in v1:
time: 201 us; the launch traced here: 198 us
  starting transfers between devices  97 us (48%)
  waiting for transfers between devices  79.7 us (40%)
  Pallas kernels  10.7 us (5%)
  other arithmetic  3.65 us (2%)
  matrix products  2.62 us (1%)
  local copies, waits for them, and re-layouts  2.58 us (1%)
    ppermute x41, starting transfers between devices, send(): return lax.ppermute(value, AXES, pairs)  81.8 us
    ppermute x41, waiting for transfers between devices, send(): return lax.ppermute(value, AXES, pairs)  65.5 us
    all_to_all x1, waiting for transfers between devices, on_device(): panel = lax.all_to_all(jnp.broadcast_to(features, (8, 512, BS)), REP, 0, 0)  14.2 us
    pallas_call x1, Pallas kernels, backward_products(): pl.pallas_call(backward_kernel, out_shape=jax.ShapeDtypeStruct((32, BS, B...  6.02 us
    all_to_all x1, starting transfers between devices, on_device(): panel = lax.all_to_all(jnp.broadcast_to(features, (8, 512, BS)), REP, 0, 0)  5.95 us
    all_to_all x1, starting transfers between devices, on_device(): parts = lax.all_to_all(columns.reshape(8, 512, BS), REP, 0, 0)  5.78 us
    pallas_call x1, Pallas kernels, forward_products(): pl.pallas_call(forward_kernel, out_shape=(half, half), in_specs=[smem, sm...  4.65 us
  transfers between devices with their start and end apart: 44, of which 19 were waited for; matrix products, arithmetic and copies ran while one was open for 2% of the time, Pallas kernels for 3%

profile of v1, /device:TPU:1, one launch (start us, length us, event | category | flops | bytes accessed | tf_op | source)
XLA Modules:
  0.0 197.9 jit_solution(18308270305064678528)
XLA Ops:
  0.7 2.1 %broadcast_in_dim.12 = bf16[8,512,128]{2,1,0:T(8,128)(2,1)} broadcast(bf16[512,128]{1,0:T(8,128)(2,1)} %bitcast.168), dimensions={1,2} | broadcast | bytes 1179648 | tf_op jit(solution)/shard_map/broadcast_in_dim | solution.py:223
  2.7 5.9 %all-to-all-start = ((bf16[8,512,128]{2,1,0:T(8,128)(2,1)}), bf16[8,512,128]{2,1,0:T(8,128)(2,1)S(1)}, u32[]{:S(2)}, u32[]{:S(2)}) async-start(bf16[8,512,128]{2,1,0:T(8,128)(2,1)} %broadcast_in_dim.12), calls=%async_computation | async-start | bytes 2097152 | tf_op jit(solution)/shard_map/all_to_all | solution.py:223
  9.4 14.2 %all-to-all-done = bf16[8,512,128]{2,1,0:T(8,128)(2,1)S(1)} async-done(((bf16[8,512,128]{2,1,0:T(8,128)(2,1)}), bf16[8,512,128]{2,1,0:T(8,128)(2,1)S(1)}, u32[]{:S(2)}, u32[]{:S(2)}) %all-to-all-start) | async-done | bytes 1048608 | tf_op jit(solution)/shard_map/all_to_all | solution.py:223
  23.6 4.6 %forward_products.1 = (bf16[64,128,128]{2,1,0:T(8,128)(2,1)S(1)}, bf16[64,128,128]{2,1,0:T(8,128)(2,1)S(1)}) custom-call(s32[384]{0:T(512)S(1)} %get-tuple-element.28.land_ref, s32[384]{0:T(512)S(1)} %reduce.1.cols_ref, s32[1]{0:T(128)} %bitcast.152.count_ref, bf16[32,128,128]{2,1,0:T(8,128)(2,1)S(1)} %bitcast.154, bf16[384,128,128]{2,1,0:T(8,128)(2,1)} %bitcast.159), custom_call_target="tpu_custom_call" | custom-call | flops 1610612736 | bytes 18874368 | tf_op jit(solution)/shard_map/forward_products/pallas_call | solution.py:104
  28.3 4.1 %collective-permute-done = bf16[64,128,128]{2,1,0:T(8,128)(2,1)S(1)} collective-permute-done((bf16[64,128,128]{2,1,0:T(8,128)(2,1)S(1)}, bf16[64,128,128]{2,1,0:T(8,128)(2,1)S(1)}, u32[]{:S(2)}, u32[]{:S(2)}) %collective-permute-start) | collective-permute-done | bytes 2097184 | tf_op jit(solution)/shard_map/ppermute | solution.py:52
  32.5 0.8 add_convert_fusion
  33.5 2.6 %collective-permute-start.10 = (bf16[2,256,128]{2,1,0:T(8,128)(2,1)S(1)}, bf16[2,256,128]{2,1,0:T(8,128)(2,1)S(1)}, u32[]{:S(2)}, u32[]{:S(2)}) collective-permute-start(bf16[2,256,128]{2,1,0:T(8,128)(2,1)S(1)} %get-tuple-element.12), channel_id=1, source_target_pairs={{0,8},{1,9},{2,10},{3,11},{4,12},{5,13},{6,14},{7,15},{8,16},{9,17... | collective-permute-start | bytes 393224 | tf_op jit(solution)/shard_map/ppermute | solution.py:52
  36.1 6.1 %collective-permute-start.11 = (bf16[2,256,128]{2,1,0:T(8,128)(2,1)S(1)}, bf16[2,256,128]{2,1,0:T(8,128)(2,1)S(1)}, u32[]{:S(2)}, u32[]{:S(2)}) collective-permute-start(bf16[2,256,128]{2,1,0:T(8,128)(2,1)S(1)} %get-tuple-element.11), channel_id=1, source_target_pairs={{0,12},{1,13},{2,14},{3,15},{4,16},{5,17},{6,18},{7,19},{8,20},{9,... | collective-permute-start | bytes 393224 | tf_op jit(solution)/shard_map/ppermute | solution.py:52
  42.2 0.5 collective-permute-start.12
  42.7 4.0 %collective-permute-start.13 = (bf16[2,256,128]{2,1,0:T(8,128)(2,1)S(1)}, bf16[2,256,128]{2,1,0:T(8,128)(2,1)S(1)}, u32[]{:S(2)}, u32[]{:S(2)}) collective-permute-start(bf16[2,256,128]{2,1,0:T(8,128)(2,1)S(1)} %get-tuple-element.9), channel_id=1, source_target_pairs={{0,20},{1,21},{2,22},{3,23},{4,24},{5,25},{6,26},{7,27},{8,28},{9,... | collective-permute-start | bytes 393224 | tf_op jit(solution)/shard_map/ppermute | solution.py:52
  46.6 1.4 collective-permute-start.14
  48.0 8.2 %collective-permute-done.11 = bf16[2,256,128]{2,1,0:T(8,128)(2,1)S(1)} collective-permute-done((bf16[2,256,128]{2,1,0:T(8,128)(2,1)S(1)}, bf16[2,256,128]{2,1,0:T(8,128)(2,1)S(1)}, u32[]{:S(2)}, u32[]{:S(2)}) %collective-permute-start.11) | collective-permute-done | bytes 131104 | tf_op jit(solution)/shard_map/ppermute | solution.py:52
  56.3 3.0 %collective-permute-done.12 = bf16[2,256,128]{2,1,0:T(8,128)(2,1)S(1)} collective-permute-done((bf16[2,256,128]{2,1,0:T(8,128)(2,1)S(1)}, bf16[2,256,128]{2,1,0:T(8,128)(2,1)S(1)}, u32[]{:S(2)}, u32[]{:S(2)}) %collective-permute-start.12) | collective-permute-done | bytes 131104 | tf_op jit(solution)/shard_map/ppermute | solution.py:52
  59.4 3.0 %collective-permute-start.1 = (bf16[8,256,128]{2,1,0:T(8,128)(2,1)S(1)}, bf16[8,256,128]{2,1,0:T(8,128)(2,1)S(1)}, u32[]{:S(2)}, u32[]{:S(2)}) collective-permute-start(bf16[8,256,128]{2,1,0:T(8,128)(2,1)S(1)} %slice_bitcast_fusion), channel_id=1, source_target_pairs={{0,2},{1,3},{2,0},{3,1},{4,6},{5,7},{6,4},{7,5},{8,10},{9,11},{10,... | collective-permute-start | bytes 1572872 | tf_op jit(solution)/shard_map/ppermute | solution.py:52
  62.3 3.9 %collective-permute-done.14 = bf16[2,256,128]{2,1,0:T(8,128)(2,1)S(1)} collective-permute-done((bf16[2,256,128]{2,1,0:T(8,128)(2,1)S(1)}, bf16[2,256,128]{2,1,0:T(8,128)(2,1)S(1)}, u32[]{:S(2)}, u32[]{:S(2)}) %collective-permute-start.14) | collective-permute-done | bytes 131104 | tf_op jit(solution)/shard_map/ppermute | solution.py:52
  66.4 3.3 %collective-permute-start.16 = (bf16[256,128]{1,0:T(8,128)(2,1)S(1)}, bf16[256,128]{1,0:T(8,128)(2,1)S(1)}, u32[]{:S(2)}, u32[]{:S(2)}) collective-permute-start(bf16[256,128]{1,0:T(8,128)(2,1)S(1)} %fusion.22), channel_id=1, source_target_pairs={{0,2},{1,3},{2,0},{3,1},{4,6},{5,7},{6,4},{7,5},{8,10},{9,11},{10,... | collective-permute-start | bytes 196616 | tf_op jit(solution)/shard_map/ppermute | solution.py:52
  69.7 3.5 %collective-permute-done.1 = bf16[8,256,128]{2,1,0:T(8,128)(2,1)S(1)} collective-permute-done((bf16[8,256,128]{2,1,0:T(8,128)(2,1)S(1)}, bf16[8,256,128]{2,1,0:T(8,128)(2,1)S(1)}, u32[]{:S(2)}, u32[]{:S(2)}) %collective-permute-start.1) | collective-permute-done | bytes 524320 | tf_op jit(solution)/shard_map/ppermute | solution.py:52
  73.5 1.9 collective-permute-start.3
  75.4 5.6 %collective-permute-start.4 = (bf16[256,128]{1,0:T(8,128)(2,1)S(1)}, bf16[256,128]{1,0:T(8,128)(2,1)S(1)}, u32[]{:S(2)}, u32[]{:S(2)}) collective-permute-start(bf16[256,128]{1,0:T(8,128)(2,1)S(1)} %get-tuple-element.19), channel_id=1, source_target_pairs={{0,12},{1,13},{2,14},{3,15},{4,16},{5,17},{6,18},{7,19},{8,20},{9,... | collective-permute-start | bytes 196616 | tf_op jit(solution)/shard_map/ppermute | solution.py:52
  80.9 4.3 %collective-permute-start.6 = (bf16[256,128]{1,0:T(8,128)(2,1)S(1)}, bf16[256,128]{1,0:T(8,128)(2,1)S(1)}, u32[]{:S(2)}, u32[]{:S(2)}) collective-permute-start(bf16[256,128]{1,0:T(8,128)(2,1)S(1)} %get-tuple-element.17), channel_id=1, source_target_pairs={{0,20},{1,21},{2,22},{3,23},{4,24},{5,25},{6,26},{7,27},{8,28},{9,... | collective-permute-start | bytes 196616 | tf_op jit(solution)/shard_map/ppermute | solution.py:52
  85.2 1.3 collective-permute-start.7
  86.5 1.4 collective-permute-start.8
  87.9 1.8 collective-permute-done.5
  89.8 2.3 %collective-permute-done.7 = bf16[256,128]{1,0:T(8,128)(2,1)S(1)} collective-permute-done((bf16[256,128]{1,0:T(8,128)(2,1)S(1)}, bf16[256,128]{1,0:T(8,128)(2,1)S(1)}, u32[]{:S(2)}, u32[]{:S(2)}) %collective-permute-start.7) | collective-permute-done | bytes 65568 | tf_op jit(solution)/shard_map/ppermute | solution.py:52
  92.0 2.6 %collective-permute-done.8 = bf16[256,128]{1,0:T(8,128)(2,1)S(1)} collective-permute-done((bf16[256,128]{1,0:T(8,128)(2,1)S(1)}, bf16[256,128]{1,0:T(8,128)(2,1)S(1)}, u32[]{:S(2)}, u32[]{:S(2)}) %collective-permute-start.8) | collective-permute-done | bytes 65568 | tf_op jit(solution)/shard_map/ppermute | solution.py:52
  95.0 1.0 fusion.2
  96.2 0.5 collective-permute-start.25
  96.8 1.8 collective-permute-start.26
  98.5 2.2 %collective-permute-start.27 = (bf16[256,128]{1,0:T(8,128)(2,1)S(1)}, bf16[256,128]{1,0:T(8,128)(2,1)S(1)}, u32[]{:S(2)}, u32[]{:S(2)}) collective-permute-start(bf16[256,128]{1,0:T(8,128)(2,1)S(1)} %get-tuple-element.32), channel_id=1, source_target_pairs={{0,12},{1,13},{2,14},{3,15},{4,16},{5,17},{6,18},{7,19},{8,20},{9,... | collective-permute-start | bytes 196616 | tf_op jit(solution)/shard_map/ppermute | solution.py:52
  100.7 2.1 %collective-permute-start.28 = (bf16[256,128]{1,0:T(8,128)(2,1)S(1)}, bf16[256,128]{1,0:T(8,128)(2,1)S(1)}, u32[]{:S(2)}, u32[]{:S(2)}) collective-permute-start(bf16[256,128]{1,0:T(8,128)(2,1)S(1)} %get-tuple-element.32), channel_id=1, source_target_pairs={{0,16},{1,17},{2,18},{3,19},{4,20},{5,21},{6,22},{7,23},{8,24},{9,... | collective-permute-start | bytes 196616 | tf_op jit(solution)/shard_map/ppermute | solution.py:52
  102.8 4.5 %collective-permute-start.29 = (bf16[256,128]{1,0:T(8,128)(2,1)S(1)}, bf16[256,128]{1,0:T(8,128)(2,1)S(1)}, u32[]{:S(2)}, u32[]{:S(2)}) collective-permute-start(bf16[256,128]{1,0:T(8,128)(2,1)S(1)} %get-tuple-element.32), channel_id=1, source_target_pairs={{0,20},{1,21},{2,22},{3,23},{4,24},{5,25},{6,26},{7,27},{8,28},{9,... | collective-permute-start | bytes 196616 | tf_op jit(solution)/shard_map/ppermute | solution.py:52
  107.5 1.1 collective-permute-start.30
  108.7 2.8 %collective-permute-start.17 = (bf16[256,128]{1,0:T(8,128)(2,1)S(1)}, bf16[256,128]{1,0:T(8,128)(2,1)S(1)}, u32[]{:S(2)}, u32[]{:S(2)}) collective-permute-start(bf16[256,128]{1,0:T(8,128)(2,1)S(1)} %convolution_convert_fusion.1), channel_id=1, source_target_pairs={{0,2},{1,3},{2,0},{3,1},{4,6},{5,7},{6,4},{7,5},{8,10},{9,11},{10,... | collective-permute-start | bytes 196616 | tf_op jit(solution)/shard_map/ppermute | solution.py:52
  111.5 2.1 %collective-permute-done.17 = bf16[256,128]{1,0:T(8,128)(2,1)S(1)} collective-permute-done((bf16[256,128]{1,0:T(8,128)(2,1)S(1)}, bf16[256,128]{1,0:T(8,128)(2,1)S(1)}, u32[]{:S(2)}, u32[]{:S(2)}) %collective-permute-start.17) | collective-permute-done | bytes 65568 | tf_op jit(solution)/shard_map/ppermute | solution.py:52
  113.5 1.5 collective-permute-start.31
  115.2 1.4 collective-permute-start.19
  116.7 1.1 collective-permute-start.20
  117.8 3.4 %collective-permute-start.21 = (bf16[2,256,128]{2,1,0:T(8,128)(2,1)S(1)}, bf16[2,256,128]{2,1,0:T(8,128)(2,1)S(1)}, u32[]{:S(2)}, u32[]{:S(2)}) collective-permute-start(bf16[2,256,128]{2,1,0:T(8,128)(2,1)S(1)} %pad_maximum_fusion), channel_id=1, source_target_pairs={{0,16},{1,17},{2,18},{3,19},{4,20},{5,21},{6,22},{7,23},{8,24},{9,... | collective-permute-start | bytes 393224 | tf_op jit(solution)/shard_map/ppermute | solution.py:52
  121.2 2.4 %collective-permute-start.22 = (bf16[2,256,128]{2,1,0:T(8,128)(2,1)S(1)}, bf16[2,256,128]{2,1,0:T(8,128)(2,1)S(1)}, u32[]{:S(2)}, u32[]{:S(2)}) collective-permute-start(bf16[2,256,128]{2,1,0:T(8,128)(2,1)S(1)} %pad_maximum_fusion), channel_id=1, source_target_pairs={{0,20},{1,21},{2,22},{3,23},{4,24},{5,25},{6,26},{7,27},{8,28},{9,... | collective-permute-start | bytes 393224 | tf_op jit(solution)/shard_map/ppermute | solution.py:52
  123.6 2.5 %collective-permute-start.23 = (bf16[2,256,128]{2,1,0:T(8,128)(2,1)S(1)}, bf16[2,256,128]{2,1,0:T(8,128)(2,1)S(1)}, u32[]{:S(2)}, u32[]{:S(2)}) collective-permute-start(bf16[2,256,128]{2,1,0:T(8,128)(2,1)S(1)} %pad_maximum_fusion), channel_id=1, source_target_pairs={{0,24},{1,25},{2,26},{3,27},{4,28},{5,29},{6,30},{7,31},{8,0},{9,1... | collective-permute-start | bytes 393224 | tf_op jit(solution)/shard_map/ppermute | solution.py:52
  126.2 1.2 collective-permute-start.24
  127.4 1.9 collective-permute-done.20
  129.3 3.4 %collective-permute-start.32 = (bf16[8,256,128]{2,1,0:T(8,128)(2,1)S(1)}, bf16[8,256,128]{2,1,0:T(8,128)(2,1)S(1)}, u32[]{:S(2)}, u32[]{:S(2)}) collective-permute-start(bf16[8,256,128]{2,1,0:T(8,128)(2,1)S(1)} %bitcast_dynamic-update-slice_fusion.8), channel_id=1, source_target_pairs={{0,2},{1,3},{2,0},{3,1},{4,6},{5,7},{6,4},{7,5},{8,10},{9,11},{10,... | collective-permute-start | bytes 1572872 | tf_op jit(solution)/shard_map/ppermute | solution.py:52
  132.7 7.4 %collective-permute-done.23 = bf16[2,256,128]{2,1,0:T(8,128)(2,1)S(1)} collective-permute-done((bf16[2,256,128]{2,1,0:T(8,128)(2,1)S(1)}, bf16[2,256,128]{2,1,0:T(8,128)(2,1)S(1)}, u32[]{:S(2)}, u32[]{:S(2)}) %collective-permute-start.23) | collective-permute-done | bytes 131104 | tf_op jit(solution)/shard_map/ppermute | solution.py:52
  140.2 4.7 %collective-permute-done.24 = bf16[2,256,128]{2,1,0:T(8,128)(2,1)S(1)} collective-permute-done((bf16[2,256,128]{2,1,0:T(8,128)(2,1)S(1)}, bf16[2,256,128]{2,1,0:T(8,128)(2,1)S(1)}, u32[]{:S(2)}, u32[]{:S(2)}) %collective-permute-start.24) | collective-permute-done | bytes 131104 | tf_op jit(solution)/shard_map/ppermute | solution.py:52
  145.0 2.5 %collective-permute-start.33 = (bf16[8,2,256,128]{3,2,1,0:T(8,128)(2,1)S(1)}, bf16[8,2,256,128]{3,2,1,0:T(8,128)(2,1)S(1)}, u32[]{:S(2)}, u32[]{:S(2)}) collective-permute-start(bf16[8,2,256,128]{3,2,1,0:T(8,128)(2,1)S(1)} %bitcast_dynamic-update-slice_fusion), channel_id=1, source_target_pairs={{0,1},{1,0},{2,3},{3,2},{4,5},{5,4},{6,7},{7,6},{8,9},{9,8},{10,11... | collective-permute-start | bytes 3145736 | tf_op jit(solution)/shard_map/ppermute | solution.py:52
  147.6 3.1 %collective-permute-start.35 = (bf16[8,256,128]{2,1,0:T(8,128)(2,1)S(1)}, bf16[8,256,128]{2,1,0:T(8,128)(2,1)}, u32[]{:S(2)}, u32[]{:S(2)}) collective-permute-start(bf16[8,256,128]{2,1,0:T(8,128)(2,1)S(1)} %collective-permute-done.32), channel_id=1, source_target_pairs={{0,1},{1,0},{2,3},{3,2},{4,5},{5,4},{6,7},{7,6},{8,9},{9,8},{10,11... | collective-permute-start | bytes 1572872 | tf_op jit(solution)/shard_map/ppermute | solution.py:52
  150.9 0.9 fusion
  151.8 3.5 %all-to-all-start.2 = ((f32[8,16,256]{2,1,0:T(8,128)}), f32[8,16,256]{2,1,0:T(8,128)S(1)}, u32[]{:S(2)}, u32[]{:S(2)}) async-start(f32[8,16,256]{2,1,0:T(8,128)} %bitcast.60), calls=%async_computation.2 | async-start | bytes 262144 | tf_op jit(solution)/shard_map/all_to_all | solution.py:262
  155.2 6.0 %backward_products.1 = bf16[32,128,128]{2,1,0:T(8,128)(2,1)} custom-call(s32[384]{0:T(512)S(1)} %get-tuple-element.27.land_ref, s32[384]{0:T(512)S(1)} %reduce.1.cols_ref, s32[1]{0:T(128)} %bitcast.153.count_ref, bf16[32,128,128]{2,1,0:T(8,128)(2,1)S(1)} %bitcast.155, bf16[16,128,128]{2,1,0:T(8,128)(2,1)S(1)} %bitcast.157, ...), custom_call_target="tpu_custom_call" | custom-call | flops 1610612736 | bytes 18874368 | tf_op jit(solution)/shard_map/backward_products/pallas_call | solution.py:158
  161.3 5.8 %all-to-all-start.1 = ((bf16[8,512,128]{2,1,0:T(8,128)(2,1)}), bf16[8,512,128]{2,1,0:T(8,128)(2,1)S(1)}, u32[]{:S(2)}, u32[]{:S(2)}) async-start(bf16[8,512,128]{2,1,0:T(8,128)(2,1)} %bitcast.57), calls=%async_computation.1 | async-start | bytes 2097152 | tf_op jit(solution)/shard_map/all_to_all | solution.py:254
  167.1 0.4 collective-permute-start.36
  167.5 0.8 collective-permute-done.36
  168.4 3.2 %collective-permute-start.37 = (f32[16,256]{1,0:T(8,128)S(1)}, f32[16,256]{1,0:T(8,128)S(1)}, u32[]{:S(2)}, u32[]{:S(2)}) collective-permute-start(f32[16,256]{1,0:T(8,128)S(1)} %add.194), channel_id=1, source_target_pairs={{0,2},{1,3},{2,0},{3,1},{4,6},{5,7},{6,4},{7,5},{8,10},{9,11},{10,... | collective-permute-start | bytes 49160 | tf_op jit(solution)/shard_map/ppermute | solution.py:52
  171.6 11.7 %collective-permute-done.37 = f32[16,256]{1,0:T(8,128)S(1)} collective-permute-done((f32[16,256]{1,0:T(8,128)S(1)}, f32[16,256]{1,0:T(8,128)S(1)}, u32[]{:S(2)}, u32[]{:S(2)}) %collective-permute-start.37) | collective-permute-done | bytes 16416 | tf_op jit(solution)/shard_map/ppermute | solution.py:52
  183.2 0.3 collective-permute-start.38
  183.6 2.3 %collective-permute-done.38 = f32[16,256]{1,0:T(8,128)S(1)} collective-permute-done((f32[16,256]{1,0:T(8,128)S(1)}, f32[16,256]{1,0:T(8,128)S(1)}, u32[]{:S(2)}, u32[]{:S(2)}) %collective-permute-start.38) | collective-permute-done | bytes 16416 | tf_op jit(solution)/shard_map/ppermute | solution.py:52
  185.8 2.7 %collective-permute-start.39 = (f32[16,256]{1,0:T(8,128)S(1)}, f32[16,256]{1,0:T(8,128)S(1)}, u32[]{:S(2)}, u32[]{:S(2)}) collective-permute-start(f32[16,256]{1,0:T(8,128)S(1)} %add.196), channel_id=1, source_target_pairs={{0,8},{1,9},{2,10},{3,11},{4,12},{5,13},{6,14},{7,15},{8,0},{9,1},... | collective-permute-start | bytes 49160 | tf_op jit(solution)/shard_map/ppermute | solution.py:52
  188.5 1.1 collective-permute-done.39
  189.6 2.0 %collective-permute-start.40 = (f32[16,256]{1,0:T(8,128)S(1)}, f32[16,256]{1,0:T(8,128)S(1)}, u32[]{:S(2)}, u32[]{:S(2)}) collective-permute-start(f32[16,256]{1,0:T(8,128)S(1)} %add.197), channel_id=1, source_target_pairs={{0,16},{1,17},{2,18},{3,19},{4,20},{5,21},{6,22},{7,23},{8,24},{9,... | collective-permute-start | bytes 49160 | tf_op jit(solution)/shard_map/ppermute | solution.py:52
  191.6 0.7 maximum_bitcast_fusion
  192.4 4.0 %collective-permute-done.40 = f32[16,256]{1,0:T(8,128)S(1)} collective-permute-done((f32[16,256]{1,0:T(8,128)S(1)}, f32[16,256]{1,0:T(8,128)S(1)}, u32[]{:S(2)}, u32[]{:S(2)}) %collective-permute-start.40) | collective-permute-done | bytes 16416 | tf_op jit(solution)/shard_map/ppermute | solution.py:52
  196.3 0.6 add.198
  197.1 0.8 fusion.10
  (87 shorter events, 2.5 us)
Async XLA Ops:
  0.6 94.2 %copy-start = (bf16[128,256]{1,0:T(8,128)(2,1)S(1)}, bf16[128,256]{1,0:T(8,128)(2,1)}, u32[]{:S(2)}) copy-start(bf16[128,256]{1,0:T(8,128)(2,1)} %param.9) | copy-start | bytes 196612
  0.6 8.0 %copy-start.5 = (s32[1,1,384]{2,1,0:T(1,128)S(1)}, s32[1,1,384]{2,1,0:T(1,128)}, u32[]{:S(2)}) copy-start(s32[1,1,384]{2,1,0:T(1,128)} %param.12) | copy-start | bytes 4612
  0.7 8.0 %copy-start.6 = (s32[1,1,384]{2,1,0:T(1,128)S(1)}, s32[1,1,384]{2,1,0:T(1,128)}, u32[]{:S(2)}) copy-start(s32[1,1,384]{2,1,0:T(1,128)} %param.13) | copy-start | bytes 4612
  2.7 20.9 %all-to-all-start = ((bf16[8,512,128]{2,1,0:T(8,128)(2,1)}), bf16[8,512,128]{2,1,0:T(8,128)(2,1)S(1)}, u32[]{:S(2)}, u32[]{:S(2)}) async-start(bf16[8,512,128]{2,1,0:T(8,128)(2,1)} %broadcast_in_dim.12), calls=%async_computation | async-start | bytes 2097152 | tf_op jit(solution)/shard_map/all_to_all | solution.py:223
  28.2 4.2 %collective-permute-start = (bf16[64,128,128]{2,1,0:T(8,128)(2,1)S(1)}, bf16[64,128,128]{2,1,0:T(8,128)(2,1)S(1)}, u32[]{:S(2)}, u32[]{:S(2)}) collective-permute-start(bf16[64,128,128]{2,1,0:T(8,128)(2,1)S(1)} %get-tuple-element.6), channel_id=1, source_target_pairs={{0,1},{1,0},{2,3},{3,2},{4,5},{5,4},{6,7},{7,6},{8,9},{9,8},{10,11... | collective-permute-start | bytes 6291464 | tf_op jit(solution)/shard_map/ppermute | solution.py:52
  33.5 14.5 %collective-permute-start.10 = (bf16[2,256,128]{2,1,0:T(8,128)(2,1)S(1)}, bf16[2,256,128]{2,1,0:T(8,128)(2,1)S(1)}, u32[]{:S(2)}, u32[]{:S(2)}) collective-permute-start(bf16[2,256,128]{2,1,0:T(8,128)(2,1)S(1)} %get-tuple-element.12), channel_id=1, source_target_pairs={{0,8},{1,9},{2,10},{3,11},{4,12},{5,13},{6,14},{7,15},{8,16},{9,17... | collective-permute-start | bytes 393224 | tf_op jit(solution)/shard_map/ppermute | solution.py:52
  36.1 20.2 %collective-permute-start.11 = (bf16[2,256,128]{2,1,0:T(8,128)(2,1)S(1)}, bf16[2,256,128]{2,1,0:T(8,128)(2,1)S(1)}, u32[]{:S(2)}, u32[]{:S(2)}) collective-permute-start(bf16[2,256,128]{2,1,0:T(8,128)(2,1)S(1)} %get-tuple-element.11), channel_id=1, source_target_pairs={{0,12},{1,13},{2,14},{3,15},{4,16},{5,17},{6,18},{7,19},{8,20},{9,... | collective-permute-start | bytes 393224 | tf_op jit(solution)/shard_map/ppermute | solution.py:52
  42.2 17.2 %collective-permute-start.12 = (bf16[2,256,128]{2,1,0:T(8,128)(2,1)S(1)}, bf16[2,256,128]{2,1,0:T(8,128)(2,1)S(1)}, u32[]{:S(2)}, u32[]{:S(2)}) collective-permute-start(bf16[2,256,128]{2,1,0:T(8,128)(2,1)S(1)} %get-tuple-element.10), channel_id=1, source_target_pairs={{0,16},{1,17},{2,18},{3,19},{4,20},{5,21},{6,22},{7,23},{8,24},{9,... | collective-permute-start | bytes 393224 | tf_op jit(solution)/shard_map/ppermute | solution.py:52
  42.7 19.7 %collective-permute-start.13 = (bf16[2,256,128]{2,1,0:T(8,128)(2,1)S(1)}, bf16[2,256,128]{2,1,0:T(8,128)(2,1)S(1)}, u32[]{:S(2)}, u32[]{:S(2)}) collective-permute-start(bf16[2,256,128]{2,1,0:T(8,128)(2,1)S(1)} %get-tuple-element.9), channel_id=1, source_target_pairs={{0,20},{1,21},{2,22},{3,23},{4,24},{5,25},{6,26},{7,27},{8,28},{9,... | collective-permute-start | bytes 393224 | tf_op jit(solution)/shard_map/ppermute | solution.py:52
  46.6 19.6 %collective-permute-start.14 = (bf16[2,256,128]{2,1,0:T(8,128)(2,1)S(1)}, bf16[2,256,128]{2,1,0:T(8,128)(2,1)S(1)}, u32[]{:S(2)}, u32[]{:S(2)}) collective-permute-start(bf16[2,256,128]{2,1,0:T(8,128)(2,1)S(1)} %get-tuple-element.8), channel_id=1, source_target_pairs={{0,24},{1,25},{2,26},{3,27},{4,28},{5,29},{6,30},{7,31},{8,0},{9,1... | collective-permute-start | bytes 393224 | tf_op jit(solution)/shard_map/ppermute | solution.py:52
  48.0 18.2 %collective-permute-start.15 = (bf16[2,256,128]{2,1,0:T(8,128)(2,1)S(1)}, bf16[2,256,128]{2,1,0:T(8,128)(2,1)S(1)}, u32[]{:S(2)}, u32[]{:S(2)}) collective-permute-start(bf16[2,256,128]{2,1,0:T(8,128)(2,1)S(1)} %get-tuple-element.13), channel_id=1, source_target_pairs={{0,28},{1,29},{2,30},{3,31},{4,0},{5,1},{6,2},{7,3},{8,4},{9,5},{1... | collective-permute-start | bytes 393224 | tf_op jit(solution)/shard_map/ppermute | solution.py:52
  56.2 10.0 %collective-permute-start.9 = (bf16[2,256,128]{2,1,0:T(8,128)(2,1)S(1)}, bf16[2,256,128]{2,1,0:T(8,128)(2,1)S(1)}, u32[]{:S(2)}, u32[]{:S(2)}) collective-permute-start(bf16[2,256,128]{2,1,0:T(8,128)(2,1)S(1)} %get-tuple-element.7), channel_id=1, source_target_pairs={{0,4},{1,5},{2,6},{3,7},{4,8},{5,9},{6,10},{7,11},{8,12},{9,13},{1... | collective-permute-start | bytes 393224 | tf_op jit(solution)/shard_map/ppermute | solution.py:52
  56.3 31.6 %copy-start.4 = (f32[1,512]{1,0:T(1,128)S(1)}, f32[1,512]{1,0:T(1,128)}, u32[]{:S(2)}) copy-start(f32[1,512]{1,0:T(1,128)} %param.11) | copy-start | bytes 6148
  56.3 38.4 %copy-start.1 = (bf16[1,512,128]{2,1,0:T(8,128)(2,1)S(1)}, bf16[1,512,128]{2,1,0:T(8,128)(2,1)}, u32[]{:S(2)}) copy-start(bf16[1,512,128]{2,1,0:T(8,128)(2,1)} %param.8) | copy-start | bytes 393220
  59.4 13.8 %collective-permute-start.1 = (bf16[8,256,128]{2,1,0:T(8,128)(2,1)S(1)}, bf16[8,256,128]{2,1,0:T(8,128)(2,1)S(1)}, u32[]{:S(2)}, u32[]{:S(2)}) collective-permute-start(bf16[8,256,128]{2,1,0:T(8,128)(2,1)S(1)} %slice_bitcast_fusion), channel_id=1, source_target_pairs={{0,2},{1,3},{2,0},{3,1},{4,6},{5,7},{6,4},{7,5},{8,10},{9,11},{10,... | collective-permute-start | bytes 1572872 | tf_op jit(solution)/shard_map/ppermute | solution.py:52
  66.4 28.6 %copy-start.7 = (bf16[1,512,256]{2,1,0:T(8,128)(2,1)S(1)}, bf16[1,512,256]{2,1,0:T(8,128)(2,1)}, u32[]{:S(2)}) copy-start(bf16[1,512,256]{2,1,0:T(8,128)(2,1)} %param.10) | copy-start | bytes 786436
  66.4 14.6 %collective-permute-start.16 = (bf16[256,128]{1,0:T(8,128)(2,1)S(1)}, bf16[256,128]{1,0:T(8,128)(2,1)S(1)}, u32[]{:S(2)}, u32[]{:S(2)}) collective-permute-start(bf16[256,128]{1,0:T(8,128)(2,1)S(1)} %fusion.22), channel_id=1, source_target_pairs={{0,2},{1,3},{2,0},{3,1},{4,6},{5,7},{6,4},{7,5},{8,10},{9,11},{10,... | collective-permute-start | bytes 196616 | tf_op jit(solution)/shard_map/ppermute | solution.py:52
  73.4 11.9 %collective-permute-start.2 = (bf16[256,128]{1,0:T(8,128)(2,1)S(1)}, bf16[256,128]{1,0:T(8,128)(2,1)S(1)}, u32[]{:S(2)}, u32[]{:S(2)}) collective-permute-start(bf16[256,128]{1,0:T(8,128)(2,1)S(1)} %get-tuple-element.14), channel_id=1, source_target_pairs={{0,4},{1,5},{2,6},{3,7},{4,8},{5,9},{6,10},{7,11},{8,12},{9,13},{1... | collective-permute-start | bytes 196616 | tf_op jit(solution)/shard_map/ppermute | solution.py:52
  73.5 13.0 %collective-permute-start.3 = (bf16[256,128]{1,0:T(8,128)(2,1)S(1)}, bf16[256,128]{1,0:T(8,128)(2,1)S(1)}, u32[]{:S(2)}, u32[]{:S(2)}) collective-permute-start(bf16[256,128]{1,0:T(8,128)(2,1)S(1)} %get-tuple-element.20), channel_id=1, source_target_pairs={{0,8},{1,9},{2,10},{3,11},{4,12},{5,13},{6,14},{7,15},{8,16},{9,17... | collective-permute-start | bytes 196616 | tf_op jit(solution)/shard_map/ppermute | solution.py:52
  75.4 12.5 %collective-permute-start.4 = (bf16[256,128]{1,0:T(8,128)(2,1)S(1)}, bf16[256,128]{1,0:T(8,128)(2,1)S(1)}, u32[]{:S(2)}, u32[]{:S(2)}) collective-permute-start(bf16[256,128]{1,0:T(8,128)(2,1)S(1)} %get-tuple-element.19), channel_id=1, source_target_pairs={{0,12},{1,13},{2,14},{3,15},{4,16},{5,17},{6,18},{7,19},{8,20},{9,... | collective-permute-start | bytes 196616 | tf_op jit(solution)/shard_map/ppermute | solution.py:52
  80.9 8.8 %collective-permute-start.5 = (bf16[256,128]{1,0:T(8,128)(2,1)S(1)}, bf16[256,128]{1,0:T(8,128)(2,1)S(1)}, u32[]{:S(2)}, u32[]{:S(2)}) collective-permute-start(bf16[256,128]{1,0:T(8,128)(2,1)S(1)} %get-tuple-element.18), channel_id=1, source_target_pairs={{0,16},{1,17},{2,18},{3,19},{4,20},{5,21},{6,22},{7,23},{8,24},{9,... | collective-permute-start | bytes 196616 | tf_op jit(solution)/shard_map/ppermute | solution.py:52
  80.9 8.8 %collective-permute-start.6 = (bf16[256,128]{1,0:T(8,128)(2,1)S(1)}, bf16[256,128]{1,0:T(8,128)(2,1)S(1)}, u32[]{:S(2)}, u32[]{:S(2)}) collective-permute-start(bf16[256,128]{1,0:T(8,128)(2,1)S(1)} %get-tuple-element.17), channel_id=1, source_target_pairs={{0,20},{1,21},{2,22},{3,23},{4,24},{5,25},{6,26},{7,27},{8,28},{9,... | collective-permute-start | bytes 196616 | tf_op jit(solution)/shard_map/ppermute | solution.py:52
  85.2 6.8 %collective-permute-start.7 = (bf16[256,128]{1,0:T(8,128)(2,1)S(1)}, bf16[256,128]{1,0:T(8,128)(2,1)S(1)}, u32[]{:S(2)}, u32[]{:S(2)}) collective-permute-start(bf16[256,128]{1,0:T(8,128)(2,1)S(1)} %get-tuple-element.16), channel_id=1, source_target_pairs={{0,24},{1,25},{2,26},{3,27},{4,28},{5,29},{6,30},{7,31},{8,0},{9,1... | collective-permute-start | bytes 196616 | tf_op jit(solution)/shard_map/ppermute | solution.py:52
  86.5 8.1 %collective-permute-start.8 = (bf16[256,128]{1,0:T(8,128)(2,1)S(1)}, bf16[256,128]{1,0:T(8,128)(2,1)S(1)}, u32[]{:S(2)}, u32[]{:S(2)}) collective-permute-start(bf16[256,128]{1,0:T(8,128)(2,1)S(1)} %get-tuple-element.15), channel_id=1, source_target_pairs={{0,28},{1,29},{2,30},{3,31},{4,0},{5,1},{6,2},{7,3},{8,4},{9,5},{1... | collective-permute-start | bytes 196616 | tf_op jit(solution)/shard_map/ppermute | solution.py:52
  96.2 11.3 %collective-permute-start.25 = (bf16[256,128]{1,0:T(8,128)(2,1)S(1)}, bf16[256,128]{1,0:T(8,128)(2,1)S(1)}, u32[]{:S(2)}, u32[]{:S(2)}) collective-permute-start(bf16[256,128]{1,0:T(8,128)(2,1)S(1)} %get-tuple-element.32), channel_id=1, source_target_pairs={{0,4},{1,5},{2,6},{3,7},{4,8},{5,9},{6,10},{7,11},{8,12},{9,13},{1... | collective-permute-start | bytes 196616 | tf_op jit(solution)/shard_map/ppermute | solution.py:52
  96.8 11.9 %collective-permute-start.26 = (bf16[256,128]{1,0:T(8,128)(2,1)S(1)}, bf16[256,128]{1,0:T(8,128)(2,1)S(1)}, u32[]{:S(2)}, u32[]{:S(2)}) collective-permute-start(bf16[256,128]{1,0:T(8,128)(2,1)S(1)} %get-tuple-element.32), channel_id=1, source_target_pairs={{0,8},{1,9},{2,10},{3,11},{4,12},{5,13},{6,14},{7,15},{8,16},{9,17... | collective-permute-start | bytes 196616 | tf_op jit(solution)/shard_map/ppermute | solution.py:52
  98.5 16.5 %collective-permute-start.27 = (bf16[256,128]{1,0:T(8,128)(2,1)S(1)}, bf16[256,128]{1,0:T(8,128)(2,1)S(1)}, u32[]{:S(2)}, u32[]{:S(2)}) collective-permute-start(bf16[256,128]{1,0:T(8,128)(2,1)S(1)} %get-tuple-element.32), channel_id=1, source_target_pairs={{0,12},{1,13},{2,14},{3,15},{4,16},{5,17},{6,18},{7,19},{8,20},{9,... | collective-permute-start | bytes 196616 | tf_op jit(solution)/shard_map/ppermute | solution.py:52
  100.7 14.5 %collective-permute-start.28 = (bf16[256,128]{1,0:T(8,128)(2,1)S(1)}, bf16[256,128]{1,0:T(8,128)(2,1)S(1)}, u32[]{:S(2)}, u32[]{:S(2)}) collective-permute-start(bf16[256,128]{1,0:T(8,128)(2,1)S(1)} %get-tuple-element.32), channel_id=1, source_target_pairs={{0,16},{1,17},{2,18},{3,19},{4,20},{5,21},{6,22},{7,23},{8,24},{9,... | collective-permute-start | bytes 196616 | tf_op jit(solution)/shard_map/ppermute | solution.py:52
  102.8 13.8 %collective-permute-start.29 = (bf16[256,128]{1,0:T(8,128)(2,1)S(1)}, bf16[256,128]{1,0:T(8,128)(2,1)S(1)}, u32[]{:S(2)}, u32[]{:S(2)}) collective-permute-start(bf16[256,128]{1,0:T(8,128)(2,1)S(1)} %get-tuple-element.32), channel_id=1, source_target_pairs={{0,20},{1,21},{2,22},{3,23},{4,24},{5,25},{6,26},{7,27},{8,28},{9,... | collective-permute-start | bytes 196616 | tf_op jit(solution)/shard_map/ppermute | solution.py:52
  107.5 10.3 %collective-permute-start.30 = (bf16[256,128]{1,0:T(8,128)(2,1)S(1)}, bf16[256,128]{1,0:T(8,128)(2,1)S(1)}, u32[]{:S(2)}, u32[]{:S(2)}) collective-permute-start(bf16[256,128]{1,0:T(8,128)(2,1)S(1)} %get-tuple-element.32), channel_id=1, source_target_pairs={{0,24},{1,25},{2,26},{3,27},{4,28},{5,29},{6,30},{7,31},{8,0},{9,1... | collective-permute-start | bytes 196616 | tf_op jit(solution)/shard_map/ppermute | solution.py:52
  108.7 4.8 %collective-permute-start.17 = (bf16[256,128]{1,0:T(8,128)(2,1)S(1)}, bf16[256,128]{1,0:T(8,128)(2,1)S(1)}, u32[]{:S(2)}, u32[]{:S(2)}) collective-permute-start(bf16[256,128]{1,0:T(8,128)(2,1)S(1)} %convolution_convert_fusion.1), channel_id=1, source_target_pairs={{0,2},{1,3},{2,0},{3,1},{4,6},{5,7},{6,4},{7,5},{8,10},{9,11},{10,... | collective-permute-start | bytes 196616 | tf_op jit(solution)/shard_map/ppermute | solution.py:52
  113.5 7.6 %collective-permute-start.31 = (bf16[256,128]{1,0:T(8,128)(2,1)S(1)}, bf16[256,128]{1,0:T(8,128)(2,1)S(1)}, u32[]{:S(2)}, u32[]{:S(2)}) collective-permute-start(bf16[256,128]{1,0:T(8,128)(2,1)S(1)} %get-tuple-element.32), channel_id=1, source_target_pairs={{0,28},{1,29},{2,30},{3,31},{4,0},{5,1},{6,2},{7,3},{8,4},{9,5},{1... | collective-permute-start | bytes 196616 | tf_op jit(solution)/shard_map/ppermute | solution.py:52
  115.1 8.5 %collective-permute-start.18 = (bf16[2,256,128]{2,1,0:T(8,128)(2,1)S(1)}, bf16[2,256,128]{2,1,0:T(8,128)(2,1)S(1)}, u32[]{:S(2)}, u32[]{:S(2)}) collective-permute-start(bf16[2,256,128]{2,1,0:T(8,128)(2,1)S(1)} %pad_maximum_fusion), channel_id=1, source_target_pairs={{0,4},{1,5},{2,6},{3,7},{4,8},{5,9},{6,10},{7,11},{8,12},{9,13},{1... | collective-permute-start | bytes 393224 | tf_op jit(solution)/shard_map/ppermute | solution.py:52
  115.2 10.9 %collective-permute-start.19 = (bf16[2,256,128]{2,1,0:T(8,128)(2,1)S(1)}, bf16[2,256,128]{2,1,0:T(8,128)(2,1)S(1)}, u32[]{:S(2)}, u32[]{:S(2)}) collective-permute-start(bf16[2,256,128]{2,1,0:T(8,128)(2,1)S(1)} %pad_maximum_fusion), channel_id=1, source_target_pairs={{0,8},{1,9},{2,10},{3,11},{4,12},{5,13},{6,14},{7,15},{8,16},{9,17... | collective-permute-start | bytes 393224 | tf_op jit(solution)/shard_map/ppermute | solution.py:52
  116.7 12.6 %collective-permute-start.20 = (bf16[2,256,128]{2,1,0:T(8,128)(2,1)S(1)}, bf16[2,256,128]{2,1,0:T(8,128)(2,1)S(1)}, u32[]{:S(2)}, u32[]{:S(2)}) collective-permute-start(bf16[2,256,128]{2,1,0:T(8,128)(2,1)S(1)} %pad_maximum_fusion), channel_id=1, source_target_pairs={{0,12},{1,13},{2,14},{3,15},{4,16},{5,17},{6,18},{7,19},{8,20},{9,... | collective-permute-start | bytes 393224 | tf_op jit(solution)/shard_map/ppermute | solution.py:52
  117.8 14.9 %collective-permute-start.21 = (bf16[2,256,128]{2,1,0:T(8,128)(2,1)S(1)}, bf16[2,256,128]{2,1,0:T(8,128)(2,1)S(1)}, u32[]{:S(2)}, u32[]{:S(2)}) collective-permute-start(bf16[2,256,128]{2,1,0:T(8,128)(2,1)S(1)} %pad_maximum_fusion), channel_id=1, source_target_pairs={{0,16},{1,17},{2,18},{3,19},{4,20},{5,21},{6,22},{7,23},{8,24},{9,... | collective-permute-start | bytes 393224 | tf_op jit(solution)/shard_map/ppermute | solution.py:52
  121.2 11.5 %collective-permute-start.22 = (bf16[2,256,128]{2,1,0:T(8,128)(2,1)S(1)}, bf16[2,256,128]{2,1,0:T(8,128)(2,1)S(1)}, u32[]{:S(2)}, u32[]{:S(2)}) collective-permute-start(bf16[2,256,128]{2,1,0:T(8,128)(2,1)S(1)} %pad_maximum_fusion), channel_id=1, source_target_pairs={{0,20},{1,21},{2,22},{3,23},{4,24},{5,25},{6,26},{7,27},{8,28},{9,... | collective-permute-start | bytes 393224 | tf_op jit(solution)/shard_map/ppermute | solution.py:52
  123.6 16.6 %collective-permute-start.23 = (bf16[2,256,128]{2,1,0:T(8,128)(2,1)S(1)}, bf16[2,256,128]{2,1,0:T(8,128)(2,1)S(1)}, u32[]{:S(2)}, u32[]{:S(2)}) collective-permute-start(bf16[2,256,128]{2,1,0:T(8,128)(2,1)S(1)} %pad_maximum_fusion), channel_id=1, source_target_pairs={{0,24},{1,25},{2,26},{3,27},{4,28},{5,29},{6,30},{7,31},{8,0},{9,1... | collective-permute-start | bytes 393224 | tf_op jit(solution)/shard_map/ppermute | solution.py:52
  126.2 18.8 %collective-permute-start.24 = (bf16[2,256,128]{2,1,0:T(8,128)(2,1)S(1)}, bf16[2,256,128]{2,1,0:T(8,128)(2,1)S(1)}, u32[]{:S(2)}, u32[]{:S(2)}) collective-permute-start(bf16[2,256,128]{2,1,0:T(8,128)(2,1)S(1)} %pad_maximum_fusion), channel_id=1, source_target_pairs={{0,28},{1,29},{2,30},{3,31},{4,0},{5,1},{6,2},{7,3},{8,4},{9,5},{1... | collective-permute-start | bytes 393224 | tf_op jit(solution)/shard_map/ppermute | solution.py:52
  129.3 18.3 %collective-permute-start.32 = (bf16[8,256,128]{2,1,0:T(8,128)(2,1)S(1)}, bf16[8,256,128]{2,1,0:T(8,128)(2,1)S(1)}, u32[]{:S(2)}, u32[]{:S(2)}) collective-permute-start(bf16[8,256,128]{2,1,0:T(8,128)(2,1)S(1)} %bitcast_dynamic-update-slice_fusion.8), channel_id=1, source_target_pairs={{0,2},{1,3},{2,0},{3,1},{4,6},{5,7},{6,4},{7,5},{8,10},{9,11},{10,... | collective-permute-start | bytes 1572872 | tf_op jit(solution)/shard_map/ppermute | solution.py:52
  145.0 10.3 %collective-permute-start.33 = (bf16[8,2,256,128]{3,2,1,0:T(8,128)(2,1)S(1)}, bf16[8,2,256,128]{3,2,1,0:T(8,128)(2,1)S(1)}, u32[]{:S(2)}, u32[]{:S(2)}) collective-permute-start(bf16[8,2,256,128]{3,2,1,0:T(8,128)(2,1)S(1)} %bitcast_dynamic-update-slice_fusion), channel_id=1, source_target_pairs={{0,1},{1,0},{2,3},{3,2},{4,5},{5,4},{6,7},{7,6},{8,9},{9,8},{10,11... | collective-permute-start | bytes 3145736 | tf_op jit(solution)/shard_map/ppermute | solution.py:52
  147.5 7.7 %collective-permute-start.34 = (bf16[8,256,128]{2,1,0:T(8,128)(2,1)S(1)}, bf16[8,256,128]{2,1,0:T(8,128)(2,1)}, u32[]{:S(2)}, u32[]{:S(2)}) collective-permute-start(bf16[8,256,128]{2,1,0:T(8,128)(2,1)S(1)} %bitcast_dynamic-update-slice_fusion.8), channel_id=1, source_target_pairs={{0,1},{1,0},{2,3},{3,2},{4,5},{5,4},{6,7},{7,6},{8,9},{9,8},{10,11... | collective-permute-start | bytes 1572872 | tf_op jit(solution)/shard_map/ppermute | solution.py:52
  147.6 7.6 %collective-permute-start.35 = (bf16[8,256,128]{2,1,0:T(8,128)(2,1)S(1)}, bf16[8,256,128]{2,1,0:T(8,128)(2,1)}, u32[]{:S(2)}, u32[]{:S(2)}) collective-permute-start(bf16[8,256,128]{2,1,0:T(8,128)(2,1)S(1)} %collective-permute-done.32), channel_id=1, source_target_pairs={{0,1},{1,0},{2,3},{3,2},{4,5},{5,4},{6,7},{7,6},{8,9},{9,8},{10,11... | collective-permute-start | bytes 1572872 | tf_op jit(solution)/shard_map/ppermute | solution.py:52
  151.8 9.5 %all-to-all-start.2 = ((f32[8,16,256]{2,1,0:T(8,128)}), f32[8,16,256]{2,1,0:T(8,128)S(1)}, u32[]{:S(2)}, u32[]{:S(2)}) async-start(f32[8,16,256]{2,1,0:T(8,128)} %bitcast.60), calls=%async_computation.2 | async-start | bytes 262144 | tf_op jit(solution)/shard_map/all_to_all | solution.py:262
  161.3 30.4 %copy-start.2 = (bf16[256,256]{1,0:T(8,128)(2,1)S(1)}, bf16[256,256]{1,0:T(8,128)(2,1)}, u32[]{:S(2)}) copy-start(bf16[256,256]{1,0:T(8,128)(2,1)} %get-tuple-element.23) | copy-start | bytes 393220
  161.3 30.4 %copy-start.3 = (bf16[256,256]{1,0:T(8,128)(2,1)S(1)}, bf16[256,256]{1,0:T(8,128)(2,1)}, u32[]{:S(2)}) copy-start(bf16[256,256]{1,0:T(8,128)(2,1)} %get-tuple-element.24) | copy-start | bytes 393220
  161.3 35.6 %all-to-all-start.1 = ((bf16[8,512,128]{2,1,0:T(8,128)(2,1)}), bf16[8,512,128]{2,1,0:T(8,128)(2,1)S(1)}, u32[]{:S(2)}, u32[]{:S(2)}) async-start(bf16[8,512,128]{2,1,0:T(8,128)(2,1)} %bitcast.57), calls=%async_computation.1 | async-start | bytes 2097152 | tf_op jit(solution)/shard_map/all_to_all | solution.py:254
  167.1 1.3 collective-permute-start.36
  168.4 14.9 %collective-permute-start.37 = (f32[16,256]{1,0:T(8,128)S(1)}, f32[16,256]{1,0:T(8,128)S(1)}, u32[]{:S(2)}, u32[]{:S(2)}) collective-permute-start(f32[16,256]{1,0:T(8,128)S(1)} %add.194), channel_id=1, source_target_pairs={{0,2},{1,3},{2,0},{3,1},{4,6},{5,7},{6,4},{7,5},{8,10},{9,11},{10,... | collective-permute-start | bytes 49160 | tf_op jit(solution)/shard_map/ppermute | solution.py:52
  183.2 2.6 %collective-permute-start.38 = (f32[16,256]{1,0:T(8,128)S(1)}, f32[16,256]{1,0:T(8,128)S(1)}, u32[]{:S(2)}, u32[]{:S(2)}) collective-permute-start(f32[16,256]{1,0:T(8,128)S(1)} %add.195), channel_id=1, source_target_pairs={{0,4},{1,5},{2,6},{3,7},{4,0},{5,1},{6,2},{7,3},{8,12},{9,13},{10,... | collective-permute-start | bytes 49160 | tf_op jit(solution)/shard_map/ppermute | solution.py:52
  185.8 3.8 %collective-permute-start.39 = (f32[16,256]{1,0:T(8,128)S(1)}, f32[16,256]{1,0:T(8,128)S(1)}, u32[]{:S(2)}, u32[]{:S(2)}) collective-permute-start(f32[16,256]{1,0:T(8,128)S(1)} %add.196), channel_id=1, source_target_pairs={{0,8},{1,9},{2,10},{3,11},{4,12},{5,13},{6,14},{7,15},{8,0},{9,1},... | collective-permute-start | bytes 49160 | tf_op jit(solution)/shard_map/ppermute | solution.py:52
  189.6 6.7 %collective-permute-start.40 = (f32[16,256]{1,0:T(8,128)S(1)}, f32[16,256]{1,0:T(8,128)S(1)}, u32[]{:S(2)}, u32[]{:S(2)}) collective-permute-start(f32[16,256]{1,0:T(8,128)S(1)} %add.197), channel_id=1, source_target_pairs={{0,16},{1,17},{2,18},{3,19},{4,20},{5,21},{6,22},{7,23},{8,24},{9,... | collective-permute-start | bytes 49160 | tf_op jit(solution)/shard_map/ppermute | solution.py:52

commit v2 on v1

--- a/solution.py
+++ b/solution.py
@@ -36,14 +36,16 @@
     return pairs
 
 
-def z_shift(k):
-    return _pairs(lambda xl, y, z, xh, c: (xl, y, (z + k) % 8, xh, c))
-
-
 def z_flip(k):
     return _pairs(lambda xl, y, z, xh, c: (xl, y, z ^ k, xh, c))
 
 
+Z_RING = _pairs(lambda xl, y, z, xh, c: (xl, y, (z + 1 - 2 * c) % 8, xh, c))
+REP_SWAPS = (
+    _pairs(lambda xl, y, z, xh, c: (1 - xl, y, z, xh, c)),
+    _pairs(lambda xl, y, z, xh, c: (xl, y ^ 2, z, xh, c)),
+    _pairs(lambda xl, y, z, xh, c: (xl, y ^ 1, z, xh, c)),
+)
 CORE_SWAP = _pairs(lambda xl, y, z, xh, c: (xl, y, z, xh, 1 - c))
 X_SWAP = _pairs(lambda xl, y, z, xh, c: (xl, y, z, 1 - xh, c))
 
@@ -82,7 +84,7 @@
 
 
 def forward_kernel(
-    land_ref, cols_ref, count_ref, panel_ref, tiles_ref, keep_ref, away_ref, acc, buf, sems
+    land_ref, cols_ref, count_ref, panel_ref, tiles_ref, keep_ref, away_far_ref, away_near_ref, acc, buf, sems
 ):
     def use(s, slot, j):
         acc[land_ref[s]] += jnp.dot(
@@ -92,20 +94,21 @@
     run = stream_tiles(count_ref[0], tiles_ref, buf, sems, use)
     acc[...] = jnp.zeros_like(acc)
     run()
-    half = acc.shape[0] // 2
-    keep_ref[...] = acc[:half].astype(jnp.bfloat16)
-    away_ref[...] = acc[half:].astype(jnp.bfloat16)
+    away_far_ref[...] = acc[96:].astype(jnp.bfloat16)
+    away_near_ref[...] = acc[64:96].astype(jnp.bfloat16)
+    keep_ref[...] = acc[:64].astype(jnp.bfloat16)
 
 
 def forward_products(land, cols, count, panel, tiles):
     smem = pl.BlockSpec(memory_space=pltpu.SMEM)
     vmem = pl.BlockSpec(memory_space=pltpu.VMEM)
-    half = jax.ShapeDtypeStruct((64, BS, BS), jnp.bfloat16)
+    kept = jax.ShapeDtypeStruct((64, BS, BS), jnp.bfloat16)
+    away = jax.ShapeDtypeStruct((32, BS, BS), jnp.bfloat16)
     return pl.pallas_call(
         forward_kernel,
-        out_shape=(half, half),
+        out_shape=(kept, away, away),
         in_specs=[smem, smem, smem, vmem, pl.BlockSpec(memory_space=pl.ANY)],
-        out_specs=(vmem, vmem),
+        out_specs=(vmem, vmem, vmem),
         scratch_shapes=[
             pltpu.VMEM((128, BS, BS), jnp.float32),
             pltpu.VMEM((BUFFERS, GROUP, BS, BS), jnp.bfloat16),
@@ -119,28 +122,40 @@
     )(land, cols, count, panel, tiles)
 
 
-def backward_kernel(
-    land_ref, cols_ref, count_ref, *refs
-):
+def piece_plan(refs):
+    near, far, cores = refs[:5], refs[5:10], refs[10:]
+    plan = []
+    at = 0
+    for side, ring in enumerate((near, far)):
+        for ref in ring:
+            plan.append((ref, 0, at, ref.shape[0]))
+            at += ref.shape[0]
+        for ref in cores:
+            size = ref.shape[0] // 2
+            plan.append((ref, side * size, at, size))
+            at += size
+    return plan
+
+
+def backward_kernel(land_ref, cols_ref, count_ref, *refs):
     piece_refs = refs[:-6]
     tiles_ref, out_ref, acc, buf, grads, sems = refs[-6:]
 
     def use(s, slot, j):
         acc[cols_ref[s]] += lax.dot_general(
             buf[slot, j],
-            grads[land_ref[s]],
+            grads[pl.ds(pl.multiple_of(land_ref[s] * BS, BS), BS)],
             (((0,), (0,)), ((), ())),
             preferred_element_type=jnp.float32,
         )
 
     copies = []
-    at = 0
-    for i, ref in enumerate(piece_refs):
-        size = ref.shape[0]
+    for i, (ref, start, at, size) in enumerate(piece_plan(piece_refs)):
         copies.append(
-            pltpu.make_async_copy(ref, grads.at[pl.ds(at, size)], sems.at[BUFFERS + i])
+            pltpu.make_async_copy(
+                ref.at[pl.ds(start, size)], grads.at[pl.ds(at, size)], sems.at[BUFFERS + i]
+            )
         )
-        at += size
     for one in copies:
         one.start()
     run = stream_tiles(count_ref[0], tiles_ref, buf, sems, use)
@@ -151,7 +166,8 @@
     out_ref[...] = acc[...].astype(jnp.bfloat16)
 
 
-def backward_products(land, cols, count, pieces, tiles):
+def backward_products(land, cols, count, near, far, cores, tiles):
+    pieces = near + far + cores
     smem = pl.BlockSpec(memory_space=pltpu.SMEM)
     vmem = pl.BlockSpec(memory_space=pltpu.VMEM)
     hbm = pl.BlockSpec(memory_space=pl.ANY)
@@ -163,8 +179,8 @@
         scratch_shapes=[
             pltpu.VMEM((32, BS, BS), jnp.float32),
             pltpu.VMEM((BUFFERS, GROUP, BS, BS), jnp.bfloat16),
-            pltpu.VMEM((128, BS, BS), jnp.bfloat16),
-            pltpu.SemaphoreType.DMA((BUFFERS + len(pieces),)),
+            pltpu.VMEM((128 * BS, BS), jnp.bfloat16),
+            pltpu.SemaphoreType.DMA((BUFFERS + 18,)),
         ],
         compiler_params=pltpu.CompilerParams(vmem_limit_bytes=40 << 20),
         cost_estimate=pl.CostEstimate(
@@ -172,6 +188,38 @@
         ),
         name="backward_products",
     )(land, cols, count, *pieces, tiles)
+
+
+def halve(value, side, swap):
+    size = value.shape[0] // 2
+    mine = lax.dynamic_slice_in_dim(value, side * size, size, 0)
+    other = lax.dynamic_slice_in_dim(value, (1 - side) * size, size, 0)
+    return mine + send(other, swap)
+
+
+def tied(*values):
+    return lax.optimization_barrier(values)
+
+
+def forward_slot(j, rel_c, rel_x):
+    mine = ((j >= 1) & (j <= 3)) | (((j == 0) | (j == 4)) & (rel_c == 0))
+    j = jnp.where(mine, j, (NZ - j) % NZ)
+    rel_c = jnp.where(mine, rel_c, 1 - rel_c)
+    block = jnp.where(j == 4, 0, jnp.where(j == 0, 7, 7 - 2 * j + rel_c))
+    return jnp.where(mine, 0, 16) + rel_x * 8 + block
+
+
+def backward_slot(j, rel_c, rel_x):
+    block = jnp.where(j < 4, 2 * j + rel_c, 9 + 2 * (7 - j) + 1 - rel_c)
+    block = jnp.where(j == 4, jnp.where(rel_c == 0, 8, 15), block)
+    return rel_x * 16 + block
+
+
+def total_of(*terms):
+    total = terms[0].astype(jnp.float32)
+    for term in terms[1:]:
+        total = total + term.astype(jnp.float32)
+    return total.astype(jnp.bfloat16)
 
 
 def add_pair(a, b):
@@ -206,63 +254,71 @@
     xh = lax.axis_index("xh")
     c = lax.axis_index("c")
     panel_at = rows // 4
-    q = rows % 4
-    half, low = q // 2, q % 2
     row_z, row_x, row_c = panel_at // 4, (panel_at // 2) % 2, panel_at % 2
     rel_c, rel_x = row_c ^ c, row_x ^ xh
-    rel_out = (row_z - z) % NZ
-    rel_in = (z - row_z) % NZ
-    land_fwd = (((rel_c * 2 + half) * 2 + rel_x) * NZ + rel_out) * 2 + low
-    land_bwd = (
-        rel_c * 64
-        + half * 32
-        + jnp.where(half == 0, rel_in * 4 + rel_x * 2, rel_x * 16 + rel_in * 2)
-        + low
-    )
+    ahead, behind = (row_z - z) % NZ, (z - row_z) % NZ
+    land_fwd = forward_slot(jnp.where(c == 0, ahead, behind), rel_c, rel_x) * 4 + rows % 4
+    land_bwd = backward_slot(jnp.where(c == 0, behind, ahead), rel_c, rel_x) * 4 + rows % 4
 
     panel = lax.all_to_all(jnp.broadcast_to(features, (8, 512, BS)), REP, 0, 0)
-    keep, away = forward_products(land_fwd, cols, count, panel.reshape(32, BS, BS), tiles)
-    summed = add_pair(keep, send(away, CORE_SWAP)).reshape(2, 2, NZ, 256, BS)
-
-    first = add_pair(summed[0, 0], send(summed[0, 1], X_SWAP))
-    total_a = first[0].astype(jnp.float32)
-    for k in range(1, NZ):
-        total_a = total_a + send(first[k], z_shift(k)).astype(jnp.float32)
-    second = summed[1]
-    total_b = second[:, 0].astype(jnp.float32)
-    for k in range(1, NZ):
-        total_b = total_b + send(second[:, k], z_shift(k)).astype(jnp.float32)
-    total_b = total_b[0] + send(total_b[1].astype(jnp.bfloat16), X_SWAP).astype(jnp.float32)
+    keep, away_far, away_near = forward_products(
+        land_fwd, cols, count, panel.reshape(32, BS, BS), tiles
+    )
+    far = add_pair(keep[32:], send(away_far, CORE_SWAP)).reshape(8, 512, BS)
+    away_near, far = tied(away_near, far)
+    far_sum = send(far[0], Z_RING)
+    near = add_pair(keep[:32], send(away_near, CORE_SWAP)).reshape(8, 512, BS)
+    near_sum = send(near[0], Z_RING)
+    far_sum = jnp.stack([add_pair(far[1], far_sum), far[2]])
+    near_sum = jnp.stack([add_pair(near[1], near_sum), near[2]])
+    for at in (3, 5):
+        far_sum = add_pair(far[at : at + 2], send(far_sum, Z_RING))
+        near_sum = add_pair(near[at : at + 2], send(near_sum, Z_RING))
+    far_sum = send(far_sum, Z_RING)
+    near_sum = send(near_sum, Z_RING)
+    far_sum = total_of(far[7], far_sum[0], send(far_sum[1], CORE_SWAP))
+    far_sum = send(far_sum, X_SWAP)
+    near_side = send(near_sum[1], CORE_SWAP)
+    total = (
+        (near[7].astype(jnp.float32) + near_sum[0].astype(jnp.float32))
+        + (near_side.astype(jnp.float32) + far_sum.astype(jnp.float32))
+    )
 
     scale = self_weight[0][:, None]
-    act_a, weight_a, grad_a = dense(
-        total_a, scale[:256], features[0, :256], weight, cotangent[0, :256]
-    )
-    act_b, weight_b, grad_b = dense(
-        total_b, scale[256:], features[0, 256:], weight, cotangent[0, 256:]
-    )
-    activated = jnp.concatenate([act_a, act_b], 0)[None]
-
-    pair = jnp.stack([grad_a, send(grad_a, X_SWAP)])
-    got_a = jnp.stack([pair] + [send(pair, z_shift(k)) for k in range(1, NZ)])
-    got_b = jnp.stack([grad_b] + [send(grad_b, z_shift(k)) for k in range(1, NZ)])
-    got_bx = send(got_b, X_SWAP)
-    pieces = [got_a, got_b, got_bx]
-    pieces = pieces + [send(piece, CORE_SWAP) for piece in pieces]
-    pieces = [piece.reshape(-1, BS, BS) for piece in pieces]
-    columns = backward_products(land_bwd, cols, count, pieces, tiles)
+    activated, weight_sum, row_grad = dense(total, scale, features[0], weight, cotangent[0])
+    row_grad, weight_sum = tied(row_grad, weight_sum * (1.0 / math.sqrt(32 * 8 * 512)))
+    y = lax.axis_index("y")
+    sides = (lax.axis_index("xl"), y // 2, y % 2)
+
+    near = jnp.concatenate([row_grad, send(row_grad, CORE_SWAP)], 0)
+    x_own = send(row_grad, X_SWAP)
+    weight_sum = weight_sum + send(weight_sum, CORE_SWAP)
+    x_weight = send(weight_sum, X_SWAP)
+    near_ring = [near]
+    near_ring.append(send(near, Z_RING))
+    x_own, x_weight = tied(x_own, x_weight)
+    weight_sum = weight_sum + x_weight
+    far = jnp.concatenate([x_own, send(x_own, CORE_SWAP)], 0)
+    far_ring = [far]
+    far_ring.append(send(far, Z_RING))
+    cores = []
+    for hop in (2, 3, 4):
+        size = 1024 if hop < 4 else 512
+        cores.append(send(jnp.concatenate([near_ring[-1], far_ring[-1]], 0), CORE_SWAP))
+        near_ring.append(send(near_ring[-1][:size], Z_RING))
+        weight_sum = halve(weight_sum, sides[hop - 2], REP_SWAPS[hop - 2])
+        near_ring[-1], weight_sum = tied(near_ring[-1], weight_sum)
+        far_ring.append(send(far_ring[-1][:size], Z_RING))
+    cores.append(send(jnp.concatenate([near_ring[-1], far_ring[-1]], 0), CORE_SWAP))
+    columns = backward_products(land_bwd, cols, count, near_ring, far_ring, cores, tiles)
+    columns, weight_sum = tied(columns, weight_sum)
     parts = lax.all_to_all(columns.reshape(8, 512, BS), REP, 0, 0)
-    row_grad = jnp.concatenate([grad_a, grad_b], 0)
+    for k in (1, 2, 4):
+        weight_sum = weight_sum + send(weight_sum, z_flip(k))
     feature_grad = (
         jnp.sum(parts.astype(jnp.float32), 0) + scale * row_grad.astype(jnp.float32)
     ).astype(jnp.bfloat16)[None]
-
-    node_total = 32 * 8 * 512
-    weight_sum = (weight_a + weight_b) * (1.0 / math.sqrt(node_total))
-    weight_sum = jnp.sum(lax.all_to_all(weight_sum.reshape(8, 16, 256), REP, 0, 0), 0)
-    for move in (CORE_SWAP, X_SWAP, z_flip(1), z_flip(2), z_flip(4)):
-        weight_sum = weight_sum + send(weight_sum, move)
-    return activated, feature_grad, weight_sum
+    return activated[None], feature_grad, weight_sum
 
 
 def solution(mesh):

time: 201 us -> 154 us (0.77)
  waiting for transfers between devices: 79.7 us -> 48.8 us
  starting transfers between devices: 97 us -> 83.3 us
    ppermute x41 -> x36, waiting for transfers between devices: 65.5 us -> 34.6 us  [send(): return lax.ppermute(value, AXES, pairs)]
    ppermute x41 -> x36, starting transfers between devices: 81.8 us -> 73.1 us  [send(): return lax.ppermute(value, AXES, pairs)]
    all_to_all x1 -> x0, starting transfers between devices: 3.45 us -> none  [on_device(): lax.all_to_all(weight_sum.reshape(8, 16, 256), REP, 0, 0)]
  transfers between devices with their start and end apart: 44 -> 38, of which waited for: 19 -> 21; matrix products, arithmetic and copies ran while one was open for 2% -> 1% of each run, Pallas kernels for 3% -> 0%
where the time goes in v2:
time: 154 us; the launch traced here: 152 us
  starting transfers between devices  83.3 us (54%)
  waiting for transfers between devices  48.8 us (32%)
  Pallas kernels  11.2 us (7%)
  other arithmetic  3.31 us (2%)
  local copies, waits for them, and re-layouts  2.31 us (2%)
  between operations  1.65 us (1%)
    ppermute x36, starting transfers between devices, send(): return lax.ppermute(value, AXES, pairs)  73.1 us
    ppermute x36, waiting for transfers between devices, send(): return lax.ppermute(value, AXES, pairs)  34.6 us
    all_to_all x1, waiting for transfers between devices, on_device(): panel = lax.all_to_all(jnp.broadcast_to(features, (8, 512, BS)), REP, 0, 0)  14.1 us
    pallas_call x1, Pallas kernels, backward_products(): pl.pallas_call(backward_kernel, out_shape=jax.ShapeDtypeStruct((32, BS, B...  6.56 us
    all_to_all x1, starting transfers between devices, on_device(): panel = lax.all_to_all(jnp.broadcast_to(features, (8, 512, BS)), REP, 0, 0)  5.95 us
    pallas_call x1, Pallas kernels, forward_products(): pl.pallas_call(forward_kernel, out_shape=(kept, away, away), in_specs=[sm...  4.65 us
    all_to_all x1, starting transfers between devices, on_device(): parts = lax.all_to_all(columns.reshape(8, 512, BS), REP, 0, 0)  4.23 us
  transfers between devices with their start and end apart: 38, of which 21 were waited for; matrix products, arithmetic and copies ran while one was open for 1% of the time, Pallas kernels for 0%

profile of v2, /device:TPU:1, one launch (start us, length us, event | category | flops | bytes accessed | tf_op | source)
XLA Modules:
  0.0 152.1 jit_solution(6065474739865393000)
XLA Ops:
  0.7 2.1 %broadcast_in_dim.28 = bf16[8,512,128]{2,1,0:T(8,128)(2,1)} broadcast(bf16[512,128]{1,0:T(8,128)(2,1)} %bitcast.71), dimensions={1,2} | broadcast | bytes 1179648 | tf_op jit(solution)/shard_map/broadcast_in_dim | solution.py:263
  2.7 5.9 %all-to-all-start = ((bf16[8,512,128]{2,1,0:T(8,128)(2,1)}), bf16[8,512,128]{2,1,0:T(8,128)(2,1)S(1)}, u32[]{:S(2)}, u32[]{:S(2)}) async-start(bf16[8,512,128]{2,1,0:T(8,128)(2,1)} %broadcast_in_dim.28), calls=%async_computation | async-start | bytes 2097152 | tf_op jit(solution)/shard_map/all_to_all | solution.py:263
  9.5 14.1 %all-to-all-done = bf16[8,512,128]{2,1,0:T(8,128)(2,1)S(1)} async-done(((bf16[8,512,128]{2,1,0:T(8,128)(2,1)}), bf16[8,512,128]{2,1,0:T(8,128)(2,1)S(1)}, u32[]{:S(2)}, u32[]{:S(2)}) %all-to-all-start) | async-done | bytes 1048608 | tf_op jit(solution)/shard_map/all_to_all | solution.py:263
  23.6 4.6 %forward_products.1 = (bf16[64,128,128]{2,1,0:T(8,128)(2,1)S(1)}, bf16[32,128,128]{2,1,0:T(8,128)(2,1)S(1)}, bf16[32,128,128]{2,1,0:T(8,128)(2,1)S(1)}) custom-call(s32[384]{0:T(512)S(1)} %fusion.26.land_ref, s32[384]{0:T(512)S(1)} %reduce.1.cols_ref, s32[1]{0:T(128)} %bitcast.59.count_ref, bf16[32,128,128]{2,1,0:T(8,128)(2,1)S(1)} %bitcast.61, ...), custom_call_target="tpu_custom_call" | custom-call | flops 1610612736 | bytes 18874368 | tf_op jit(solution)/shard_map/forward_products/pallas_call | solution.py:107
  28.3 2.6 %collective-permute-done = bf16[32,128,128]{2,1,0:T(8,128)(2,1)S(1)} collective-permute-done((bf16[32,128,128]{2,1,0:T(8,128)(2,1)S(1)}, bf16[32,128,128]{2,1,0:T(8,128)(2,1)S(1)}, u32[]{:S(2)}, u32[]{:S(2)}) %collective-permute-start) | collective-permute-done | bytes 1048608 | tf_op jit(solution)/shard_map/ppermute | solution.py:54
  31.0 0.4 add_convert_fusion.1
  31.4 0.2 collective-permute-start.1
  31.6 6.1 %collective-permute-start.7 = (bf16[512,128]{1,0:T(8,128)(2,1)S(1)}, bf16[512,128]{1,0:T(8,128)(2,1)S(1)}, u32[]{:S(2)}, u32[]{:S(2)}) collective-permute-start(bf16[512,128]{1,0:T(8,128)(2,1)S(1)} %get-tuple-element.45), channel_id=1, source_target_pairs={{0,4},{1,29},{2,6},{3,31},{4,8},{5,1},{6,10},{7,3},{8,12},{9,5},{1... | collective-permute-start | bytes 393224 | tf_op jit(solution)/shard_map/ppermute | solution.py:54
  37.7 1.9 %collective-permute-done.7 = bf16[512,128]{1,0:T(8,128)(2,1)S(1)} collective-permute-done((bf16[512,128]{1,0:T(8,128)(2,1)S(1)}, bf16[512,128]{1,0:T(8,128)(2,1)S(1)}, u32[]{:S(2)}, u32[]{:S(2)}) %collective-permute-start.7) | collective-permute-done | bytes 131104 | tf_op jit(solution)/shard_map/ppermute | solution.py:54
  39.7 3.2 %collective-permute-start.8 = (bf16[2,512,128]{2,1,0:T(8,128)(2,1)S(1)}, bf16[2,512,128]{2,1,0:T(8,128)(2,1)S(1)}, u32[]{:S(2)}, u32[]{:S(2)}) collective-permute-start(bf16[2,512,128]{2,1,0:T(8,128)(2,1)S(1)} %pad_maximum_fusion.4), channel_id=1, source_target_pairs={{0,4},{1,29},{2,6},{3,31},{4,8},{5,1},{6,10},{7,3},{8,12},{9,5},{1... | collective-permute-start | bytes 786440 | tf_op jit(solution)/shard_map/ppermute | solution.py:54
  42.9 0.5 add_convert_fusion
  43.5 2.7 %collective-permute-done.8 = bf16[2,512,128]{2,1,0:T(8,128)(2,1)S(1)} collective-permute-done((bf16[2,512,128]{2,1,0:T(8,128)(2,1)S(1)}, bf16[2,512,128]{2,1,0:T(8,128)(2,1)S(1)}, u32[]{:S(2)}, u32[]{:S(2)}) %collective-permute-start.8) | collective-permute-done | bytes 262176 | tf_op jit(solution)/shard_map/ppermute | solution.py:54
  46.3 3.2 %collective-permute-start.9 = (bf16[2,512,128]{2,1,0:T(8,128)(2,1)S(1)}, bf16[2,512,128]{2,1,0:T(8,128)(2,1)S(1)}, u32[]{:S(2)}, u32[]{:S(2)}) collective-permute-start(bf16[2,512,128]{2,1,0:T(8,128)(2,1)S(1)} %add_convert_fusion.3), channel_id=1, source_target_pairs={{0,4},{1,29},{2,6},{3,31},{4,8},{5,1},{6,10},{7,3},{8,12},{9,5},{1... | collective-permute-start | bytes 786440 | tf_op jit(solution)/shard_map/ppermute | solution.py:54
  49.6 1.3 collective-permute-start.3
  50.9 1.9 %collective-permute-done.9 = bf16[2,512,128]{2,1,0:T(8,128)(2,1)S(1)} collective-permute-done((bf16[2,512,128]{2,1,0:T(8,128)(2,1)S(1)}, bf16[2,512,128]{2,1,0:T(8,128)(2,1)S(1)}, u32[]{:S(2)}, u32[]{:S(2)}) %collective-permute-start.9) | collective-permute-done | bytes 262176 | tf_op jit(solution)/shard_map/ppermute | solution.py:54
  52.9 3.2 %collective-permute-start.10 = (bf16[2,512,128]{2,1,0:T(8,128)(2,1)S(1)}, bf16[2,512,128]{2,1,0:T(8,128)(2,1)S(1)}, u32[]{:S(2)}, u32[]{:S(2)}) collective-permute-start(bf16[2,512,128]{2,1,0:T(8,128)(2,1)S(1)} %add_convert_fusion.2), channel_id=1, source_target_pairs={{0,4},{1,29},{2,6},{3,31},{4,8},{5,1},{6,10},{7,3},{8,12},{9,5},{1... | collective-permute-start | bytes 786440 | tf_op jit(solution)/shard_map/ppermute | solution.py:54
  56.2 2.7 %collective-permute-start.4 = (bf16[2,512,128]{2,1,0:T(8,128)(2,1)S(1)}, bf16[2,512,128]{2,1,0:T(8,128)(2,1)S(1)}, u32[]{:S(2)}, u32[]{:S(2)}) collective-permute-start(bf16[2,512,128]{2,1,0:T(8,128)(2,1)S(1)} %fusion.1), channel_id=1, source_target_pairs={{0,4},{1,29},{2,6},{3,31},{4,8},{5,1},{6,10},{7,3},{8,12},{9,5},{1... | collective-permute-start | bytes 786440 | tf_op jit(solution)/shard_map/ppermute | solution.py:54
  58.9 0.5 collective-permute-done.10
  59.4 5.2 %collective-permute-start.11 = (bf16[512,128]{1,0:T(8,128)(2,1)S(1)}, bf16[512,128]{1,0:T(8,128)(2,1)S(1)}, u32[]{:S(2)}, u32[]{:S(2)}) collective-permute-start(bf16[512,128]{1,0:T(8,128)(2,1)S(1)} %slice_bitcast_fusion), channel_id=1, source_target_pairs={{0,1},{1,0},{2,3},{3,2},{4,5},{5,4},{6,7},{7,6},{8,9},{9,8},{10,11... | collective-permute-start | bytes 393224 | tf_op jit(solution)/shard_map/ppermute | solution.py:54
  64.7 0.8 collective-permute-start.5
  65.5 0.2 collective-permute-done.11
  65.7 3.1 %collective-permute-start.12 = (bf16[512,128]{1,0:T(8,128)(2,1)S(1)}, bf16[512,128]{1,0:T(8,128)(2,1)S(1)}, u32[]{:S(2)}, u32[]{:S(2)}) collective-permute-start(bf16[512,128]{1,0:T(8,128)(2,1)S(1)} %fusion.8), channel_id=1, source_target_pairs={{0,2},{1,3},{2,0},{3,1},{4,6},{5,7},{6,4},{7,5},{8,10},{9,11},{10,... | collective-permute-start | bytes 393224 | tf_op jit(solution)/shard_map/ppermute | solution.py:54
  68.8 1.2 collective-permute-done.5
  70.0 5.3 %collective-permute-start.6 = (bf16[512,128]{1,0:T(8,128)(2,1)S(1)}, bf16[512,128]{1,0:T(8,128)(2,1)S(1)}, u32[]{:S(2)}, u32[]{:S(2)}) collective-permute-start(bf16[512,128]{1,0:T(8,128)(2,1)S(1)} %slice_bitcast_fusion.1), channel_id=1, source_target_pairs={{0,1},{1,0},{2,3},{3,2},{4,5},{5,4},{6,7},{7,6},{8,9},{9,8},{10,11... | collective-permute-start | bytes 393224 | tf_op jit(solution)/shard_map/ppermute | solution.py:54
  75.3 1.0 collective-permute-done.6
  76.5 1.1 fusion
  77.6 0.2 convolution_multiply_fusion
  77.8 0.2 convolution_convert_fusion
  78.0 0.4 collective-permute-start.16
  78.5 0.1 collective-permute-start.13
  78.6 2.9 %collective-permute-start.17 = (bf16[512,128]{1,0:T(8,128)(2,1)S(1)}, bf16[512,128]{1,0:T(8,128)(2,1)S(1)}, u32[]{:S(2)}, u32[]{:S(2)}) collective-permute-start(bf16[512,128]{1,0:T(8,128)(2,1)S(1)} %convolution_convert_fusion), channel_id=1, source_target_pairs={{0,2},{1,3},{2,0},{3,1},{4,6},{5,7},{6,4},{7,5},{8,10},{9,11},{10,... | collective-permute-start | bytes 393224 | tf_op jit(solution)/shard_map/ppermute | solution.py:54
  81.6 0.9 collective-permute-start.18
  82.6 0.4 collective-permute-start.14
  83.0 1.9 %collective-permute-done.17 = bf16[512,128]{1,0:T(8,128)(2,1)S(1)} collective-permute-done((bf16[512,128]{1,0:T(8,128)(2,1)S(1)}, bf16[512,128]{1,0:T(8,128)(2,1)S(1)}, u32[]{:S(2)}, u32[]{:S(2)}) %collective-permute-start.17) | collective-permute-done | bytes 131104 | tf_op jit(solution)/shard_map/ppermute | solution.py:54
  84.9 2.8 %collective-permute-done.18 = f32[128,256]{1,0:T(8,128)S(1)} collective-permute-done((f32[128,256]{1,0:T(8,128)S(1)}, f32[128,256]{1,0:T(8,128)S(1)}, u32[]{:S(2)}, u32[]{:S(2)}) %collective-permute-start.18) | collective-permute-done | bytes 131104 | tf_op jit(solution)/shard_map/ppermute | solution.py:54
  87.7 1.6 %collective-permute-start.24 = (bf16[512,128]{1,0:T(8,128)(2,1)S(1)}, bf16[512,128]{1,0:T(8,128)(2,1)S(1)}, u32[]{:S(2)}, u32[]{:S(2)}) collective-permute-start(bf16[512,128]{1,0:T(8,128)(2,1)S(1)} %collective-permute-done.17), channel_id=1, source_target_pairs={{0,1},{1,0},{2,3},{3,2},{4,5},{5,4},{6,7},{7,6},{8,9},{9,8},{10,11... | collective-permute-start | bytes 393224 | tf_op jit(solution)/shard_map/ppermute | solution.py:54
  89.3 0.9 collective-permute-start.19
  90.2 0.4 collective-permute-start.15
  90.8 2.1 %collective-permute-done.19 = f32[64,256]{1,0:T(8,128)S(1)} collective-permute-done((f32[64,256]{1,0:T(8,128)S(1)}, f32[64,256]{1,0:T(8,128)S(1)}, u32[]{:S(2)}, u32[]{:S(2)}) %collective-permute-start.19) | collective-permute-done | bytes 65568 | tf_op jit(solution)/shard_map/ppermute | solution.py:54
  92.8 3.0 %collective-permute-done.15.refs_2_ = bf16[1024,128]{1,0:T(8,128)(2,1)S(1)} collective-permute-done((bf16[1024,128]{1,0:T(8,128)(2,1)S(1)}, bf16[1024,128]{1,0:T(8,128)(2,1)S(1)}, u32[]{:S(2)}, u32[]{:S(2)}) %collective-permute-start.15) | collective-permute-done | bytes 262176 | tf_op jit(solution)/shard_map/ppermute | solution.py:54
  95.8 1.1 collective-permute-start.21
  96.9 1.2 collective-permute-start.20
  98.1 0.5 collective-permute-done.25.refs_6_
  98.6 1.2 collective-permute-start.26
  99.9 1.5 collective-permute-start.29
  101.4 0.7 collective-permute-done.20.refs_3_
  102.1 3.1 %collective-permute-done.26.refs_7_ = bf16[1024,128]{1,0:T(8,128)(2,1)S(1)} collective-permute-done((bf16[1024,128]{1,0:T(8,128)(2,1)S(1)}, bf16[1024,128]{1,0:T(8,128)(2,1)S(1)}, u32[]{:S(2)}, u32[]{:S(2)}) %collective-permute-start.26) | collective-permute-done | bytes 262176 | tf_op jit(solution)/shard_map/ppermute | solution.py:54
  105.2 2.2 %collective-permute-start.27 = (bf16[1024,128]{1,0:T(8,128)(2,1)S(1)}, bf16[1024,128]{1,0:T(8,128)(2,1)S(1)}, u32[]{:S(2)}, u32[]{:S(2)}) collective-permute-start(bf16[1024,128]{1,0:T(8,128)(2,1)S(1)} %collective-permute-done.26.refs_7_), channel_id=1, source_target_pairs={{0,4},{1,29},{2,6},{3,31},{4,8},{5,1},{6,10},{7,3},{8,12},{9,5},{1... | collective-permute-start | bytes 786440 | tf_op jit(solution)/shard_map/ppermute | solution.py:54
  107.4 0.6 collective-permute-start.23
  108.1 3.1 %collective-permute-start.30 = (bf16[2048,128]{1,0:T(8,128)(2,1)S(1)}, bf16[2048,128]{1,0:T(8,128)(2,1)S(1)}, u32[]{:S(2)}, u32[]{:S(2)}) collective-permute-start(bf16[2048,128]{1,0:T(8,128)(2,1)S(1)} %pad_maximum_fusion.1), channel_id=1, source_target_pairs={{0,1},{1,0},{2,3},{3,2},{4,5},{5,4},{6,7},{7,6},{8,9},{9,8},{10,11... | collective-permute-start | bytes 1572872 | tf_op jit(solution)/shard_map/ppermute | solution.py:54
  111.2 3.2 %collective-permute-start.28 = (bf16[512,128]{1,0:T(8,128)(2,1)S(1)}, bf16[512,128]{1,0:T(8,128)(2,1)S(1)}, u32[]{:S(2)}, u32[]{:S(2)}) collective-permute-start(bf16[512,128]{1,0:T(8,128)(2,1)S(1)} %slice.99), channel_id=1, source_target_pairs={{0,4},{1,29},{2,6},{3,31},{4,8},{5,1},{6,10},{7,3},{8,12},{9,5},{1... | collective-permute-start | bytes 393224 | tf_op jit(solution)/shard_map/ppermute | solution.py:54
  114.5 3.6 %collective-permute-start.31 = (bf16[2048,128]{1,0:T(8,128)(2,1)S(1)}, bf16[2048,128]{1,0:T(8,128)(2,1)S(1)}, u32[]{:S(2)}, u32[]{:S(2)}) collective-permute-start(bf16[2048,128]{1,0:T(8,128)(2,1)S(1)} %pad_maximum_fusion.2), channel_id=1, source_target_pairs={{0,1},{1,0},{2,3},{3,2},{4,5},{5,4},{6,7},{7,6},{8,9},{9,8},{10,11... | collective-permute-start | bytes 1572872 | tf_op jit(solution)/shard_map/ppermute | solution.py:54
  118.1 6.1 %collective-permute-start.32 = (bf16[1024,128]{1,0:T(8,128)(2,1)S(1)}, bf16[1024,128]{1,0:T(8,128)(2,1)S(1)}, u32[]{:S(2)}, u32[]{:S(2)}) collective-permute-start(bf16[1024,128]{1,0:T(8,128)(2,1)S(1)} %pad_maximum_fusion.5), channel_id=1, source_target_pairs={{0,1},{1,0},{2,3},{3,2},{4,5},{5,4},{6,7},{7,6},{8,9},{9,8},{10,11... | collective-permute-start | bytes 786440 | tf_op jit(solution)/shard_map/ppermute | solution.py:54
  124.2 1.2 collective-permute-done.32.refs_13_
  125.4 6.6 %backward_products.1 = bf16[32,128,128]{2,1,0:T(8,128)(2,1)} custom-call(s32[384]{0:T(512)S(1)} %get-tuple-element.37.land_ref, s32[384]{0:T(512)S(1)} %reduce.1.cols_ref, s32[1]{0:T(128)} %bitcast.60.count_ref, bf16[1024,128]{1,0:T(8,128)(2,1)S(1)} %constant_dynamic-update-slice_fusion.refs_0_, bf16[1024,128]{1,0:T(8,128)(2,1)S(1)} %collective-permute-done.14.refs_1_, ...), custom_call_target="tpu_custom_call" | custom-call | flops 1610612736 | bytes 18874368 | tf_op jit(solution)/shard_map/backward_products/pallas_call | solution.py:174
  132.0 4.2 %all-to-all-start.1 = ((bf16[8,512,128]{2,1,0:T(8,128)(2,1)}), bf16[8,512,128]{2,1,0:T(8,128)(2,1)S(1)}, u32[]{:S(2)}, u32[]{:S(2)}) async-start(bf16[8,512,128]{2,1,0:T(8,128)(2,1)} %bitcast.22), calls=%async_computation.1 | async-start | bytes 2097152 | tf_op jit(solution)/shard_map/all_to_all | solution.py:315
  136.2 2.6 %collective-permute-done.33 = f32[16,256]{1,0:T(8,128)S(1)} collective-permute-done((f32[16,256]{1,0:T(8,128)S(1)}, f32[16,256]{1,0:T(8,128)S(1)}, u32[]{:S(2)}, u32[]{:S(2)}) %collective-permute-start.33) | collective-permute-done | bytes 16416 | tf_op jit(solution)/shard_map/ppermute | solution.py:54
  138.8 3.7 %collective-permute-start.34 = (f32[16,256]{1,0:T(8,128)S(1)}, f32[16,256]{1,0:T(8,128)S(1)}, u32[]{:S(2)}, u32[]{:S(2)}) collective-permute-start(f32[16,256]{1,0:T(8,128)S(1)} %add.207), channel_id=1, source_target_pairs={{0,8},{1,9},{2,10},{3,11},{4,12},{5,13},{6,14},{7,15},{8,0},{9,1},... | collective-permute-start | bytes 49160 | tf_op jit(solution)/shard_map/ppermute | solution.py:54
  142.5 1.4 collective-permute-done.34
  143.9 3.2 %collective-permute-start.35 = (f32[16,256]{1,0:T(8,128)S(1)}, f32[16,256]{1,0:T(8,128)S(1)}, u32[]{:S(2)}, u32[]{:S(2)}) collective-permute-start(f32[16,256]{1,0:T(8,128)S(1)} %add.208), channel_id=1, source_target_pairs={{0,16},{1,17},{2,18},{3,19},{4,20},{5,21},{6,22},{7,23},{8,24},{9,... | collective-permute-start | bytes 49160 | tf_op jit(solution)/shard_map/ppermute | solution.py:54
  147.1 3.3 %collective-permute-done.35 = f32[16,256]{1,0:T(8,128)S(1)} collective-permute-done((f32[16,256]{1,0:T(8,128)S(1)}, f32[16,256]{1,0:T(8,128)S(1)}, u32[]{:S(2)}, u32[]{:S(2)}) %collective-permute-start.35) | collective-permute-done | bytes 16416 | tf_op jit(solution)/shard_map/ppermute | solution.py:54
  150.4 0.6 add.209
  151.1 0.1 convert_reduce_fusion
  151.3 0.8 fusion.10
  (74 shorter events, 1.7 us)
Async XLA Ops:
  0.6 75.9 %copy-start = (bf16[128,256]{1,0:T(8,128)(2,1)S(1)}, bf16[128,256]{1,0:T(8,128)(2,1)}, u32[]{:S(2)}) copy-start(bf16[128,256]{1,0:T(8,128)(2,1)} %param.9) | copy-start | bytes 196612
  0.6 8.7 %copy-start.3 = (s32[1,1,384]{2,1,0:T(1,128)S(1)}, s32[1,1,384]{2,1,0:T(1,128)}, u32[]{:S(2)}) copy-start(s32[1,1,384]{2,1,0:T(1,128)} %param.12) | copy-start | bytes 4612
  0.7 8.7 %copy-start.4 = (s32[1,1,384]{2,1,0:T(1,128)S(1)}, s32[1,1,384]{2,1,0:T(1,128)}, u32[]{:S(2)}) copy-start(s32[1,1,384]{2,1,0:T(1,128)} %param.13) | copy-start | bytes 4612
  2.7 20.9 %all-to-all-start = ((bf16[8,512,128]{2,1,0:T(8,128)(2,1)}), bf16[8,512,128]{2,1,0:T(8,128)(2,1)S(1)}, u32[]{:S(2)}, u32[]{:S(2)}) async-start(bf16[8,512,128]{2,1,0:T(8,128)(2,1)} %broadcast_in_dim.28), calls=%async_computation | async-start | bytes 2097152 | tf_op jit(solution)/shard_map/all_to_all | solution.py:263
  28.2 2.7 %collective-permute-start = (bf16[32,128,128]{2,1,0:T(8,128)(2,1)S(1)}, bf16[32,128,128]{2,1,0:T(8,128)(2,1)S(1)}, u32[]{:S(2)}, u32[]{:S(2)}) collective-permute-start(bf16[32,128,128]{2,1,0:T(8,128)(2,1)S(1)} %get-tuple-element.22), channel_id=1, source_target_pairs={{0,1},{1,0},{2,3},{3,2},{4,5},{5,4},{6,7},{7,6},{8,9},{9,8},{10,11... | collective-permute-start | bytes 3145736 | tf_op jit(solution)/shard_map/ppermute | solution.py:54
  31.4 11.5 %collective-permute-start.1 = (bf16[32,128,128]{2,1,0:T(8,128)(2,1)S(1)}, bf16[32,128,128]{2,1,0:T(8,128)(2,1)S(1)}, u32[]{:S(2)}, u32[]{:S(2)}) collective-permute-start(bf16[32,128,128]{2,1,0:T(8,128)(2,1)S(1)} %get-tuple-element.23), channel_id=1, source_target_pairs={{0,1},{1,0},{2,3},{3,2},{4,5},{5,4},{6,7},{7,6},{8,9},{9,8},{10,11... | collective-permute-start | bytes 3145736 | tf_op jit(solution)/shard_map/ppermute | solution.py:54
  31.6 8.0 %collective-permute-start.7 = (bf16[512,128]{1,0:T(8,128)(2,1)S(1)}, bf16[512,128]{1,0:T(8,128)(2,1)S(1)}, u32[]{:S(2)}, u32[]{:S(2)}) collective-permute-start(bf16[512,128]{1,0:T(8,128)(2,1)S(1)} %get-tuple-element.45), channel_id=1, source_target_pairs={{0,4},{1,29},{2,6},{3,31},{4,8},{5,1},{6,10},{7,3},{8,12},{9,5},{1... | collective-permute-start | bytes 393224 | tf_op jit(solution)/shard_map/ppermute | solution.py:54
  39.7 6.5 %collective-permute-start.8 = (bf16[2,512,128]{2,1,0:T(8,128)(2,1)S(1)}, bf16[2,512,128]{2,1,0:T(8,128)(2,1)S(1)}, u32[]{:S(2)}, u32[]{:S(2)}) collective-permute-start(bf16[2,512,128]{2,1,0:T(8,128)(2,1)S(1)} %pad_maximum_fusion.4), channel_id=1, source_target_pairs={{0,4},{1,29},{2,6},{3,31},{4,8},{5,1},{6,10},{7,3},{8,12},{9,5},{1... | collective-permute-start | bytes 786440 | tf_op jit(solution)/shard_map/ppermute | solution.py:54
  43.4 6.1 %collective-permute-start.2 = (bf16[512,128]{1,0:T(8,128)(2,1)S(1)}, bf16[512,128]{1,0:T(8,128)(2,1)S(1)}, u32[]{:S(2)}, u32[]{:S(2)}) collective-permute-start(bf16[512,128]{1,0:T(8,128)(2,1)S(1)} %bitcast.73), channel_id=1, source_target_pairs={{0,4},{1,29},{2,6},{3,31},{4,8},{5,1},{6,10},{7,3},{8,12},{9,5},{1... | collective-permute-start | bytes 393224 | tf_op jit(solution)/shard_map/ppermute | solution.py:54
  46.3 6.5 %collective-permute-start.9 = (bf16[2,512,128]{2,1,0:T(8,128)(2,1)S(1)}, bf16[2,512,128]{2,1,0:T(8,128)(2,1)S(1)}, u32[]{:S(2)}, u32[]{:S(2)}) collective-permute-start(bf16[2,512,128]{2,1,0:T(8,128)(2,1)S(1)} %add_convert_fusion.3), channel_id=1, source_target_pairs={{0,4},{1,29},{2,6},{3,31},{4,8},{5,1},{6,10},{7,3},{8,12},{9,5},{1... | collective-permute-start | bytes 786440 | tf_op jit(solution)/shard_map/ppermute | solution.py:54
  49.6 26.8 %copy-start.1 = (bf16[1,512,128]{2,1,0:T(8,128)(2,1)S(1)}, bf16[1,512,128]{2,1,0:T(8,128)(2,1)}, u32[]{:S(2)}) copy-start(bf16[1,512,128]{2,1,0:T(8,128)(2,1)} %param.8) | copy-start | bytes 393220
  49.6 26.8 %copy-start.2 = (f32[1,512]{1,0:T(1,128)S(1)}, f32[1,512]{1,0:T(1,128)}, u32[]{:S(2)}) copy-start(f32[1,512]{1,0:T(1,128)} %param.11) | copy-start | bytes 6148
  49.6 6.5 %collective-permute-start.3 = (bf16[2,512,128]{2,1,0:T(8,128)(2,1)S(1)}, bf16[2,512,128]{2,1,0:T(8,128)(2,1)S(1)}, u32[]{:S(2)}, u32[]{:S(2)}) collective-permute-start(bf16[2,512,128]{2,1,0:T(8,128)(2,1)S(1)} %pad_maximum_fusion.3), channel_id=1, source_target_pairs={{0,4},{1,29},{2,6},{3,31},{4,8},{5,1},{6,10},{7,3},{8,12},{9,5},{1... | collective-permute-start | bytes 786440 | tf_op jit(solution)/shard_map/ppermute | solution.py:54
  52.9 23.6 %copy-start.5 = (bf16[1,512,256]{2,1,0:T(8,128)(2,1)S(1)}, bf16[1,512,256]{2,1,0:T(8,128)(2,1)}, u32[]{:S(2)}) copy-start(bf16[1,512,256]{2,1,0:T(8,128)(2,1)} %param.10) | copy-start | bytes 786436
  52.9 6.5 %collective-permute-start.10 = (bf16[2,512,128]{2,1,0:T(8,128)(2,1)S(1)}, bf16[2,512,128]{2,1,0:T(8,128)(2,1)S(1)}, u32[]{:S(2)}, u32[]{:S(2)}) collective-permute-start(bf16[2,512,128]{2,1,0:T(8,128)(2,1)S(1)} %add_convert_fusion.2), channel_id=1, source_target_pairs={{0,4},{1,29},{2,6},{3,31},{4,8},{5,1},{6,10},{7,3},{8,12},{9,5},{1... | collective-permute-start | bytes 786440 | tf_op jit(solution)/shard_map/ppermute | solution.py:54
  56.2 8.4 %collective-permute-start.4 = (bf16[2,512,128]{2,1,0:T(8,128)(2,1)S(1)}, bf16[2,512,128]{2,1,0:T(8,128)(2,1)S(1)}, u32[]{:S(2)}, u32[]{:S(2)}) collective-permute-start(bf16[2,512,128]{2,1,0:T(8,128)(2,1)S(1)} %fusion.1), channel_id=1, source_target_pairs={{0,4},{1,29},{2,6},{3,31},{4,8},{5,1},{6,10},{7,3},{8,12},{9,5},{1... | collective-permute-start | bytes 786440 | tf_op jit(solution)/shard_map/ppermute | solution.py:54
  59.4 6.2 %collective-permute-start.11 = (bf16[512,128]{1,0:T(8,128)(2,1)S(1)}, bf16[512,128]{1,0:T(8,128)(2,1)S(1)}, u32[]{:S(2)}, u32[]{:S(2)}) collective-permute-start(bf16[512,128]{1,0:T(8,128)(2,1)S(1)} %slice_bitcast_fusion), channel_id=1, source_target_pairs={{0,1},{1,0},{2,3},{3,2},{4,5},{5,4},{6,7},{7,6},{8,9},{9,8},{10,11... | collective-permute-start | bytes 393224 | tf_op jit(solution)/shard_map/ppermute | solution.py:54
  64.7 5.3 %collective-permute-start.5 = (bf16[2,512,128]{2,1,0:T(8,128)(2,1)S(1)}, bf16[2,512,128]{2,1,0:T(8,128)(2,1)S(1)}, u32[]{:S(2)}, u32[]{:S(2)}) collective-permute-start(bf16[2,512,128]{2,1,0:T(8,128)(2,1)S(1)} %fusion.2), channel_id=1, source_target_pairs={{0,4},{1,29},{2,6},{3,31},{4,8},{5,1},{6,10},{7,3},{8,12},{9,5},{1... | collective-permute-start | bytes 786440 | tf_op jit(solution)/shard_map/ppermute | solution.py:54
  65.7 9.7 %collective-permute-start.12 = (bf16[512,128]{1,0:T(8,128)(2,1)S(1)}, bf16[512,128]{1,0:T(8,128)(2,1)S(1)}, u32[]{:S(2)}, u32[]{:S(2)}) collective-permute-start(bf16[512,128]{1,0:T(8,128)(2,1)S(1)} %fusion.8), channel_id=1, source_target_pairs={{0,2},{1,3},{2,0},{3,1},{4,6},{5,7},{6,4},{7,5},{8,10},{9,11},{10,... | collective-permute-start | bytes 393224 | tf_op jit(solution)/shard_map/ppermute | solution.py:54
  70.0 6.3 %collective-permute-start.6 = (bf16[512,128]{1,0:T(8,128)(2,1)S(1)}, bf16[512,128]{1,0:T(8,128)(2,1)S(1)}, u32[]{:S(2)}, u32[]{:S(2)}) collective-permute-start(bf16[512,128]{1,0:T(8,128)(2,1)S(1)} %slice_bitcast_fusion.1), channel_id=1, source_target_pairs={{0,1},{1,0},{2,3},{3,2},{4,5},{5,4},{6,7},{7,6},{8,9},{9,8},{10,11... | collective-permute-start | bytes 393224 | tf_op jit(solution)/shard_map/ppermute | solution.py:54
  78.0 3.6 %collective-permute-start.16 = (f32[128,256]{1,0:T(8,128)S(1)}, f32[128,256]{1,0:T(8,128)S(1)}, u32[]{:S(2)}, u32[]{:S(2)}) collective-permute-start(f32[128,256]{1,0:T(8,128)S(1)} %convolution_multiply_fusion), channel_id=1, source_target_pairs={{0,1},{1,0},{2,3},{3,2},{4,5},{5,4},{6,7},{7,6},{8,9},{9,8},{10,11... | collective-permute-start | bytes 393224 | tf_op jit(solution)/shard_map/ppermute | solution.py:54
  78.5 4.0 %collective-permute-start.13 = (bf16[512,128]{1,0:T(8,128)(2,1)S(1)}, bf16[512,128]{1,0:T(8,128)(2,1)S(1)}, u32[]{:S(2)}, u32[]{:S(2)}) collective-permute-start(bf16[512,128]{1,0:T(8,128)(2,1)S(1)} %convolution_convert_fusion), channel_id=1, source_target_pairs={{0,1},{1,0},{2,3},{3,2},{4,5},{5,4},{6,7},{7,6},{8,9},{9,8},{10,11... | collective-permute-start | bytes 393224 | tf_op jit(solution)/shard_map/ppermute | solution.py:54
  78.6 6.2 %collective-permute-start.17 = (bf16[512,128]{1,0:T(8,128)(2,1)S(1)}, bf16[512,128]{1,0:T(8,128)(2,1)S(1)}, u32[]{:S(2)}, u32[]{:S(2)}) collective-permute-start(bf16[512,128]{1,0:T(8,128)(2,1)S(1)} %convolution_convert_fusion), channel_id=1, source_target_pairs={{0,2},{1,3},{2,0},{3,1},{4,6},{5,7},{6,4},{7,5},{8,10},{9,11},{10,... | collective-permute-start | bytes 393224 | tf_op jit(solution)/shard_map/ppermute | solution.py:54
  81.6 6.0 %collective-permute-start.18 = (f32[128,256]{1,0:T(8,128)S(1)}, f32[128,256]{1,0:T(8,128)S(1)}, u32[]{:S(2)}, u32[]{:S(2)}) collective-permute-start(f32[128,256]{1,0:T(8,128)S(1)} %add.194), channel_id=1, source_target_pairs={{0,2},{1,3},{2,0},{3,1},{4,6},{5,7},{6,4},{7,5},{8,10},{9,11},{10,... | collective-permute-start | bytes 393224 | tf_op jit(solution)/shard_map/ppermute | solution.py:54
  82.6 7.7 %collective-permute-start.14 = (bf16[1024,128]{1,0:T(8,128)(2,1)S(1)}, bf16[1024,128]{1,0:T(8,128)(2,1)S(1)}, u32[]{:S(2)}, u32[]{:S(2)}) collective-permute-start(bf16[1024,128]{1,0:T(8,128)(2,1)S(1)} %constant_dynamic-update-slice_fusion.refs_0_), channel_id=1, source_target_pairs={{0,4},{1,29},{2,6},{3,31},{4,8},{5,1},{6,10},{7,3},{8,12},{9,5},{1... | collective-permute-start | bytes 786440 | tf_op jit(solution)/shard_map/ppermute | solution.py:54
  87.7 3.0 %collective-permute-start.24 = (bf16[512,128]{1,0:T(8,128)(2,1)S(1)}, bf16[512,128]{1,0:T(8,128)(2,1)S(1)}, u32[]{:S(2)}, u32[]{:S(2)}) collective-permute-start(bf16[512,128]{1,0:T(8,128)(2,1)S(1)} %collective-permute-done.17), channel_id=1, source_target_pairs={{0,1},{1,0},{2,3},{3,2},{4,5},{5,4},{6,7},{7,6},{8,9},{9,8},{10,11... | collective-permute-start | bytes 393224 | tf_op jit(solution)/shard_map/ppermute | solution.py:54
  89.3 3.6 %collective-permute-start.19 = (f32[64,256]{1,0:T(8,128)S(1)}, f32[64,256]{1,0:T(8,128)S(1)}, u32[]{:S(2)}, u32[]{:S(2)}) collective-permute-start(f32[64,256]{1,0:T(8,128)S(1)} %constant_dynamic-slice_fusion.2), channel_id=1, source_target_pairs={{0,128},{1,129},{2,130},{3,131},{4,132},{5,133},{6,134},{7,135},{8... | collective-permute-start | bytes 196616 | tf_op jit(solution)/shard_map/ppermute | solution.py:54
  90.2 5.6 %collective-permute-start.15 = (bf16[1024,128]{1,0:T(8,128)(2,1)S(1)}, bf16[1024,128]{1,0:T(8,128)(2,1)S(1)}, u32[]{:S(2)}, u32[]{:S(2)}) collective-permute-start(bf16[1024,128]{1,0:T(8,128)(2,1)S(1)} %collective-permute-done.14.refs_1_), channel_id=1, source_target_pairs={{0,4},{1,29},{2,6},{3,31},{4,8},{5,1},{6,10},{7,3},{8,12},{9,5},{1... | collective-permute-start | bytes 786440 | tf_op jit(solution)/shard_map/ppermute | solution.py:54
  90.7 8.0 %collective-permute-start.25 = (bf16[1024,128]{1,0:T(8,128)(2,1)S(1)}, bf16[1024,128]{1,0:T(8,128)(2,1)S(1)}, u32[]{:S(2)}, u32[]{:S(2)}) collective-permute-start(bf16[1024,128]{1,0:T(8,128)(2,1)S(1)} %constant_dynamic-update-slice_fusion.2.refs_5_), channel_id=1, source_target_pairs={{0,4},{1,29},{2,6},{3,31},{4,8},{5,1},{6,10},{7,3},{8,12},{9,5},{1... | collective-permute-start | bytes 786440 | tf_op jit(solution)/shard_map/ppermute | solution.py:54
  95.8 5.6 %collective-permute-start.21 = (f32[32,256]{1,0:T(8,128)S(1)}, f32[32,256]{1,0:T(8,128)S(1)}, u32[]{:S(2)}, u32[]{:S(2)}) collective-permute-start(f32[32,256]{1,0:T(8,128)S(1)} %constant_dynamic-slice_fusion.1), channel_id=1, source_target_pairs={{0,64},{1,65},{2,66},{3,67},{4,68},{5,69},{6,70},{7,71},{8,72},{9,... | collective-permute-start | bytes 98312 | tf_op jit(solution)/shard_map/ppermute | solution.py:54
  96.9 5.2 %collective-permute-start.20 = (bf16[1024,128]{1,0:T(8,128)(2,1)S(1)}, bf16[1024,128]{1,0:T(8,128)(2,1)S(1)}, u32[]{:S(2)}, u32[]{:S(2)}) collective-permute-start(bf16[1024,128]{1,0:T(8,128)(2,1)S(1)} %collective-permute-done.15.refs_2_), channel_id=1, source_target_pairs={{0,4},{1,29},{2,6},{3,31},{4,8},{5,1},{6,10},{7,3},{8,12},{9,5},{1... | collective-permute-start | bytes 786440 | tf_op jit(solution)/shard_map/ppermute | solution.py:54
  98.6 6.6 %collective-permute-start.26 = (bf16[1024,128]{1,0:T(8,128)(2,1)S(1)}, bf16[1024,128]{1,0:T(8,128)(2,1)S(1)}, u32[]{:S(2)}, u32[]{:S(2)}) collective-permute-start(bf16[1024,128]{1,0:T(8,128)(2,1)S(1)} %collective-permute-done.25.refs_6_), channel_id=1, source_target_pairs={{0,4},{1,29},{2,6},{3,31},{4,8},{5,1},{6,10},{7,3},{8,12},{9,5},{1... | collective-permute-start | bytes 786440 | tf_op jit(solution)/shard_map/ppermute | solution.py:54
  99.9 24.3 %collective-permute-start.29 = (bf16[2048,128]{1,0:T(8,128)(2,1)S(1)}, bf16[2048,128]{1,0:T(8,128)(2,1)S(1)}, u32[]{:S(2)}, u32[]{:S(2)}) collective-permute-start(bf16[2048,128]{1,0:T(8,128)(2,1)S(1)} %pad_maximum_fusion), channel_id=1, source_target_pairs={{0,1},{1,0},{2,3},{3,2},{4,5},{5,4},{6,7},{7,6},{8,9},{9,8},{10,11... | collective-permute-start | bytes 1572872 | tf_op jit(solution)/shard_map/ppermute | solution.py:54
  105.2 6.0 %collective-permute-start.27 = (bf16[1024,128]{1,0:T(8,128)(2,1)S(1)}, bf16[1024,128]{1,0:T(8,128)(2,1)S(1)}, u32[]{:S(2)}, u32[]{:S(2)}) collective-permute-start(bf16[1024,128]{1,0:T(8,128)(2,1)S(1)} %collective-permute-done.26.refs_7_), channel_id=1, source_target_pairs={{0,4},{1,29},{2,6},{3,31},{4,8},{5,1},{6,10},{7,3},{8,12},{9,5},{1... | collective-permute-start | bytes 786440 | tf_op jit(solution)/shard_map/ppermute | solution.py:54
  107.4 7.1 %collective-permute-start.23 = (f32[16,256]{1,0:T(8,128)S(1)}, f32[16,256]{1,0:T(8,128)S(1)}, u32[]{:S(2)}, u32[]{:S(2)}) collective-permute-start(f32[16,256]{1,0:T(8,128)S(1)} %constant_dynamic-slice_fusion), channel_id=1, source_target_pairs={{0,32},{1,33},{2,34},{3,35},{4,36},{5,37},{6,38},{7,39},{8,40},{9,... | collective-permute-start | bytes 49160 | tf_op jit(solution)/shard_map/ppermute | solution.py:54
  108.0 10.1 %collective-permute-start.22 = (bf16[512,128]{1,0:T(8,128)(2,1)S(1)}, bf16[512,128]{1,0:T(8,128)(2,1)S(1)}, u32[]{:S(2)}, u32[]{:S(2)}) collective-permute-start(bf16[512,128]{1,0:T(8,128)(2,1)S(1)} %slice.87), channel_id=1, source_target_pairs={{0,4},{1,29},{2,6},{3,31},{4,8},{5,1},{6,10},{7,3},{8,12},{9,5},{1... | collective-permute-start | bytes 393224 | tf_op jit(solution)/shard_map/ppermute | solution.py:54
  108.1 16.1 %collective-permute-start.30 = (bf16[2048,128]{1,0:T(8,128)(2,1)S(1)}, bf16[2048,128]{1,0:T(8,128)(2,1)S(1)}, u32[]{:S(2)}, u32[]{:S(2)}) collective-permute-start(bf16[2048,128]{1,0:T(8,128)(2,1)S(1)} %pad_maximum_fusion.1), channel_id=1, source_target_pairs={{0,1},{1,0},{2,3},{3,2},{4,5},{5,4},{6,7},{7,6},{8,9},{9,8},{10,11... | collective-permute-start | bytes 1572872 | tf_op jit(solution)/shard_map/ppermute | solution.py:54
  111.2 6.9 %collective-permute-start.28 = (bf16[512,128]{1,0:T(8,128)(2,1)S(1)}, bf16[512,128]{1,0:T(8,128)(2,1)S(1)}, u32[]{:S(2)}, u32[]{:S(2)}) collective-permute-start(bf16[512,128]{1,0:T(8,128)(2,1)S(1)} %slice.99), channel_id=1, source_target_pairs={{0,4},{1,29},{2,6},{3,31},{4,8},{5,1},{6,10},{7,3},{8,12},{9,5},{1... | collective-permute-start | bytes 393224 | tf_op jit(solution)/shard_map/ppermute | solution.py:54
  114.5 10.9 %collective-permute-start.31 = (bf16[2048,128]{1,0:T(8,128)(2,1)S(1)}, bf16[2048,128]{1,0:T(8,128)(2,1)S(1)}, u32[]{:S(2)}, u32[]{:S(2)}) collective-permute-start(bf16[2048,128]{1,0:T(8,128)(2,1)S(1)} %pad_maximum_fusion.2), channel_id=1, source_target_pairs={{0,1},{1,0},{2,3},{3,2},{4,5},{5,4},{6,7},{7,6},{8,9},{9,8},{10,11... | collective-permute-start | bytes 1572872 | tf_op jit(solution)/shard_map/ppermute | solution.py:54
  118.1 7.3 %collective-permute-start.32 = (bf16[1024,128]{1,0:T(8,128)(2,1)S(1)}, bf16[1024,128]{1,0:T(8,128)(2,1)S(1)}, u32[]{:S(2)}, u32[]{:S(2)}) collective-permute-start(bf16[1024,128]{1,0:T(8,128)(2,1)S(1)} %pad_maximum_fusion.5), channel_id=1, source_target_pairs={{0,1},{1,0},{2,3},{3,2},{4,5},{5,4},{6,7},{7,6},{8,9},{9,8},{10,11... | collective-permute-start | bytes 786440 | tf_op jit(solution)/shard_map/ppermute | solution.py:54
  132.0 19.2 %all-to-all-start.1 = ((bf16[8,512,128]{2,1,0:T(8,128)(2,1)}), bf16[8,512,128]{2,1,0:T(8,128)(2,1)S(1)}, u32[]{:S(2)}, u32[]{:S(2)}) async-start(bf16[8,512,128]{2,1,0:T(8,128)(2,1)} %bitcast.22), calls=%async_computation.1 | async-start | bytes 2097152 | tf_op jit(solution)/shard_map/all_to_all | solution.py:315
  136.2 2.6 %collective-permute-start.33 = (f32[16,256]{1,0:T(8,128)S(1)}, f32[16,256]{1,0:T(8,128)S(1)}, u32[]{:S(2)}, u32[]{:S(2)}) collective-permute-start(f32[16,256]{1,0:T(8,128)S(1)} %dynamic-slice_add_fusion.2), channel_id=1, source_target_pairs={{0,4},{1,5},{2,6},{3,7},{4,0},{5,1},{6,2},{7,3},{8,12},{9,13},{10,... | collective-permute-start | bytes 49160 | tf_op jit(solution)/shard_map/ppermute | solution.py:54
  138.8 5.1 %collective-permute-start.34 = (f32[16,256]{1,0:T(8,128)S(1)}, f32[16,256]{1,0:T(8,128)S(1)}, u32[]{:S(2)}, u32[]{:S(2)}) collective-permute-start(f32[16,256]{1,0:T(8,128)S(1)} %add.207), channel_id=1, source_target_pairs={{0,8},{1,9},{2,10},{3,11},{4,12},{5,13},{6,14},{7,15},{8,0},{9,1},... | collective-permute-start | bytes 49160 | tf_op jit(solution)/shard_map/ppermute | solution.py:54
  143.9 6.5 %collective-permute-start.35 = (f32[16,256]{1,0:T(8,128)S(1)}, f32[16,256]{1,0:T(8,128)S(1)}, u32[]{:S(2)}, u32[]{:S(2)}) collective-permute-start(f32[16,256]{1,0:T(8,128)S(1)} %add.208), channel_id=1, source_target_pairs={{0,16},{1,17},{2,18},{3,19},{4,20},{5,21},{6,22},{7,23},{8,24},{9,... | collective-permute-start | bytes 49160 | tf_op jit(solution)/shard_map/ppermute | solution.py:54

commit v3 on v2

--- a/solution.py
+++ b/solution.py
@@ -81,6 +81,27 @@
         return carry
 
     return lambda: lax.fori_loop(0, groups, one_group, 0)
+
+
+def spread_kernel(one_ref, all_ref, sems):
+    copies = [
+        pltpu.make_async_copy(one_ref, all_ref.at[i], sems.at[i]) for i in range(all_ref.shape[0])
+    ]
+    for one in copies:
+        one.start()
+    for one in copies:
+        one.wait()
+
+
+def spread(value, count):
+    return pl.pallas_call(
+        spread_kernel,
+        out_shape=jax.ShapeDtypeStruct((count,) + value.shape, value.dtype),
+        in_specs=[pl.BlockSpec(memory_space=pltpu.VMEM)],
+        out_specs=pl.BlockSpec(memory_space=pl.ANY),
+        scratch_shapes=[pltpu.SemaphoreType.DMA((count,))],
+        name="spread",
+    )(value)
 
 
 def forward_kernel(
@@ -260,7 +281,7 @@
     land_fwd = forward_slot(jnp.where(c == 0, ahead, behind), rel_c, rel_x) * 4 + rows % 4
     land_bwd = backward_slot(jnp.where(c == 0, behind, ahead), rel_c, rel_x) * 4 + rows % 4
 
-    panel = lax.all_to_all(jnp.broadcast_to(features, (8, 512, BS)), REP, 0, 0)
+    panel = lax.all_to_all(spread(features[0], 8), REP, 0, 0)
     keep, away_far, away_near = forward_products(
         land_fwd, cols, count, panel.reshape(32, BS, BS), tiles
     )
@@ -293,27 +314,27 @@
     near = jnp.concatenate([row_grad, send(row_grad, CORE_SWAP)], 0)
     x_own = send(row_grad, X_SWAP)
     weight_sum = weight_sum + send(weight_sum, CORE_SWAP)
-    x_weight = send(weight_sum, X_SWAP)
-    near_ring = [near]
-    near_ring.append(send(near, Z_RING))
-    x_own, x_weight = tied(x_own, x_weight)
-    weight_sum = weight_sum + x_weight
+    near_ring = [near, send(near, Z_RING)]
+    weight_sum = halve(weight_sum, sides[0], REP_SWAPS[0])
+    near_ring[-1], weight_sum = tied(near_ring[-1], weight_sum)
     far = jnp.concatenate([x_own, send(x_own, CORE_SWAP)], 0)
-    far_ring = [far]
-    far_ring.append(send(far, Z_RING))
+    far_ring = [far, send(far, Z_RING)]
     cores = []
     for hop in (2, 3, 4):
         size = 1024 if hop < 4 else 512
         cores.append(send(jnp.concatenate([near_ring[-1], far_ring[-1]], 0), CORE_SWAP))
         near_ring.append(send(near_ring[-1][:size], Z_RING))
-        weight_sum = halve(weight_sum, sides[hop - 2], REP_SWAPS[hop - 2])
+        if hop < 4:
+            weight_sum = halve(weight_sum, sides[hop - 1], REP_SWAPS[hop - 1])
+        else:
+            weight_sum = weight_sum + send(weight_sum, X_SWAP)
         near_ring[-1], weight_sum = tied(near_ring[-1], weight_sum)
         far_ring.append(send(far_ring[-1][:size], Z_RING))
     cores.append(send(jnp.concatenate([near_ring[-1], far_ring[-1]], 0), CORE_SWAP))
     columns = backward_products(land_bwd, cols, count, near_ring, far_ring, cores, tiles)
     columns, weight_sum = tied(columns, weight_sum)
     parts = lax.all_to_all(columns.reshape(8, 512, BS), REP, 0, 0)
-    for k in (1, 2, 4):
+    for k in (1, 3, 7):
         weight_sum = weight_sum + send(weight_sum, z_flip(k))
     feature_grad = (
         jnp.sum(parts.astype(jnp.float32), 0) + scale * row_grad.astype(jnp.float32)

time: 154 us -> 147 us (0.955); the launches traced: 152 us -> 147 us
  starting transfers between devices: 83.3 us -> 76.5 us
  waiting for transfers between devices: 48.8 us -> 51.4 us
  local copies, waits for them, and re-layouts: 2.31 us -> 0.24 us
    ppermute x36, starting transfers between devices: 73.1 us -> 66.7 us  [send(): return lax.ppermute(value, AXES, pairs)]
    all_to_all x1, waiting for transfers between devices: 0.13 us -> 2.97 us  [on_device(): parts = lax.all_to_all(columns.reshape(8, 512, BS), REP, 0, 0)]
    broadcast_in_dim x1 -> x0, local copies, waits for them, and re-layouts: 2.06 us -> none  [on_device(): panel = lax.all_to_all(jnp.broadcast_to(features, (8, 512, BS)), REP, 0, 0)]
    pallas_call x0 -> x1, Pallas kernels: none -> 2 us  [spread(): pl.pallas_call(spread_kernel, out_shape=jax.ShapeDtypeStruct((count,) + v...]
  transfers between devices with their start and end apart: 38 -> 38, of which waited for: 21 -> 22; matrix products, arithmetic and copies ran while one was open for 1% -> 1% of each run, Pallas kernels for 0% -> 0%
where the time goes in v3:
time: 147 us
  starting transfers between devices  76.5 us (52%)
  waiting for transfers between devices  51.4 us (35%)
  Pallas kernels  12.2 us (8%)
  other arithmetic  3.2 us (2%)
  between operations  1.63 us (1%)
  matrix products  1.53 us (1%)
    ppermute x36, starting transfers between devices, send(): return lax.ppermute(value, AXES, pairs)  66.7 us
    ppermute x36, waiting for transfers between devices, send(): return lax.ppermute(value, AXES, pairs)  34.3 us
    all_to_all x1, waiting for transfers between devices, on_device(): panel = lax.all_to_all(spread(features[0], 8), REP, 0, 0)  14.1 us
    pallas_call x1, Pallas kernels, backward_products(): pl.pallas_call(backward_kernel, out_shape=jax.ShapeDtypeStruct((32, BS, B...  6.06 us
    all_to_all x1, starting transfers between devices, on_device(): panel = lax.all_to_all(spread(features[0], 8), REP, 0, 0)  5.96 us
    pallas_call x1, Pallas kernels, forward_products(): pl.pallas_call(forward_kernel, out_shape=(kept, away, away), in_specs=[sm...  4.17 us
    all_to_all x1, starting transfers between devices, on_device(): parts = lax.all_to_all(columns.reshape(8, 512, BS), REP, 0, 0)  3.86 us
    all_to_all x1, waiting for transfers between devices, on_device(): parts = lax.all_to_all(columns.reshape(8, 512, BS), REP, 0, 0)  2.97 us
  transfers between devices with their start and end apart: 38, of which 22 were waited for; matrix products, arithmetic and copies ran while one was open for 1% of the time, Pallas kernels for 0%

profile of v3, /device:TPU:1, one launch (start us, length us, event | category | flops | bytes accessed | tf_op | source)
XLA Modules:
  0.0 146.7 jit_solution(13531192829106365908)
XLA Ops:
  0.7 2.0 %spread.1 = bf16[8,512,128]{2,1,0:T(8,128)(2,1)} custom-call(bf16[512,128]{1,0:T(8,128)(2,1)} %bitcast.71), custom_call_target="tpu_custom_call" | custom-call | tf_op jit(solution)/shard_map/spread/pallas_call | solution.py:97
  2.7 6.0 %all-to-all-start = ((bf16[8,512,128]{2,1,0:T(8,128)(2,1)}), bf16[8,512,128]{2,1,0:T(8,128)(2,1)S(1)}, u32[]{:S(2)}, u32[]{:S(2)}) async-start(bf16[8,512,128]{2,1,0:T(8,128)(2,1)} %spread.1), calls=%async_computation | async-start | bytes 2097152 | tf_op jit(solution)/shard_map/all_to_all | solution.py:284
  9.4 14.1 %all-to-all-done = bf16[8,512,128]{2,1,0:T(8,128)(2,1)S(1)} async-done(((bf16[8,512,128]{2,1,0:T(8,128)(2,1)}), bf16[8,512,128]{2,1,0:T(8,128)(2,1)S(1)}, u32[]{:S(2)}, u32[]{:S(2)}) %all-to-all-start) | async-done | bytes 1048608 | tf_op jit(solution)/shard_map/all_to_all | solution.py:284
  23.5 4.2 %forward_products.1 = (bf16[64,128,128]{2,1,0:T(8,128)(2,1)S(1)}, bf16[32,128,128]{2,1,0:T(8,128)(2,1)S(1)}, bf16[32,128,128]{2,1,0:T(8,128)(2,1)S(1)}) custom-call(s32[384]{0:T(512)S(1)} %fusion.26.land_ref, s32[384]{0:T(512)S(1)} %reduce.1.cols_ref, s32[1]{0:T(128)} %bitcast.59.count_ref, bf16[32,128,128]{2,1,0:T(8,128)(2,1)S(1)} %bitcast.61, ...), custom_call_target="tpu_custom_call" | custom-call | flops 1610612736 | bytes 18874368 | tf_op jit(solution)/shard_map/forward_products/pallas_call | solution.py:128
  27.7 0.9 collective-permute-start
  28.6 2.3 %collective-permute-done = bf16[32,128,128]{2,1,0:T(8,128)(2,1)S(1)} collective-permute-done((bf16[32,128,128]{2,1,0:T(8,128)(2,1)S(1)}, bf16[32,128,128]{2,1,0:T(8,128)(2,1)S(1)}, u32[]{:S(2)}, u32[]{:S(2)}) %collective-permute-start) | collective-permute-done | bytes 1048608 | tf_op jit(solution)/shard_map/ppermute | solution.py:54
  30.9 0.4 add_convert_fusion.1
  31.3 0.5 collective-permute-start.1
  31.8 5.7 %collective-permute-start.7 = (bf16[512,128]{1,0:T(8,128)(2,1)S(1)}, bf16[512,128]{1,0:T(8,128)(2,1)S(1)}, u32[]{:S(2)}, u32[]{:S(2)}) collective-permute-start(bf16[512,128]{1,0:T(8,128)(2,1)S(1)} %get-tuple-element.45), channel_id=1, source_target_pairs={{0,4},{1,29},{2,6},{3,31},{4,8},{5,1},{6,10},{7,3},{8,12},{9,5},{1... | collective-permute-start | bytes 393224 | tf_op jit(solution)/shard_map/ppermute | solution.py:54
  37.4 1.9 %collective-permute-done.7 = bf16[512,128]{1,0:T(8,128)(2,1)S(1)} collective-permute-done((bf16[512,128]{1,0:T(8,128)(2,1)S(1)}, bf16[512,128]{1,0:T(8,128)(2,1)S(1)}, u32[]{:S(2)}, u32[]{:S(2)}) %collective-permute-start.7) | collective-permute-done | bytes 131104 | tf_op jit(solution)/shard_map/ppermute | solution.py:54
  39.5 3.2 %collective-permute-start.8 = (bf16[2,512,128]{2,1,0:T(8,128)(2,1)S(1)}, bf16[2,512,128]{2,1,0:T(8,128)(2,1)S(1)}, u32[]{:S(2)}, u32[]{:S(2)}) collective-permute-start(bf16[2,512,128]{2,1,0:T(8,128)(2,1)S(1)} %pad_maximum_fusion.4), channel_id=1, source_target_pairs={{0,4},{1,29},{2,6},{3,31},{4,8},{5,1},{6,10},{7,3},{8,12},{9,5},{1... | collective-permute-start | bytes 786440 | tf_op jit(solution)/shard_map/ppermute | solution.py:54
  42.6 0.4 add_convert_fusion
  43.2 2.8 %collective-permute-done.8 = bf16[2,512,128]{2,1,0:T(8,128)(2,1)S(1)} collective-permute-done((bf16[2,512,128]{2,1,0:T(8,128)(2,1)S(1)}, bf16[2,512,128]{2,1,0:T(8,128)(2,1)S(1)}, u32[]{:S(2)}, u32[]{:S(2)}) %collective-permute-start.8) | collective-permute-done | bytes 262176 | tf_op jit(solution)/shard_map/ppermute | solution.py:54
  46.0 3.2 %collective-permute-start.9 = (bf16[2,512,128]{2,1,0:T(8,128)(2,1)S(1)}, bf16[2,512,128]{2,1,0:T(8,128)(2,1)S(1)}, u32[]{:S(2)}, u32[]{:S(2)}) collective-permute-start(bf16[2,512,128]{2,1,0:T(8,128)(2,1)S(1)} %add_convert_fusion.3), channel_id=1, source_target_pairs={{0,4},{1,29},{2,6},{3,31},{4,8},{5,1},{6,10},{7,3},{8,12},{9,5},{1... | collective-permute-start | bytes 786440 | tf_op jit(solution)/shard_map/ppermute | solution.py:54
  49.3 1.3 collective-permute-start.3
  50.7 1.9 %collective-permute-done.9 = bf16[2,512,128]{2,1,0:T(8,128)(2,1)S(1)} collective-permute-done((bf16[2,512,128]{2,1,0:T(8,128)(2,1)S(1)}, bf16[2,512,128]{2,1,0:T(8,128)(2,1)S(1)}, u32[]{:S(2)}, u32[]{:S(2)}) %collective-permute-start.9) | collective-permute-done | bytes 262176 | tf_op jit(solution)/shard_map/ppermute | solution.py:54
  52.6 3.2 %collective-permute-start.10 = (bf16[2,512,128]{2,1,0:T(8,128)(2,1)S(1)}, bf16[2,512,128]{2,1,0:T(8,128)(2,1)S(1)}, u32[]{:S(2)}, u32[]{:S(2)}) collective-permute-start(bf16[2,512,128]{2,1,0:T(8,128)(2,1)S(1)} %add_convert_fusion.2), channel_id=1, source_target_pairs={{0,4},{1,29},{2,6},{3,31},{4,8},{5,1},{6,10},{7,3},{8,12},{9,5},{1... | collective-permute-start | bytes 786440 | tf_op jit(solution)/shard_map/ppermute | solution.py:54
  55.9 2.7 %collective-permute-start.4 = (bf16[2,512,128]{2,1,0:T(8,128)(2,1)S(1)}, bf16[2,512,128]{2,1,0:T(8,128)(2,1)S(1)}, u32[]{:S(2)}, u32[]{:S(2)}) collective-permute-start(bf16[2,512,128]{2,1,0:T(8,128)(2,1)S(1)} %fusion.1), channel_id=1, source_target_pairs={{0,4},{1,29},{2,6},{3,31},{4,8},{5,1},{6,10},{7,3},{8,12},{9,5},{1... | collective-permute-start | bytes 786440 | tf_op jit(solution)/shard_map/ppermute | solution.py:54
  58.6 0.5 collective-permute-done.10
  59.1 5.0 %collective-permute-start.11 = (bf16[512,128]{1,0:T(8,128)(2,1)S(1)}, bf16[512,128]{1,0:T(8,128)(2,1)S(1)}, u32[]{:S(2)}, u32[]{:S(2)}) collective-permute-start(bf16[512,128]{1,0:T(8,128)(2,1)S(1)} %slice_bitcast_fusion), channel_id=1, source_target_pairs={{0,1},{1,0},{2,3},{3,2},{4,5},{5,4},{6,7},{7,6},{8,9},{9,8},{10,11... | collective-permute-start | bytes 393224 | tf_op jit(solution)/shard_map/ppermute | solution.py:54
  64.2 1.0 collective-permute-start.5
  65.3 3.5 %collective-permute-start.12 = (bf16[512,128]{1,0:T(8,128)(2,1)S(1)}, bf16[512,128]{1,0:T(8,128)(2,1)S(1)}, u32[]{:S(2)}, u32[]{:S(2)}) collective-permute-start(bf16[512,128]{1,0:T(8,128)(2,1)S(1)} %fusion.8), channel_id=1, source_target_pairs={{0,2},{1,3},{2,0},{3,1},{4,6},{5,7},{6,4},{7,5},{8,10},{9,11},{10,... | collective-permute-start | bytes 393224 | tf_op jit(solution)/shard_map/ppermute | solution.py:54
  68.8 0.7 collective-permute-done.5
  69.5 5.3 %collective-permute-start.6 = (bf16[512,128]{1,0:T(8,128)(2,1)S(1)}, bf16[512,128]{1,0:T(8,128)(2,1)S(1)}, u32[]{:S(2)}, u32[]{:S(2)}) collective-permute-start(bf16[512,128]{1,0:T(8,128)(2,1)S(1)} %slice_bitcast_fusion.1), channel_id=1, source_target_pairs={{0,1},{1,0},{2,3},{3,2},{4,5},{5,4},{6,7},{7,6},{8,9},{9,8},{10,11... | collective-permute-start | bytes 393224 | tf_op jit(solution)/shard_map/ppermute | solution.py:54
  74.9 1.0 collective-permute-done.6
  76.0 1.1 fusion
  77.1 0.2 convolution_multiply_fusion
  77.3 0.2 convolution_convert_fusion
  77.6 0.4 collective-permute-start.15
  78.0 3.4 %collective-permute-start.23 = (bf16[512,128]{1,0:T(8,128)(2,1)S(1)}, bf16[512,128]{1,0:T(8,128)(2,1)S(1)}, u32[]{:S(2)}, u32[]{:S(2)}) collective-permute-start(bf16[512,128]{1,0:T(8,128)(2,1)S(1)} %convolution_convert_fusion), channel_id=1, source_target_pairs={{0,2},{1,3},{2,0},{3,1},{4,6},{5,7},{6,4},{7,5},{8,10},{9,11},{10,... | collective-permute-start | bytes 393224 | tf_op jit(solution)/shard_map/ppermute | solution.py:54
  81.4 0.4 collective-permute-start.13
  82.1 0.7 collective-permute-done.13
  82.9 0.4 collective-permute-start.14
  83.3 1.8 %collective-permute-done.23 = bf16[512,128]{1,0:T(8,128)(2,1)S(1)} collective-permute-done((bf16[512,128]{1,0:T(8,128)(2,1)S(1)}, bf16[512,128]{1,0:T(8,128)(2,1)S(1)}, u32[]{:S(2)}, u32[]{:S(2)}) %collective-permute-start.23) | collective-permute-done | bytes 131104 | tf_op jit(solution)/shard_map/ppermute | solution.py:54
  85.1 0.7 collective-permute-start.24
  85.9 0.5 collective-permute-done.16
  86.4 0.4 collective-permute-done.24
  86.9 0.5 collective-permute-start.25
  87.4 1.1 collective-permute-done.14.refs_1_
  88.5 1.3 collective-permute-start.17
  89.7 1.0 collective-permute-start.18
  90.8 3.2 %collective-permute-done.18 = f32[32,256]{1,0:T(8,128)S(1)} collective-permute-done((f32[32,256]{1,0:T(8,128)S(1)}, f32[32,256]{1,0:T(8,128)S(1)}, u32[]{:S(2)}, u32[]{:S(2)}) %collective-permute-start.18) | collective-permute-done | bytes 32800 | tf_op jit(solution)/shard_map/ppermute | solution.py:54
  94.1 1.2 collective-permute-done.17.refs_2_
  95.3 3.3 %collective-permute-start.29 = (bf16[2048,128]{1,0:T(8,128)(2,1)S(1)}, bf16[2048,128]{1,0:T(8,128)(2,1)S(1)}, u32[]{:S(2)}, u32[]{:S(2)}) collective-permute-start(bf16[2048,128]{1,0:T(8,128)(2,1)S(1)} %pad_maximum_fusion), channel_id=1, source_target_pairs={{0,1},{1,0},{2,3},{3,2},{4,5},{5,4},{6,7},{7,6},{8,9},{9,8},{10,11... | collective-permute-start | bytes 1572872 | tf_op jit(solution)/shard_map/ppermute | solution.py:54
  98.6 1.0 collective-permute-start.19
  99.6 1.6 %collective-permute-start.27 = (bf16[1024,128]{1,0:T(8,128)(2,1)S(1)}, bf16[1024,128]{1,0:T(8,128)(2,1)S(1)}, u32[]{:S(2)}, u32[]{:S(2)}) collective-permute-start(bf16[1024,128]{1,0:T(8,128)(2,1)S(1)} %collective-permute-done.26.refs_7_), channel_id=1, source_target_pairs={{0,4},{1,29},{2,6},{3,31},{4,8},{5,1},{6,10},{7,3},{8,12},{9,5},{1... | collective-permute-start | bytes 786440 | tf_op jit(solution)/shard_map/ppermute | solution.py:54
  101.3 2.8 %collective-permute-start.30 = (bf16[2048,128]{1,0:T(8,128)(2,1)S(1)}, bf16[2048,128]{1,0:T(8,128)(2,1)S(1)}, u32[]{:S(2)}, u32[]{:S(2)}) collective-permute-start(bf16[2048,128]{1,0:T(8,128)(2,1)S(1)} %pad_maximum_fusion.1), channel_id=1, source_target_pairs={{0,1},{1,0},{2,3},{3,2},{4,5},{5,4},{6,7},{7,6},{8,9},{9,8},{10,11... | collective-permute-start | bytes 1572872 | tf_op jit(solution)/shard_map/ppermute | solution.py:54
  104.1 2.7 %collective-permute-start.22 = (f32[16,256]{1,0:T(8,128)S(1)}, f32[16,256]{1,0:T(8,128)S(1)}, u32[]{:S(2)}, u32[]{:S(2)}) collective-permute-start(f32[16,256]{1,0:T(8,128)S(1)} %dynamic-slice_add_fusion.2), channel_id=1, source_target_pairs={{0,2},{1,3},{2,0},{3,1},{4,6},{5,7},{6,4},{7,5},{8,10},{9,11},{10,... | collective-permute-start | bytes 49160 | tf_op jit(solution)/shard_map/ppermute | solution.py:54
  106.9 4.8 %collective-permute-start.31 = (bf16[2048,128]{1,0:T(8,128)(2,1)S(1)}, bf16[2048,128]{1,0:T(8,128)(2,1)S(1)}, u32[]{:S(2)}, u32[]{:S(2)}) collective-permute-start(bf16[2048,128]{1,0:T(8,128)(2,1)S(1)} %pad_maximum_fusion.2), channel_id=1, source_target_pairs={{0,1},{1,0},{2,3},{3,2},{4,5},{5,4},{6,7},{7,6},{8,9},{9,8},{10,11... | collective-permute-start | bytes 1572872 | tf_op jit(solution)/shard_map/ppermute | solution.py:54
  111.7 0.8 collective-permute-start.21
  112.7 3.2 %collective-permute-done.21.refs_4_ = bf16[512,128]{1,0:T(8,128)(2,1)S(1)} collective-permute-done((bf16[512,128]{1,0:T(8,128)(2,1)S(1)}, bf16[512,128]{1,0:T(8,128)(2,1)S(1)}, u32[]{:S(2)}, u32[]{:S(2)}) %collective-permute-start.21) | collective-permute-done | bytes 131104 | tf_op jit(solution)/shard_map/ppermute | solution.py:54
  115.8 1.7 %collective-permute-done.28.refs_9_ = bf16[512,128]{1,0:T(8,128)(2,1)S(1)} collective-permute-done((bf16[512,128]{1,0:T(8,128)(2,1)S(1)}, bf16[512,128]{1,0:T(8,128)(2,1)S(1)}, u32[]{:S(2)}, u32[]{:S(2)}) %collective-permute-start.28) | collective-permute-done | bytes 131104 | tf_op jit(solution)/shard_map/ppermute | solution.py:54
  117.6 2.2 %collective-permute-start.32 = (bf16[1024,128]{1,0:T(8,128)(2,1)S(1)}, bf16[1024,128]{1,0:T(8,128)(2,1)S(1)}, u32[]{:S(2)}, u32[]{:S(2)}) collective-permute-start(bf16[1024,128]{1,0:T(8,128)(2,1)S(1)} %pad_maximum_fusion.5), channel_id=1, source_target_pairs={{0,1},{1,0},{2,3},{3,2},{4,5},{5,4},{6,7},{7,6},{8,9},{9,8},{10,11... | collective-permute-start | bytes 786440 | tf_op jit(solution)/shard_map/ppermute | solution.py:54
  119.7 1.2 collective-permute-done.32.refs_13_
  120.9 6.1 %backward_products.1 = bf16[32,128,128]{2,1,0:T(8,128)(2,1)} custom-call(s32[384]{0:T(512)S(1)} %get-tuple-element.37.land_ref, s32[384]{0:T(512)S(1)} %reduce.1.cols_ref, s32[1]{0:T(128)} %bitcast.60.count_ref, bf16[1024,128]{1,0:T(8,128)(2,1)S(1)} %constant_dynamic-update-slice_fusion.refs_0_, bf16[1024,128]{1,0:T(8,128)(2,1)S(1)} %collective-permute-done.14.refs_1_, ...), custom_call_target="tpu_custom_call" | custom-call | flops 1610612736 | bytes 18874368 | tf_op jit(solution)/shard_map/backward_products/pallas_call | solution.py:195
  127.0 3.9 %all-to-all-start.1 = ((bf16[8,512,128]{2,1,0:T(8,128)(2,1)}), bf16[8,512,128]{2,1,0:T(8,128)(2,1)S(1)}, u32[]{:S(2)}, u32[]{:S(2)}) async-start(bf16[8,512,128]{2,1,0:T(8,128)(2,1)} %bitcast.22), calls=%async_computation.1 | async-start | bytes 2097152 | tf_op jit(solution)/shard_map/all_to_all | solution.py:336
  130.8 2.6 %collective-permute-done.33 = f32[16,256]{1,0:T(8,128)S(1)} collective-permute-done((f32[16,256]{1,0:T(8,128)S(1)}, f32[16,256]{1,0:T(8,128)S(1)}, u32[]{:S(2)}, u32[]{:S(2)}) %collective-permute-start.33) | collective-permute-done | bytes 16416 | tf_op jit(solution)/shard_map/ppermute | solution.py:54
  133.4 1.9 %collective-permute-start.34 = (f32[16,256]{1,0:T(8,128)S(1)}, f32[16,256]{1,0:T(8,128)S(1)}, u32[]{:S(2)}, u32[]{:S(2)}) collective-permute-start(f32[16,256]{1,0:T(8,128)S(1)} %add.207), channel_id=1, source_target_pairs={{0,12},{1,13},{2,14},{3,15},{4,8},{5,9},{6,10},{7,11},{8,4},{9,5},... | collective-permute-start | bytes 49160 | tf_op jit(solution)/shard_map/ppermute | solution.py:54
  135.3 2.8 %collective-permute-done.34 = f32[16,256]{1,0:T(8,128)S(1)} collective-permute-done((f32[16,256]{1,0:T(8,128)S(1)}, f32[16,256]{1,0:T(8,128)S(1)}, u32[]{:S(2)}, u32[]{:S(2)}) %collective-permute-start.34) | collective-permute-done | bytes 16416 | tf_op jit(solution)/shard_map/ppermute | solution.py:54
  138.1 1.4 collective-permute-start.35
  139.5 2.7 %collective-permute-done.35 = f32[16,256]{1,0:T(8,128)S(1)} collective-permute-done((f32[16,256]{1,0:T(8,128)S(1)}, f32[16,256]{1,0:T(8,128)S(1)}, u32[]{:S(2)}, u32[]{:S(2)}) %collective-permute-start.35) | collective-permute-done | bytes 16416 | tf_op jit(solution)/shard_map/ppermute | solution.py:54
  142.2 0.6 add.209
  142.8 3.0 %all-to-all-done.1 = bf16[8,512,128]{2,1,0:T(8,128)(2,1)S(1)} async-done(((bf16[8,512,128]{2,1,0:T(8,128)(2,1)}), bf16[8,512,128]{2,1,0:T(8,128)(2,1)S(1)}, u32[]{:S(2)}, u32[]{:S(2)}) %all-to-all-start.1) | async-done | bytes 1048608 | tf_op jit(solution)/shard_map/all_to_all | solution.py:336
  145.9 0.8 fusion.10
  (74 shorter events, 1.8 us)
Async XLA Ops:
  0.6 75.4 %copy-start = (bf16[128,256]{1,0:T(8,128)(2,1)S(1)}, bf16[128,256]{1,0:T(8,128)(2,1)}, u32[]{:S(2)}) copy-start(bf16[128,256]{1,0:T(8,128)(2,1)} %param.9) | copy-start | bytes 196612
  0.6 8.6 %copy-start.3 = (s32[1,1,384]{2,1,0:T(1,128)S(1)}, s32[1,1,384]{2,1,0:T(1,128)}, u32[]{:S(2)}) copy-start(s32[1,1,384]{2,1,0:T(1,128)} %param.12) | copy-start | bytes 4612
  0.7 8.7 %copy-start.4 = (s32[1,1,384]{2,1,0:T(1,128)S(1)}, s32[1,1,384]{2,1,0:T(1,128)}, u32[]{:S(2)}) copy-start(s32[1,1,384]{2,1,0:T(1,128)} %param.13) | copy-start | bytes 4612
  2.7 20.9 %all-to-all-start = ((bf16[8,512,128]{2,1,0:T(8,128)(2,1)}), bf16[8,512,128]{2,1,0:T(8,128)(2,1)S(1)}, u32[]{:S(2)}, u32[]{:S(2)}) async-start(bf16[8,512,128]{2,1,0:T(8,128)(2,1)} %spread.1), calls=%async_computation | async-start | bytes 2097152 | tf_op jit(solution)/shard_map/all_to_all | solution.py:284
  27.7 3.2 %collective-permute-start = (bf16[32,128,128]{2,1,0:T(8,128)(2,1)S(1)}, bf16[32,128,128]{2,1,0:T(8,128)(2,1)S(1)}, u32[]{:S(2)}, u32[]{:S(2)}) collective-permute-start(bf16[32,128,128]{2,1,0:T(8,128)(2,1)S(1)} %get-tuple-element.22), channel_id=1, source_target_pairs={{0,1},{1,0},{2,3},{3,2},{4,5},{5,4},{6,7},{7,6},{8,9},{9,8},{10,11... | collective-permute-start | bytes 3145736 | tf_op jit(solution)/shard_map/ppermute | solution.py:54
  31.3 11.3 %collective-permute-start.1 = (bf16[32,128,128]{2,1,0:T(8,128)(2,1)S(1)}, bf16[32,128,128]{2,1,0:T(8,128)(2,1)S(1)}, u32[]{:S(2)}, u32[]{:S(2)}) collective-permute-start(bf16[32,128,128]{2,1,0:T(8,128)(2,1)S(1)} %get-tuple-element.23), channel_id=1, source_target_pairs={{0,1},{1,0},{2,3},{3,2},{4,5},{5,4},{6,7},{7,6},{8,9},{9,8},{10,11... | collective-permute-start | bytes 3145736 | tf_op jit(solution)/shard_map/ppermute | solution.py:54
  31.8 7.6 %collective-permute-start.7 = (bf16[512,128]{1,0:T(8,128)(2,1)S(1)}, bf16[512,128]{1,0:T(8,128)(2,1)S(1)}, u32[]{:S(2)}, u32[]{:S(2)}) collective-permute-start(bf16[512,128]{1,0:T(8,128)(2,1)S(1)} %get-tuple-element.45), channel_id=1, source_target_pairs={{0,4},{1,29},{2,6},{3,31},{4,8},{5,1},{6,10},{7,3},{8,12},{9,5},{1... | collective-permute-start | bytes 393224 | tf_op jit(solution)/shard_map/ppermute | solution.py:54
  39.5 6.5 %collective-permute-start.8 = (bf16[2,512,128]{2,1,0:T(8,128)(2,1)S(1)}, bf16[2,512,128]{2,1,0:T(8,128)(2,1)S(1)}, u32[]{:S(2)}, u32[]{:S(2)}) collective-permute-start(bf16[2,512,128]{2,1,0:T(8,128)(2,1)S(1)} %pad_maximum_fusion.4), channel_id=1, source_target_pairs={{0,4},{1,29},{2,6},{3,31},{4,8},{5,1},{6,10},{7,3},{8,12},{9,5},{1... | collective-permute-start | bytes 786440 | tf_op jit(solution)/shard_map/ppermute | solution.py:54
  43.1 6.2 %collective-permute-start.2 = (bf16[512,128]{1,0:T(8,128)(2,1)S(1)}, bf16[512,128]{1,0:T(8,128)(2,1)S(1)}, u32[]{:S(2)}, u32[]{:S(2)}) collective-permute-start(bf16[512,128]{1,0:T(8,128)(2,1)S(1)} %bitcast.73), channel_id=1, source_target_pairs={{0,4},{1,29},{2,6},{3,31},{4,8},{5,1},{6,10},{7,3},{8,12},{9,5},{1... | collective-permute-start | bytes 393224 | tf_op jit(solution)/shard_map/ppermute | solution.py:54
  46.0 6.5 %collective-permute-start.9 = (bf16[2,512,128]{2,1,0:T(8,128)(2,1)S(1)}, bf16[2,512,128]{2,1,0:T(8,128)(2,1)S(1)}, u32[]{:S(2)}, u32[]{:S(2)}) collective-permute-start(bf16[2,512,128]{2,1,0:T(8,128)(2,1)S(1)} %add_convert_fusion.3), channel_id=1, source_target_pairs={{0,4},{1,29},{2,6},{3,31},{4,8},{5,1},{6,10},{7,3},{8,12},{9,5},{1... | collective-permute-start | bytes 786440 | tf_op jit(solution)/shard_map/ppermute | solution.py:54
  49.3 26.5 %copy-start.1 = (bf16[1,512,128]{2,1,0:T(8,128)(2,1)S(1)}, bf16[1,512,128]{2,1,0:T(8,128)(2,1)}, u32[]{:S(2)}) copy-start(bf16[1,512,128]{2,1,0:T(8,128)(2,1)} %param.8) | copy-start | bytes 393220
  49.3 26.5 %copy-start.2 = (f32[1,512]{1,0:T(1,128)S(1)}, f32[1,512]{1,0:T(1,128)}, u32[]{:S(2)}) copy-start(f32[1,512]{1,0:T(1,128)} %param.11) | copy-start | bytes 6148
  49.3 6.5 %collective-permute-start.3 = (bf16[2,512,128]{2,1,0:T(8,128)(2,1)S(1)}, bf16[2,512,128]{2,1,0:T(8,128)(2,1)S(1)}, u32[]{:S(2)}, u32[]{:S(2)}) collective-permute-start(bf16[2,512,128]{2,1,0:T(8,128)(2,1)S(1)} %pad_maximum_fusion.3), channel_id=1, source_target_pairs={{0,4},{1,29},{2,6},{3,31},{4,8},{5,1},{6,10},{7,3},{8,12},{9,5},{1... | collective-permute-start | bytes 786440 | tf_op jit(solution)/shard_map/ppermute | solution.py:54
  52.6 23.4 %copy-start.5 = (bf16[1,512,256]{2,1,0:T(8,128)(2,1)S(1)}, bf16[1,512,256]{2,1,0:T(8,128)(2,1)}, u32[]{:S(2)}) copy-start(bf16[1,512,256]{2,1,0:T(8,128)(2,1)} %param.10) | copy-start | bytes 786436
  52.6 6.5 %collective-permute-start.10 = (bf16[2,512,128]{2,1,0:T(8,128)(2,1)S(1)}, bf16[2,512,128]{2,1,0:T(8,128)(2,1)S(1)}, u32[]{:S(2)}, u32[]{:S(2)}) collective-permute-start(bf16[2,512,128]{2,1,0:T(8,128)(2,1)S(1)} %add_convert_fusion.2), channel_id=1, source_target_pairs={{0,4},{1,29},{2,6},{3,31},{4,8},{5,1},{6,10},{7,3},{8,12},{9,5},{1... | collective-permute-start | bytes 786440 | tf_op jit(solution)/shard_map/ppermute | solution.py:54
  55.9 8.2 %collective-permute-start.4 = (bf16[2,512,128]{2,1,0:T(8,128)(2,1)S(1)}, bf16[2,512,128]{2,1,0:T(8,128)(2,1)S(1)}, u32[]{:S(2)}, u32[]{:S(2)}) collective-permute-start(bf16[2,512,128]{2,1,0:T(8,128)(2,1)S(1)} %fusion.1), channel_id=1, source_target_pairs={{0,4},{1,29},{2,6},{3,31},{4,8},{5,1},{6,10},{7,3},{8,12},{9,5},{1... | collective-permute-start | bytes 786440 | tf_op jit(solution)/shard_map/ppermute | solution.py:54
  59.1 6.1 %collective-permute-start.11 = (bf16[512,128]{1,0:T(8,128)(2,1)S(1)}, bf16[512,128]{1,0:T(8,128)(2,1)S(1)}, u32[]{:S(2)}, u32[]{:S(2)}) collective-permute-start(bf16[512,128]{1,0:T(8,128)(2,1)S(1)} %slice_bitcast_fusion), channel_id=1, source_target_pairs={{0,1},{1,0},{2,3},{3,2},{4,5},{5,4},{6,7},{7,6},{8,9},{9,8},{10,11... | collective-permute-start | bytes 393224 | tf_op jit(solution)/shard_map/ppermute | solution.py:54
  64.2 5.3 %collective-permute-start.5 = (bf16[2,512,128]{2,1,0:T(8,128)(2,1)S(1)}, bf16[2,512,128]{2,1,0:T(8,128)(2,1)S(1)}, u32[]{:S(2)}, u32[]{:S(2)}) collective-permute-start(bf16[2,512,128]{2,1,0:T(8,128)(2,1)S(1)} %fusion.2), channel_id=1, source_target_pairs={{0,4},{1,29},{2,6},{3,31},{4,8},{5,1},{6,10},{7,3},{8,12},{9,5},{1... | collective-permute-start | bytes 786440 | tf_op jit(solution)/shard_map/ppermute | solution.py:54
  65.3 9.6 %collective-permute-start.12 = (bf16[512,128]{1,0:T(8,128)(2,1)S(1)}, bf16[512,128]{1,0:T(8,128)(2,1)S(1)}, u32[]{:S(2)}, u32[]{:S(2)}) collective-permute-start(bf16[512,128]{1,0:T(8,128)(2,1)S(1)} %fusion.8), channel_id=1, source_target_pairs={{0,2},{1,3},{2,0},{3,1},{4,6},{5,7},{6,4},{7,5},{8,10},{9,11},{10,... | collective-permute-start | bytes 393224 | tf_op jit(solution)/shard_map/ppermute | solution.py:54
  69.5 6.3 %collective-permute-start.6 = (bf16[512,128]{1,0:T(8,128)(2,1)S(1)}, bf16[512,128]{1,0:T(8,128)(2,1)S(1)}, u32[]{:S(2)}, u32[]{:S(2)}) collective-permute-start(bf16[512,128]{1,0:T(8,128)(2,1)S(1)} %slice_bitcast_fusion.1), channel_id=1, source_target_pairs={{0,1},{1,0},{2,3},{3,2},{4,5},{5,4},{6,7},{7,6},{8,9},{9,8},{10,11... | collective-permute-start | bytes 393224 | tf_op jit(solution)/shard_map/ppermute | solution.py:54
  77.6 4.3 %collective-permute-start.15 = (f32[128,256]{1,0:T(8,128)S(1)}, f32[128,256]{1,0:T(8,128)S(1)}, u32[]{:S(2)}, u32[]{:S(2)}) collective-permute-start(f32[128,256]{1,0:T(8,128)S(1)} %convolution_multiply_fusion), channel_id=1, source_target_pairs={{0,1},{1,0},{2,3},{3,2},{4,5},{5,4},{6,7},{7,6},{8,9},{9,8},{10,11... | collective-permute-start | bytes 393224 | tf_op jit(solution)/shard_map/ppermute | solution.py:54
  78.0 7.1 %collective-permute-start.23 = (bf16[512,128]{1,0:T(8,128)(2,1)S(1)}, bf16[512,128]{1,0:T(8,128)(2,1)S(1)}, u32[]{:S(2)}, u32[]{:S(2)}) collective-permute-start(bf16[512,128]{1,0:T(8,128)(2,1)S(1)} %convolution_convert_fusion), channel_id=1, source_target_pairs={{0,2},{1,3},{2,0},{3,1},{4,6},{5,7},{6,4},{7,5},{8,10},{9,11},{10,... | collective-permute-start | bytes 393224 | tf_op jit(solution)/shard_map/ppermute | solution.py:54
  81.4 1.4 collective-permute-start.13
  81.9 4.5 %collective-permute-start.16 = (f32[64,256]{1,0:T(8,128)S(1)}, f32[64,256]{1,0:T(8,128)S(1)}, u32[]{:S(2)}, u32[]{:S(2)}) collective-permute-start(f32[64,256]{1,0:T(8,128)S(1)} %constant_dynamic-slice_fusion.2), channel_id=1, source_target_pairs={{0,128},{1,129},{2,130},{3,131},{4,132},{5,133},{6,134},{7,135},{8... | collective-permute-start | bytes 196616 | tf_op jit(solution)/shard_map/ppermute | solution.py:54
  82.9 5.6 %collective-permute-start.14 = (bf16[1024,128]{1,0:T(8,128)(2,1)S(1)}, bf16[1024,128]{1,0:T(8,128)(2,1)S(1)}, u32[]{:S(2)}, u32[]{:S(2)}) collective-permute-start(bf16[1024,128]{1,0:T(8,128)(2,1)S(1)} %constant_dynamic-update-slice_fusion.refs_0_), channel_id=1, source_target_pairs={{0,4},{1,29},{2,6},{3,31},{4,8},{5,1},{6,10},{7,3},{8,12},{9,5},{1... | collective-permute-start | bytes 786440 | tf_op jit(solution)/shard_map/ppermute | solution.py:54
  85.1 1.7 %collective-permute-start.24 = (bf16[512,128]{1,0:T(8,128)(2,1)S(1)}, bf16[512,128]{1,0:T(8,128)(2,1)S(1)}, u32[]{:S(2)}, u32[]{:S(2)}) collective-permute-start(bf16[512,128]{1,0:T(8,128)(2,1)S(1)} %collective-permute-done.23), channel_id=1, source_target_pairs={{0,1},{1,0},{2,3},{3,2},{4,5},{5,4},{6,7},{7,6},{8,9},{9,8},{10,11... | collective-permute-start | bytes 393224 | tf_op jit(solution)/shard_map/ppermute | solution.py:54
  86.9 7.1 %collective-permute-start.25 = (bf16[1024,128]{1,0:T(8,128)(2,1)S(1)}, bf16[1024,128]{1,0:T(8,128)(2,1)S(1)}, u32[]{:S(2)}, u32[]{:S(2)}) collective-permute-start(bf16[1024,128]{1,0:T(8,128)(2,1)S(1)} %constant_dynamic-update-slice_fusion.2.refs_5_), channel_id=1, source_target_pairs={{0,4},{1,29},{2,6},{3,31},{4,8},{5,1},{6,10},{7,3},{8,12},{9,5},{1... | collective-permute-start | bytes 786440 | tf_op jit(solution)/shard_map/ppermute | solution.py:54
  88.5 6.8 %collective-permute-start.17 = (bf16[1024,128]{1,0:T(8,128)(2,1)S(1)}, bf16[1024,128]{1,0:T(8,128)(2,1)S(1)}, u32[]{:S(2)}, u32[]{:S(2)}) collective-permute-start(bf16[1024,128]{1,0:T(8,128)(2,1)S(1)} %collective-permute-done.14.refs_1_), channel_id=1, source_target_pairs={{0,4},{1,29},{2,6},{3,31},{4,8},{5,1},{6,10},{7,3},{8,12},{9,5},{1... | collective-permute-start | bytes 786440 | tf_op jit(solution)/shard_map/ppermute | solution.py:54
  89.7 4.3 %collective-permute-start.18 = (f32[32,256]{1,0:T(8,128)S(1)}, f32[32,256]{1,0:T(8,128)S(1)}, u32[]{:S(2)}, u32[]{:S(2)}) collective-permute-start(f32[32,256]{1,0:T(8,128)S(1)} %constant_dynamic-slice_fusion.1), channel_id=1, source_target_pairs={{0,64},{1,65},{2,66},{3,67},{4,68},{5,69},{6,70},{7,71},{8,72},{9,... | collective-permute-start | bytes 98312 | tf_op jit(solution)/shard_map/ppermute | solution.py:54
  94.0 5.6 %collective-permute-start.26 = (bf16[1024,128]{1,0:T(8,128)(2,1)S(1)}, bf16[1024,128]{1,0:T(8,128)(2,1)S(1)}, u32[]{:S(2)}, u32[]{:S(2)}) collective-permute-start(bf16[1024,128]{1,0:T(8,128)(2,1)S(1)} %collective-permute-done.25.refs_6_), channel_id=1, source_target_pairs={{0,4},{1,29},{2,6},{3,31},{4,8},{5,1},{6,10},{7,3},{8,12},{9,5},{1... | collective-permute-start | bytes 786440 | tf_op jit(solution)/shard_map/ppermute | solution.py:54
  95.3 6.0 %collective-permute-start.20 = (f32[16,256]{1,0:T(8,128)S(1)}, f32[16,256]{1,0:T(8,128)S(1)}, u32[]{:S(2)}, u32[]{:S(2)}) collective-permute-start(f32[16,256]{1,0:T(8,128)S(1)} %constant_dynamic-slice_fusion), channel_id=1, source_target_pairs={{0,32},{1,33},{2,34},{3,35},{4,36},{5,37},{6,38},{7,39},{8,40},{9,... | collective-permute-start | bytes 49160 | tf_op jit(solution)/shard_map/ppermute | solution.py:54
  95.3 24.4 %collective-permute-start.29 = (bf16[2048,128]{1,0:T(8,128)(2,1)S(1)}, bf16[2048,128]{1,0:T(8,128)(2,1)S(1)}, u32[]{:S(2)}, u32[]{:S(2)}) collective-permute-start(bf16[2048,128]{1,0:T(8,128)(2,1)S(1)} %pad_maximum_fusion), channel_id=1, source_target_pairs={{0,1},{1,0},{2,3},{3,2},{4,5},{5,4},{6,7},{7,6},{8,9},{9,8},{10,11... | collective-permute-start | bytes 1572872 | tf_op jit(solution)/shard_map/ppermute | solution.py:54
  98.6 5.5 %collective-permute-start.19 = (bf16[1024,128]{1,0:T(8,128)(2,1)S(1)}, bf16[1024,128]{1,0:T(8,128)(2,1)S(1)}, u32[]{:S(2)}, u32[]{:S(2)}) collective-permute-start(bf16[1024,128]{1,0:T(8,128)(2,1)S(1)} %collective-permute-done.17.refs_2_), channel_id=1, source_target_pairs={{0,4},{1,29},{2,6},{3,31},{4,8},{5,1},{6,10},{7,3},{8,12},{9,5},{1... | collective-permute-start | bytes 786440 | tf_op jit(solution)/shard_map/ppermute | solution.py:54
  99.6 7.3 %collective-permute-start.27 = (bf16[1024,128]{1,0:T(8,128)(2,1)S(1)}, bf16[1024,128]{1,0:T(8,128)(2,1)S(1)}, u32[]{:S(2)}, u32[]{:S(2)}) collective-permute-start(bf16[1024,128]{1,0:T(8,128)(2,1)S(1)} %collective-permute-done.26.refs_7_), channel_id=1, source_target_pairs={{0,4},{1,29},{2,6},{3,31},{4,8},{5,1},{6,10},{7,3},{8,12},{9,5},{1... | collective-permute-start | bytes 786440 | tf_op jit(solution)/shard_map/ppermute | solution.py:54
  101.3 18.4 %collective-permute-start.30 = (bf16[2048,128]{1,0:T(8,128)(2,1)S(1)}, bf16[2048,128]{1,0:T(8,128)(2,1)S(1)}, u32[]{:S(2)}, u32[]{:S(2)}) collective-permute-start(bf16[2048,128]{1,0:T(8,128)(2,1)S(1)} %pad_maximum_fusion.1), channel_id=1, source_target_pairs={{0,1},{1,0},{2,3},{3,2},{4,5},{5,4},{6,7},{7,6},{8,9},{9,8},{10,11... | collective-permute-start | bytes 1572872 | tf_op jit(solution)/shard_map/ppermute | solution.py:54
  104.1 8.4 %collective-permute-start.22 = (f32[16,256]{1,0:T(8,128)S(1)}, f32[16,256]{1,0:T(8,128)S(1)}, u32[]{:S(2)}, u32[]{:S(2)}) collective-permute-start(f32[16,256]{1,0:T(8,128)S(1)} %dynamic-slice_add_fusion.2), channel_id=1, source_target_pairs={{0,2},{1,3},{2,0},{3,1},{4,6},{5,7},{6,4},{7,5},{8,10},{9,11},{10,... | collective-permute-start | bytes 49160 | tf_op jit(solution)/shard_map/ppermute | solution.py:54
  106.9 14.0 %collective-permute-start.31 = (bf16[2048,128]{1,0:T(8,128)(2,1)S(1)}, bf16[2048,128]{1,0:T(8,128)(2,1)S(1)}, u32[]{:S(2)}, u32[]{:S(2)}) collective-permute-start(bf16[2048,128]{1,0:T(8,128)(2,1)S(1)} %pad_maximum_fusion.2), channel_id=1, source_target_pairs={{0,1},{1,0},{2,3},{3,2},{4,5},{5,4},{6,7},{7,6},{8,9},{9,8},{10,11... | collective-permute-start | bytes 1572872 | tf_op jit(solution)/shard_map/ppermute | solution.py:54
  111.7 4.1 %collective-permute-start.21 = (bf16[512,128]{1,0:T(8,128)(2,1)S(1)}, bf16[512,128]{1,0:T(8,128)(2,1)S(1)}, u32[]{:S(2)}, u32[]{:S(2)}) collective-permute-start(bf16[512,128]{1,0:T(8,128)(2,1)S(1)} %slice.87), channel_id=1, source_target_pairs={{0,4},{1,29},{2,6},{3,31},{4,8},{5,1},{6,10},{7,3},{8,12},{9,5},{1... | collective-permute-start | bytes 393224 | tf_op jit(solution)/shard_map/ppermute | solution.py:54
  112.6 5.0 %collective-permute-start.28 = (bf16[512,128]{1,0:T(8,128)(2,1)S(1)}, bf16[512,128]{1,0:T(8,128)(2,1)S(1)}, u32[]{:S(2)}, u32[]{:S(2)}) collective-permute-start(bf16[512,128]{1,0:T(8,128)(2,1)S(1)} %slice.99), channel_id=1, source_target_pairs={{0,4},{1,29},{2,6},{3,31},{4,8},{5,1},{6,10},{7,3},{8,12},{9,5},{1... | collective-permute-start | bytes 393224 | tf_op jit(solution)/shard_map/ppermute | solution.py:54
  117.6 3.3 %collective-permute-start.32 = (bf16[1024,128]{1,0:T(8,128)(2,1)S(1)}, bf16[1024,128]{1,0:T(8,128)(2,1)S(1)}, u32[]{:S(2)}, u32[]{:S(2)}) collective-permute-start(bf16[1024,128]{1,0:T(8,128)(2,1)S(1)} %pad_maximum_fusion.5), channel_id=1, source_target_pairs={{0,1},{1,0},{2,3},{3,2},{4,5},{5,4},{6,7},{7,6},{8,9},{9,8},{10,11... | collective-permute-start | bytes 786440 | tf_op jit(solution)/shard_map/ppermute | solution.py:54
  127.0 18.8 %all-to-all-start.1 = ((bf16[8,512,128]{2,1,0:T(8,128)(2,1)}), bf16[8,512,128]{2,1,0:T(8,128)(2,1)S(1)}, u32[]{:S(2)}, u32[]{:S(2)}) async-start(bf16[8,512,128]{2,1,0:T(8,128)(2,1)} %bitcast.22), calls=%async_computation.1 | async-start | bytes 2097152 | tf_op jit(solution)/shard_map/all_to_all | solution.py:336
  130.8 2.6 %collective-permute-start.33 = (f32[16,256]{1,0:T(8,128)S(1)}, f32[16,256]{1,0:T(8,128)S(1)}, u32[]{:S(2)}, u32[]{:S(2)}) collective-permute-start(f32[16,256]{1,0:T(8,128)S(1)} %add.205), channel_id=1, source_target_pairs={{0,4},{1,5},{2,6},{3,7},{4,0},{5,1},{6,2},{7,3},{8,12},{9,13},{10,... | collective-permute-start | bytes 49160 | tf_op jit(solution)/shard_map/ppermute | solution.py:54
  133.4 4.7 %collective-permute-start.34 = (f32[16,256]{1,0:T(8,128)S(1)}, f32[16,256]{1,0:T(8,128)S(1)}, u32[]{:S(2)}, u32[]{:S(2)}) collective-permute-start(f32[16,256]{1,0:T(8,128)S(1)} %add.207), channel_id=1, source_target_pairs={{0,12},{1,13},{2,14},{3,15},{4,8},{5,9},{6,10},{7,11},{8,4},{9,5},... | collective-permute-start | bytes 49160 | tf_op jit(solution)/shard_map/ppermute | solution.py:54
  138.1 4.1 %collective-permute-start.35 = (f32[16,256]{1,0:T(8,128)S(1)}, f32[16,256]{1,0:T(8,128)S(1)}, u32[]{:S(2)}, u32[]{:S(2)}) collective-permute-start(f32[16,256]{1,0:T(8,128)S(1)} %add.208), channel_id=1, source_target_pairs={{0,28},{1,29},{2,30},{3,31},{4,24},{5,25},{6,26},{7,27},{8,20},{9,... | collective-permute-start | bytes 49160 | tf_op jit(solution)/shard_map/ppermute | solution.py:54

commit v4 on v3

--- a/solution.py
+++ b/solution.py
@@ -14,8 +14,8 @@
 BLK = ("z", "xh", "c")
 NZ = 8
 BS = 128
-GROUP = 32
-BUFFERS = 4
+GROUP = 64
+BUFFERS = 3
 
 
 def _pairs(move):
@@ -143,72 +143,42 @@
     )(land, cols, count, panel, tiles)
 
 
-def piece_plan(refs):
-    near, far, cores = refs[:5], refs[5:10], refs[10:]
-    plan = []
-    at = 0
-    for side, ring in enumerate((near, far)):
-        for ref in ring:
-            plan.append((ref, 0, at, ref.shape[0]))
-            at += ref.shape[0]
-        for ref in cores:
-            size = ref.shape[0] // 2
-            plan.append((ref, side * size, at, size))
-            at += size
-    return plan
-
-
-def backward_kernel(land_ref, cols_ref, count_ref, *refs):
-    piece_refs = refs[:-6]
-    tiles_ref, out_ref, acc, buf, grads, sems = refs[-6:]
-
+def backward_kernel(
+    land_ref, cols_ref, count_ref, grads_ref, tiles_ref, out_ref, acc, buf, sems
+):
     def use(s, slot, j):
         acc[cols_ref[s]] += lax.dot_general(
             buf[slot, j],
-            grads[pl.ds(pl.multiple_of(land_ref[s] * BS, BS), BS)],
+            grads_ref[land_ref[s]],
             (((0,), (0,)), ((), ())),
             preferred_element_type=jnp.float32,
         )
 
-    copies = []
-    for i, (ref, start, at, size) in enumerate(piece_plan(piece_refs)):
-        copies.append(
-            pltpu.make_async_copy(
-                ref.at[pl.ds(start, size)], grads.at[pl.ds(at, size)], sems.at[BUFFERS + i]
-            )
-        )
-    for one in copies:
-        one.start()
     run = stream_tiles(count_ref[0], tiles_ref, buf, sems, use)
     acc[...] = jnp.zeros_like(acc)
-    for one in copies:
-        one.wait()
     run()
     out_ref[...] = acc[...].astype(jnp.bfloat16)
 
 
-def backward_products(land, cols, count, near, far, cores, tiles):
-    pieces = near + far + cores
+def backward_products(land, cols, count, grads, tiles):
     smem = pl.BlockSpec(memory_space=pltpu.SMEM)
     vmem = pl.BlockSpec(memory_space=pltpu.VMEM)
-    hbm = pl.BlockSpec(memory_space=pl.ANY)
     return pl.pallas_call(
         backward_kernel,
         out_shape=jax.ShapeDtypeStruct((32, BS, BS), jnp.bfloat16),
-        in_specs=[smem, smem, smem] + [hbm] * (len(pieces) + 1),
+        in_specs=[smem, smem, smem, vmem, pl.BlockSpec(memory_space=pl.ANY)],
         out_specs=vmem,
         scratch_shapes=[
             pltpu.VMEM((32, BS, BS), jnp.float32),
             pltpu.VMEM((BUFFERS, GROUP, BS, BS), jnp.bfloat16),
-            pltpu.VMEM((128 * BS, BS), jnp.bfloat16),
-            pltpu.SemaphoreType.DMA((BUFFERS + 18,)),
+            pltpu.SemaphoreType.DMA((BUFFERS,)),
         ],
-        compiler_params=pltpu.CompilerParams(vmem_limit_bytes=40 << 20),
+        compiler_params=pltpu.CompilerParams(vmem_limit_bytes=44 << 20),
         cost_estimate=pl.CostEstimate(
             flops=384 * 2 * BS**3, bytes_accessed=18 << 20, transcendentals=0
         ),
         name="backward_products",
-    )(land, cols, count, *pieces, tiles)
+    )(land, cols, count, grads, tiles)
 
 
 def halve(value, side, swap):
@@ -331,7 +301,12 @@
         near_ring[-1], weight_sum = tied(near_ring[-1], weight_sum)
         far_ring.append(send(far_ring[-1][:size], Z_RING))
     cores.append(send(jnp.concatenate([near_ring[-1], far_ring[-1]], 0), CORE_SWAP))
-    columns = backward_products(land_bwd, cols, count, near_ring, far_ring, cores, tiles)
+    near_ring, far_ring, cores = tied(near_ring, far_ring, cores)
+    halves = [jnp.split(core, 2) for core in cores]
+    grads = near_ring + [half[0] for half in halves]
+    grads += far_ring + [half[1] for half in halves]
+    grads = jnp.concatenate(grads, 0).reshape(128, BS, BS)
+    columns = backward_products(land_bwd, cols, count, grads, tiles)
     columns, weight_sum = tied(columns, weight_sum)
     parts = lax.all_to_all(columns.reshape(8, 512, BS), REP, 0, 0)
     for k in (1, 3, 7):

time: 147 us -> 147 us (level)
  transfers between devices with their start and end apart: 38 -> 38, of which waited for: 22 -> 21; matrix products, arithmetic and copies ran while one was open for 1% -> 2% of each run, Pallas kernels for 0% -> 0%
where the time goes in v4:
time: 147 us; the launch traced here: 146 us
  starting transfers between devices  75.5 us (51%)
  waiting for transfers between devices  50.9 us (35%)
  Pallas kernels  11.4 us (8%)
  other arithmetic  4.57 us (3%)
  between operations  1.75 us (1%)
  matrix products  1.53 us (1%)
    ppermute x36, starting transfers between devices, send(): return lax.ppermute(value, AXES, pairs)  65.5 us
    ppermute x36, waiting for transfers between devices, send(): return lax.ppermute(value, AXES, pairs)  35.1 us
    all_to_all x1, waiting for transfers between devices, on_device(): panel = lax.all_to_all(spread(features[0], 8), REP, 0, 0)  12.8 us
    all_to_all x1, starting transfers between devices, on_device(): panel = lax.all_to_all(spread(features[0], 8), REP, 0, 0)  5.96 us
    pallas_call x1, Pallas kernels, backward_products(): pl.pallas_call(backward_kernel, out_shape=jax.ShapeDtypeStruct((32, BS, B...  5.09 us
    pallas_call x1, Pallas kernels, forward_products(): pl.pallas_call(forward_kernel, out_shape=(kept, away, away), in_specs=[sm...  4.31 us
    all_to_all x1, starting transfers between devices, on_device(): parts = lax.all_to_all(columns.reshape(8, 512, BS), REP, 0, 0)  4.02 us
    all_to_all x1, waiting for transfers between devices, on_device(): parts = lax.all_to_all(columns.reshape(8, 512, BS), REP, 0, 0)  2.95 us
  transfers between devices with their start and end apart: 38, of which 21 were waited for; matrix products, arithmetic and copies ran while one was open for 2% of the time, Pallas kernels for 0%

profile of v4, /device:TPU:1, one launch (start us, length us, event | category | flops | bytes accessed | tf_op | source)
XLA Modules:
  0.0 146.4 jit_solution(4904606101512344836)
XLA Ops:
  0.6 2.0 %spread.1 = bf16[8,512,128]{2,1,0:T(8,128)(2,1)} custom-call(bf16[512,128]{1,0:T(8,128)(2,1)} %bitcast.73), custom_call_target="tpu_custom_call" | custom-call | tf_op jit(solution)/shard_map/spread/pallas_call | solution.py:97
  2.6 6.0 %all-to-all-start = ((bf16[8,512,128]{2,1,0:T(8,128)(2,1)}), bf16[8,512,128]{2,1,0:T(8,128)(2,1)S(1)}, u32[]{:S(2)}, u32[]{:S(2)}) async-start(bf16[8,512,128]{2,1,0:T(8,128)(2,1)} %spread.1), calls=%async_computation | async-start | bytes 2097152 | tf_op jit(solution)/shard_map/all_to_all | solution.py:254
  9.3 0.7 reduce
  10.0 0.7 reduce.1.cols_ref
  10.7 12.8 %all-to-all-done = bf16[8,512,128]{2,1,0:T(8,128)(2,1)S(1)} async-done(((bf16[8,512,128]{2,1,0:T(8,128)(2,1)}), bf16[8,512,128]{2,1,0:T(8,128)(2,1)S(1)}, u32[]{:S(2)}, u32[]{:S(2)}) %all-to-all-start) | async-done | bytes 1048608 | tf_op jit(solution)/shard_map/all_to_all | solution.py:254
  23.5 4.3 %forward_products.1 = (bf16[64,128,128]{2,1,0:T(8,128)(2,1)S(1)}, bf16[32,128,128]{2,1,0:T(8,128)(2,1)S(1)}, bf16[32,128,128]{2,1,0:T(8,128)(2,1)S(1)}) custom-call(s32[384]{0:T(512)S(1)} %fusion.26.land_ref, s32[384]{0:T(512)S(1)} %reduce.1.cols_ref, s32[1]{0:T(128)} %bitcast.60.count_ref, bf16[32,128,128]{2,1,0:T(8,128)(2,1)S(1)} %bitcast.63, ...), custom_call_target="tpu_custom_call" | custom-call | flops 1610612736 | bytes 18874368 | tf_op jit(solution)/shard_map/forward_products/pallas_call | solution.py:128
  27.8 1.8 %collective-permute-start = (bf16[32,128,128]{2,1,0:T(8,128)(2,1)S(1)}, bf16[32,128,128]{2,1,0:T(8,128)(2,1)S(1)}, u32[]{:S(2)}, u32[]{:S(2)}) collective-permute-start(bf16[32,128,128]{2,1,0:T(8,128)(2,1)S(1)} %get-tuple-element.36), channel_id=1, source_target_pairs={{0,1},{1,0},{2,3},{3,2},{4,5},{5,4},{6,7},{7,6},{8,9},{9,8},{10,11... | collective-permute-start | bytes 3145736 | tf_op jit(solution)/shard_map/ppermute | solution.py:54
  29.7 2.3 %collective-permute-done = bf16[32,128,128]{2,1,0:T(8,128)(2,1)S(1)} collective-permute-done((bf16[32,128,128]{2,1,0:T(8,128)(2,1)S(1)}, bf16[32,128,128]{2,1,0:T(8,128)(2,1)S(1)}, u32[]{:S(2)}, u32[]{:S(2)}) %collective-permute-start) | collective-permute-done | bytes 1048608 | tf_op jit(solution)/shard_map/ppermute | solution.py:54
  32.3 0.5 collective-permute-start.1
  32.8 5.7 %collective-permute-start.7 = (bf16[512,128]{1,0:T(8,128)(2,1)S(1)}, bf16[512,128]{1,0:T(8,128)(2,1)S(1)}, u32[]{:S(2)}, u32[]{:S(2)}) collective-permute-start(bf16[512,128]{1,0:T(8,128)(2,1)S(1)} %get-tuple-element.73), channel_id=1, source_target_pairs={{0,4},{1,29},{2,6},{3,31},{4,8},{5,1},{6,10},{7,3},{8,12},{9,5},{1... | collective-permute-start | bytes 393224 | tf_op jit(solution)/shard_map/ppermute | solution.py:54
  38.5 1.9 %collective-permute-done.7 = bf16[512,128]{1,0:T(8,128)(2,1)S(1)} collective-permute-done((bf16[512,128]{1,0:T(8,128)(2,1)S(1)}, bf16[512,128]{1,0:T(8,128)(2,1)S(1)}, u32[]{:S(2)}, u32[]{:S(2)}) %collective-permute-start.7) | collective-permute-done | bytes 131104 | tf_op jit(solution)/shard_map/ppermute | solution.py:54
  40.5 3.2 %collective-permute-start.8 = (bf16[2,512,128]{2,1,0:T(8,128)(2,1)S(1)}, bf16[2,512,128]{2,1,0:T(8,128)(2,1)S(1)}, u32[]{:S(2)}, u32[]{:S(2)}) collective-permute-start(bf16[2,512,128]{2,1,0:T(8,128)(2,1)S(1)} %pad_maximum_fusion.4), channel_id=1, source_target_pairs={{0,4},{1,29},{2,6},{3,31},{4,8},{5,1},{6,10},{7,3},{8,12},{9,5},{1... | collective-permute-start | bytes 786440 | tf_op jit(solution)/shard_map/ppermute | solution.py:54
  43.7 0.4 add_convert_fusion
  44.2 2.8 %collective-permute-done.8 = bf16[2,512,128]{2,1,0:T(8,128)(2,1)S(1)} collective-permute-done((bf16[2,512,128]{2,1,0:T(8,128)(2,1)S(1)}, bf16[2,512,128]{2,1,0:T(8,128)(2,1)S(1)}, u32[]{:S(2)}, u32[]{:S(2)}) %collective-permute-start.8) | collective-permute-done | bytes 262176 | tf_op jit(solution)/shard_map/ppermute | solution.py:54
  47.0 3.2 %collective-permute-start.9 = (bf16[2,512,128]{2,1,0:T(8,128)(2,1)S(1)}, bf16[2,512,128]{2,1,0:T(8,128)(2,1)S(1)}, u32[]{:S(2)}, u32[]{:S(2)}) collective-permute-start(bf16[2,512,128]{2,1,0:T(8,128)(2,1)S(1)} %add_convert_fusion.3), channel_id=1, source_target_pairs={{0,4},{1,29},{2,6},{3,31},{4,8},{5,1},{6,10},{7,3},{8,12},{9,5},{1... | collective-permute-start | bytes 786440 | tf_op jit(solution)/shard_map/ppermute | solution.py:54
  50.3 1.3 collective-permute-start.3
  51.7 1.9 %collective-permute-done.9 = bf16[2,512,128]{2,1,0:T(8,128)(2,1)S(1)} collective-permute-done((bf16[2,512,128]{2,1,0:T(8,128)(2,1)S(1)}, bf16[2,512,128]{2,1,0:T(8,128)(2,1)S(1)}, u32[]{:S(2)}, u32[]{:S(2)}) %collective-permute-start.9) | collective-permute-done | bytes 262176 | tf_op jit(solution)/shard_map/ppermute | solution.py:54
  53.6 3.2 %collective-permute-start.10 = (bf16[2,512,128]{2,1,0:T(8,128)(2,1)S(1)}, bf16[2,512,128]{2,1,0:T(8,128)(2,1)S(1)}, u32[]{:S(2)}, u32[]{:S(2)}) collective-permute-start(bf16[2,512,128]{2,1,0:T(8,128)(2,1)S(1)} %add_convert_fusion.2), channel_id=1, source_target_pairs={{0,4},{1,29},{2,6},{3,31},{4,8},{5,1},{6,10},{7,3},{8,12},{9,5},{1... | collective-permute-start | bytes 786440 | tf_op jit(solution)/shard_map/ppermute | solution.py:54
  57.0 2.7 %collective-permute-start.4 = (bf16[2,512,128]{2,1,0:T(8,128)(2,1)S(1)}, bf16[2,512,128]{2,1,0:T(8,128)(2,1)S(1)}, u32[]{:S(2)}, u32[]{:S(2)}) collective-permute-start(bf16[2,512,128]{2,1,0:T(8,128)(2,1)S(1)} %fusion.1), channel_id=1, source_target_pairs={{0,4},{1,29},{2,6},{3,31},{4,8},{5,1},{6,10},{7,3},{8,12},{9,5},{1... | collective-permute-start | bytes 786440 | tf_op jit(solution)/shard_map/ppermute | solution.py:54
  59.6 0.5 collective-permute-done.10
  60.2 5.0 %collective-permute-start.11 = (bf16[512,128]{1,0:T(8,128)(2,1)S(1)}, bf16[512,128]{1,0:T(8,128)(2,1)S(1)}, u32[]{:S(2)}, u32[]{:S(2)}) collective-permute-start(bf16[512,128]{1,0:T(8,128)(2,1)S(1)} %slice_bitcast_fusion), channel_id=1, source_target_pairs={{0,1},{1,0},{2,3},{3,2},{4,5},{5,4},{6,7},{7,6},{8,9},{9,8},{10,11... | collective-permute-start | bytes 393224 | tf_op jit(solution)/shard_map/ppermute | solution.py:54
  65.2 1.0 collective-permute-start.5
  66.3 1.6 %collective-permute-start.12 = (bf16[512,128]{1,0:T(8,128)(2,1)S(1)}, bf16[512,128]{1,0:T(8,128)(2,1)S(1)}, u32[]{:S(2)}, u32[]{:S(2)}) collective-permute-start(bf16[512,128]{1,0:T(8,128)(2,1)S(1)} %fusion.8), channel_id=1, source_target_pairs={{0,2},{1,3},{2,0},{3,1},{4,6},{5,7},{6,4},{7,5},{8,10},{9,11},{10,... | collective-permute-start | bytes 393224 | tf_op jit(solution)/shard_map/ppermute | solution.py:54
  67.9 2.6 %collective-permute-done.5 = bf16[2,512,128]{2,1,0:T(8,128)(2,1)S(1)} collective-permute-done((bf16[2,512,128]{2,1,0:T(8,128)(2,1)S(1)}, bf16[2,512,128]{2,1,0:T(8,128)(2,1)S(1)}, u32[]{:S(2)}, u32[]{:S(2)}) %collective-permute-start.5) | collective-permute-done | bytes 262176 | tf_op jit(solution)/shard_map/ppermute | solution.py:54
  70.5 5.3 %collective-permute-start.6 = (bf16[512,128]{1,0:T(8,128)(2,1)S(1)}, bf16[512,128]{1,0:T(8,128)(2,1)S(1)}, u32[]{:S(2)}, u32[]{:S(2)}) collective-permute-start(bf16[512,128]{1,0:T(8,128)(2,1)S(1)} %slice_bitcast_fusion.1), channel_id=1, source_target_pairs={{0,1},{1,0},{2,3},{3,2},{4,5},{5,4},{6,7},{7,6},{8,9},{9,8},{10,11... | collective-permute-start | bytes 393224 | tf_op jit(solution)/shard_map/ppermute | solution.py:54
  75.9 1.0 collective-permute-done.6
  77.0 1.1 fusion
  78.6 0.4 collective-permute-start.15
  79.0 1.6 %collective-permute-start.23 = (bf16[512,128]{1,0:T(8,128)(2,1)S(1)}, bf16[512,128]{1,0:T(8,128)(2,1)S(1)}, u32[]{:S(2)}, u32[]{:S(2)}) collective-permute-start(bf16[512,128]{1,0:T(8,128)(2,1)S(1)} %convolution_convert_fusion), channel_id=1, source_target_pairs={{0,2},{1,3},{2,0},{3,1},{4,6},{5,7},{6,4},{7,5},{8,10},{9,11},{10,... | collective-permute-start | bytes 393224 | tf_op jit(solution)/shard_map/ppermute | solution.py:54
  80.6 0.4 collective-permute-start.13
  81.1 1.6 %collective-permute-start.16 = (f32[64,256]{1,0:T(8,128)S(1)}, f32[64,256]{1,0:T(8,128)S(1)}, u32[]{:S(2)}, u32[]{:S(2)}) collective-permute-start(f32[64,256]{1,0:T(8,128)S(1)} %constant_dynamic-slice_fusion.2), channel_id=1, source_target_pairs={{0,128},{1,129},{2,130},{3,131},{4,132},{5,133},{6,134},{7,135},{8... | collective-permute-start | bytes 196616 | tf_op jit(solution)/shard_map/ppermute | solution.py:54
  82.7 0.4 collective-permute-start.14
  83.1 2.4 %collective-permute-done.23 = bf16[512,128]{1,0:T(8,128)(2,1)S(1)} collective-permute-done((bf16[512,128]{1,0:T(8,128)(2,1)S(1)}, bf16[512,128]{1,0:T(8,128)(2,1)S(1)}, u32[]{:S(2)}, u32[]{:S(2)}) %collective-permute-start.23) | collective-permute-done | bytes 131104 | tf_op jit(solution)/shard_map/ppermute | solution.py:54
  85.5 1.5 %collective-permute-start.24 = (bf16[512,128]{1,0:T(8,128)(2,1)S(1)}, bf16[512,128]{1,0:T(8,128)(2,1)S(1)}, u32[]{:S(2)}, u32[]{:S(2)}) collective-permute-start(bf16[512,128]{1,0:T(8,128)(2,1)S(1)} %collective-permute-done.23), channel_id=1, source_target_pairs={{0,1},{1,0},{2,3},{3,2},{4,5},{5,4},{6,7},{7,6},{8,9},{9,8},{10,11... | collective-permute-start | bytes 393224 | tf_op jit(solution)/shard_map/ppermute | solution.py:54
  87.1 0.9 collective-permute-done.24
  88.0 0.4 collective-permute-start.25
  88.5 1.1 collective-permute-start.17
  89.6 0.9 collective-permute-start.18
  90.4 3.4 %collective-permute-done.18 = f32[32,256]{1,0:T(8,128)S(1)} collective-permute-done((f32[32,256]{1,0:T(8,128)S(1)}, f32[32,256]{1,0:T(8,128)S(1)}, u32[]{:S(2)}, u32[]{:S(2)}) %collective-permute-start.18) | collective-permute-done | bytes 32800 | tf_op jit(solution)/shard_map/ppermute | solution.py:54
  93.8 1.0 collective-permute-start.26
  94.9 1.5 %collective-permute-done.17 = bf16[1024,128]{1,0:T(8,128)(2,1)S(1)} collective-permute-done((bf16[1024,128]{1,0:T(8,128)(2,1)S(1)}, bf16[1024,128]{1,0:T(8,128)(2,1)S(1)}, u32[]{:S(2)}, u32[]{:S(2)}) %collective-permute-start.17) | collective-permute-done | bytes 262176 | tf_op jit(solution)/shard_map/ppermute | solution.py:54
  96.5 2.8 %collective-permute-start.29 = (bf16[2048,128]{1,0:T(8,128)(2,1)S(1)}, bf16[2048,128]{1,0:T(8,128)(2,1)S(1)}, u32[]{:S(2)}, u32[]{:S(2)}) collective-permute-start(bf16[2048,128]{1,0:T(8,128)(2,1)S(1)} %pad_maximum_fusion), channel_id=1, source_target_pairs={{0,1},{1,0},{2,3},{3,2},{4,5},{5,4},{6,7},{7,6},{8,9},{9,8},{10,11... | collective-permute-start | bytes 1572872 | tf_op jit(solution)/shard_map/ppermute | solution.py:54
  99.3 0.9 collective-permute-start.19
  100.1 1.6 %collective-permute-start.27 = (bf16[1024,128]{1,0:T(8,128)(2,1)S(1)}, bf16[1024,128]{1,0:T(8,128)(2,1)S(1)}, u32[]{:S(2)}, u32[]{:S(2)}) collective-permute-start(bf16[1024,128]{1,0:T(8,128)(2,1)S(1)} %collective-permute-done.26), channel_id=1, source_target_pairs={{0,4},{1,29},{2,6},{3,31},{4,8},{5,1},{6,10},{7,3},{8,12},{9,5},{1... | collective-permute-start | bytes 786440 | tf_op jit(solution)/shard_map/ppermute | solution.py:54
  101.8 2.1 %collective-permute-start.30 = (bf16[2048,128]{1,0:T(8,128)(2,1)S(1)}, bf16[2048,128]{1,0:T(8,128)(2,1)S(1)}, u32[]{:S(2)}, u32[]{:S(2)}) collective-permute-start(bf16[2048,128]{1,0:T(8,128)(2,1)S(1)} %pad_maximum_fusion.1), channel_id=1, source_target_pairs={{0,1},{1,0},{2,3},{3,2},{4,5},{5,4},{6,7},{7,6},{8,9},{9,8},{10,11... | collective-permute-start | bytes 1572872 | tf_op jit(solution)/shard_map/ppermute | solution.py:54
  103.9 0.9 collective-permute-done.19
  104.8 2.1 %collective-permute-start.22 = (f32[16,256]{1,0:T(8,128)S(1)}, f32[16,256]{1,0:T(8,128)S(1)}, u32[]{:S(2)}, u32[]{:S(2)}) collective-permute-start(f32[16,256]{1,0:T(8,128)S(1)} %dynamic-slice_add_fusion.2), channel_id=1, source_target_pairs={{0,2},{1,3},{2,0},{3,1},{4,6},{5,7},{6,4},{7,5},{8,10},{9,11},{10,... | collective-permute-start | bytes 49160 | tf_op jit(solution)/shard_map/ppermute | solution.py:54
  106.9 0.4 collective-permute-done.27
  107.4 4.1 %collective-permute-start.31 = (bf16[2048,128]{1,0:T(8,128)(2,1)S(1)}, bf16[2048,128]{1,0:T(8,128)(2,1)S(1)}, u32[]{:S(2)}, u32[]{:S(2)}) collective-permute-start(bf16[2048,128]{1,0:T(8,128)(2,1)S(1)} %pad_maximum_fusion.2), channel_id=1, source_target_pairs={{0,1},{1,0},{2,3},{3,2},{4,5},{5,4},{6,7},{7,6},{8,9},{9,8},{10,11... | collective-permute-start | bytes 1572872 | tf_op jit(solution)/shard_map/ppermute | solution.py:54
  111.5 0.8 collective-permute-start.21
  112.5 3.2 %collective-permute-done.21 = bf16[512,128]{1,0:T(8,128)(2,1)S(1)} collective-permute-done((bf16[512,128]{1,0:T(8,128)(2,1)S(1)}, bf16[512,128]{1,0:T(8,128)(2,1)S(1)}, u32[]{:S(2)}, u32[]{:S(2)}) %collective-permute-start.21) | collective-permute-done | bytes 131104 | tf_op jit(solution)/shard_map/ppermute | solution.py:54
  115.6 1.7 %collective-permute-done.28 = bf16[512,128]{1,0:T(8,128)(2,1)S(1)} collective-permute-done((bf16[512,128]{1,0:T(8,128)(2,1)S(1)}, bf16[512,128]{1,0:T(8,128)(2,1)S(1)}, u32[]{:S(2)}, u32[]{:S(2)}) %collective-permute-start.28) | collective-permute-done | bytes 131104 | tf_op jit(solution)/shard_map/ppermute | solution.py:54
  117.3 2.2 %collective-permute-start.32 = (bf16[1024,128]{1,0:T(8,128)(2,1)S(1)}, bf16[1024,128]{1,0:T(8,128)(2,1)S(1)}, u32[]{:S(2)}, u32[]{:S(2)}) collective-permute-start(bf16[1024,128]{1,0:T(8,128)(2,1)S(1)} %pad_maximum_fusion.5), channel_id=1, source_target_pairs={{0,1},{1,0},{2,3},{3,2},{4,5},{5,4},{6,7},{7,6},{8,9},{9,8},{10,11... | collective-permute-start | bytes 786440 | tf_op jit(solution)/shard_map/ppermute | solution.py:54
  119.5 1.2 collective-permute-done.32
  121.4 5.1 %backward_products.1 = bf16[32,128,128]{2,1,0:T(8,128)(2,1)} custom-call(s32[384]{0:T(512)S(1)} %get-tuple-element.65.land_ref, s32[384]{0:T(512)S(1)} %reduce.1.cols_ref, s32[1]{0:T(128)} %bitcast.61.count_ref, bf16[128,128,128]{2,1,0:T(8,128)(2,1)S(1)} %bitcast.62, bf16[384,128,128]{2,1,0:T(8,128)(2,1)} %bitcast.65), custom_call_target="tpu_custom_call" | custom-call | flops 1610612736 | bytes 18874368 | tf_op jit(solution)/shard_map/backward_products/pallas_call | solution.py:166
  126.5 4.0 %all-to-all-start.1 = ((bf16[8,512,128]{2,1,0:T(8,128)(2,1)}), bf16[8,512,128]{2,1,0:T(8,128)(2,1)S(1)}, u32[]{:S(2)}, u32[]{:S(2)}) async-start(bf16[8,512,128]{2,1,0:T(8,128)(2,1)} %bitcast.23), calls=%async_computation.1 | async-start | bytes 2097152 | tf_op jit(solution)/shard_map/all_to_all | solution.py:311
  130.5 2.6 %collective-permute-done.33 = f32[16,256]{1,0:T(8,128)S(1)} collective-permute-done((f32[16,256]{1,0:T(8,128)S(1)}, f32[16,256]{1,0:T(8,128)S(1)}, u32[]{:S(2)}, u32[]{:S(2)}) %collective-permute-start.33) | collective-permute-done | bytes 16416 | tf_op jit(solution)/shard_map/ppermute | solution.py:54
  133.1 2.9 %collective-permute-start.34 = (f32[16,256]{1,0:T(8,128)S(1)}, f32[16,256]{1,0:T(8,128)S(1)}, u32[]{:S(2)}, u32[]{:S(2)}) collective-permute-start(f32[16,256]{1,0:T(8,128)S(1)} %add.207), channel_id=1, source_target_pairs={{0,12},{1,13},{2,14},{3,15},{4,8},{5,9},{6,10},{7,11},{8,4},{9,5},... | collective-permute-start | bytes 49160 | tf_op jit(solution)/shard_map/ppermute | solution.py:54
  136.0 1.8 %collective-permute-done.34 = f32[16,256]{1,0:T(8,128)S(1)} collective-permute-done((f32[16,256]{1,0:T(8,128)S(1)}, f32[16,256]{1,0:T(8,128)S(1)}, u32[]{:S(2)}, u32[]{:S(2)}) %collective-permute-start.34) | collective-permute-done | bytes 16416 | tf_op jit(solution)/shard_map/ppermute | solution.py:54
  137.8 1.9 %collective-permute-start.35 = (f32[16,256]{1,0:T(8,128)S(1)}, f32[16,256]{1,0:T(8,128)S(1)}, u32[]{:S(2)}, u32[]{:S(2)}) collective-permute-start(f32[16,256]{1,0:T(8,128)S(1)} %add.208), channel_id=1, source_target_pairs={{0,28},{1,29},{2,30},{3,31},{4,24},{5,25},{6,26},{7,27},{8,20},{9,... | collective-permute-start | bytes 49160 | tf_op jit(solution)/shard_map/ppermute | solution.py:54
  139.7 2.2 %collective-permute-done.35 = f32[16,256]{1,0:T(8,128)S(1)} collective-permute-done((f32[16,256]{1,0:T(8,128)S(1)}, f32[16,256]{1,0:T(8,128)S(1)}, u32[]{:S(2)}, u32[]{:S(2)}) %collective-permute-start.35) | collective-permute-done | bytes 16416 | tf_op jit(solution)/shard_map/ppermute | solution.py:54
  141.9 0.6 add.209
  142.5 3.0 %all-to-all-done.1 = bf16[8,512,128]{2,1,0:T(8,128)(2,1)S(1)} async-done(((bf16[8,512,128]{2,1,0:T(8,128)(2,1)}), bf16[8,512,128]{2,1,0:T(8,128)(2,1)S(1)}, u32[]{:S(2)}, u32[]{:S(2)}) %all-to-all-start.1) | async-done | bytes 1048608 | tf_op jit(solution)/shard_map/all_to_all | solution.py:311
  145.6 0.8 fusion.10
  (88 shorter events, 2.9 us)
Async XLA Ops:
  0.6 76.4 %copy-start = (bf16[128,256]{1,0:T(8,128)(2,1)S(1)}, bf16[128,256]{1,0:T(8,128)(2,1)}, u32[]{:S(2)}) copy-start(bf16[128,256]{1,0:T(8,128)(2,1)} %param.9) | copy-start | bytes 196612
  2.6 20.9 %all-to-all-start = ((bf16[8,512,128]{2,1,0:T(8,128)(2,1)}), bf16[8,512,128]{2,1,0:T(8,128)(2,1)S(1)}, u32[]{:S(2)}, u32[]{:S(2)}) async-start(bf16[8,512,128]{2,1,0:T(8,128)(2,1)} %spread.1), calls=%async_computation | async-start | bytes 2097152 | tf_op jit(solution)/shard_map/all_to_all | solution.py:254
  27.8 4.1 %collective-permute-start = (bf16[32,128,128]{2,1,0:T(8,128)(2,1)S(1)}, bf16[32,128,128]{2,1,0:T(8,128)(2,1)S(1)}, u32[]{:S(2)}, u32[]{:S(2)}) collective-permute-start(bf16[32,128,128]{2,1,0:T(8,128)(2,1)S(1)} %get-tuple-element.36), channel_id=1, source_target_pairs={{0,1},{1,0},{2,3},{3,2},{4,5},{5,4},{6,7},{7,6},{8,9},{9,8},{10,11... | collective-permute-start | bytes 3145736 | tf_op jit(solution)/shard_map/ppermute | solution.py:54
  32.3 11.3 %collective-permute-start.1 = (bf16[32,128,128]{2,1,0:T(8,128)(2,1)S(1)}, bf16[32,128,128]{2,1,0:T(8,128)(2,1)S(1)}, u32[]{:S(2)}, u32[]{:S(2)}) collective-permute-start(bf16[32,128,128]{2,1,0:T(8,128)(2,1)S(1)} %get-tuple-element.37), channel_id=1, source_target_pairs={{0,1},{1,0},{2,3},{3,2},{4,5},{5,4},{6,7},{7,6},{8,9},{9,8},{10,11... | collective-permute-start | bytes 3145736 | tf_op jit(solution)/shard_map/ppermute | solution.py:54
  32.8 7.6 %collective-permute-start.7 = (bf16[512,128]{1,0:T(8,128)(2,1)S(1)}, bf16[512,128]{1,0:T(8,128)(2,1)S(1)}, u32[]{:S(2)}, u32[]{:S(2)}) collective-permute-start(bf16[512,128]{1,0:T(8,128)(2,1)S(1)} %get-tuple-element.73), channel_id=1, source_target_pairs={{0,4},{1,29},{2,6},{3,31},{4,8},{5,1},{6,10},{7,3},{8,12},{9,5},{1... | collective-permute-start | bytes 393224 | tf_op jit(solution)/shard_map/ppermute | solution.py:54
  40.5 6.5 %collective-permute-start.8 = (bf16[2,512,128]{2,1,0:T(8,128)(2,1)S(1)}, bf16[2,512,128]{2,1,0:T(8,128)(2,1)S(1)}, u32[]{:S(2)}, u32[]{:S(2)}) collective-permute-start(bf16[2,512,128]{2,1,0:T(8,128)(2,1)S(1)} %pad_maximum_fusion.4), channel_id=1, source_target_pairs={{0,4},{1,29},{2,6},{3,31},{4,8},{5,1},{6,10},{7,3},{8,12},{9,5},{1... | collective-permute-start | bytes 786440 | tf_op jit(solution)/shard_map/ppermute | solution.py:54
  44.0 32.8 %copy-start.1 = (bf16[1,512,128]{2,1,0:T(8,128)(2,1)S(1)}, bf16[1,512,128]{2,1,0:T(8,128)(2,1)}, u32[]{:S(2)}) copy-start(bf16[1,512,128]{2,1,0:T(8,128)(2,1)} %param.8) | copy-start | bytes 393220
  44.0 32.8 %copy-start.2 = (f32[1,512]{1,0:T(1,128)S(1)}, f32[1,512]{1,0:T(1,128)}, u32[]{:S(2)}) copy-start(f32[1,512]{1,0:T(1,128)} %param.11) | copy-start | bytes 6148
  44.1 33.0 %copy-start.3 = (bf16[1,512,256]{2,1,0:T(8,128)(2,1)S(1)}, bf16[1,512,256]{2,1,0:T(8,128)(2,1)}, u32[]{:S(2)}) copy-start(bf16[1,512,256]{2,1,0:T(8,128)(2,1)} %param.10) | copy-start | bytes 786436
  44.1 6.1 %collective-permute-start.2 = (bf16[512,128]{1,0:T(8,128)(2,1)S(1)}, bf16[512,128]{1,0:T(8,128)(2,1)S(1)}, u32[]{:S(2)}, u32[]{:S(2)}) collective-permute-start(bf16[512,128]{1,0:T(8,128)(2,1)S(1)} %bitcast.75), channel_id=1, source_target_pairs={{0,4},{1,29},{2,6},{3,31},{4,8},{5,1},{6,10},{7,3},{8,12},{9,5},{1... | collective-permute-start | bytes 393224 | tf_op jit(solution)/shard_map/ppermute | solution.py:54
  47.0 6.5 %collective-permute-start.9 = (bf16[2,512,128]{2,1,0:T(8,128)(2,1)S(1)}, bf16[2,512,128]{2,1,0:T(8,128)(2,1)S(1)}, u32[]{:S(2)}, u32[]{:S(2)}) collective-permute-start(bf16[2,512,128]{2,1,0:T(8,128)(2,1)S(1)} %add_convert_fusion.3), channel_id=1, source_target_pairs={{0,4},{1,29},{2,6},{3,31},{4,8},{5,1},{6,10},{7,3},{8,12},{9,5},{1... | collective-permute-start | bytes 786440 | tf_op jit(solution)/shard_map/ppermute | solution.py:54
  50.3 6.5 %collective-permute-start.3 = (bf16[2,512,128]{2,1,0:T(8,128)(2,1)S(1)}, bf16[2,512,128]{2,1,0:T(8,128)(2,1)S(1)}, u32[]{:S(2)}, u32[]{:S(2)}) collective-permute-start(bf16[2,512,128]{2,1,0:T(8,128)(2,1)S(1)} %pad_maximum_fusion.3), channel_id=1, source_target_pairs={{0,4},{1,29},{2,6},{3,31},{4,8},{5,1},{6,10},{7,3},{8,12},{9,5},{1... | collective-permute-start | bytes 786440 | tf_op jit(solution)/shard_map/ppermute | solution.py:54
  53.6 6.5 %collective-permute-start.10 = (bf16[2,512,128]{2,1,0:T(8,128)(2,1)S(1)}, bf16[2,512,128]{2,1,0:T(8,128)(2,1)S(1)}, u32[]{:S(2)}, u32[]{:S(2)}) collective-permute-start(bf16[2,512,128]{2,1,0:T(8,128)(2,1)S(1)} %add_convert_fusion.2), channel_id=1, source_target_pairs={{0,4},{1,29},{2,6},{3,31},{4,8},{5,1},{6,10},{7,3},{8,12},{9,5},{1... | collective-permute-start | bytes 786440 | tf_op jit(solution)/shard_map/ppermute | solution.py:54
  57.0 8.2 %collective-permute-start.4 = (bf16[2,512,128]{2,1,0:T(8,128)(2,1)S(1)}, bf16[2,512,128]{2,1,0:T(8,128)(2,1)S(1)}, u32[]{:S(2)}, u32[]{:S(2)}) collective-permute-start(bf16[2,512,128]{2,1,0:T(8,128)(2,1)S(1)} %fusion.1), channel_id=1, source_target_pairs={{0,4},{1,29},{2,6},{3,31},{4,8},{5,1},{6,10},{7,3},{8,12},{9,5},{1... | collective-permute-start | bytes 786440 | tf_op jit(solution)/shard_map/ppermute | solution.py:54
  60.2 6.1 %collective-permute-start.11 = (bf16[512,128]{1,0:T(8,128)(2,1)S(1)}, bf16[512,128]{1,0:T(8,128)(2,1)S(1)}, u32[]{:S(2)}, u32[]{:S(2)}) collective-permute-start(bf16[512,128]{1,0:T(8,128)(2,1)S(1)} %slice_bitcast_fusion), channel_id=1, source_target_pairs={{0,1},{1,0},{2,3},{3,2},{4,5},{5,4},{6,7},{7,6},{8,9},{9,8},{10,11... | collective-permute-start | bytes 393224 | tf_op jit(solution)/shard_map/ppermute | solution.py:54
  65.2 5.3 %collective-permute-start.5 = (bf16[2,512,128]{2,1,0:T(8,128)(2,1)S(1)}, bf16[2,512,128]{2,1,0:T(8,128)(2,1)S(1)}, u32[]{:S(2)}, u32[]{:S(2)}) collective-permute-start(bf16[2,512,128]{2,1,0:T(8,128)(2,1)S(1)} %fusion.2), channel_id=1, source_target_pairs={{0,4},{1,29},{2,6},{3,31},{4,8},{5,1},{6,10},{7,3},{8,12},{9,5},{1... | collective-permute-start | bytes 786440 | tf_op jit(solution)/shard_map/ppermute | solution.py:54
  66.3 9.6 %collective-permute-start.12 = (bf16[512,128]{1,0:T(8,128)(2,1)S(1)}, bf16[512,128]{1,0:T(8,128)(2,1)S(1)}, u32[]{:S(2)}, u32[]{:S(2)}) collective-permute-start(bf16[512,128]{1,0:T(8,128)(2,1)S(1)} %fusion.8), channel_id=1, source_target_pairs={{0,2},{1,3},{2,0},{3,1},{4,6},{5,7},{6,4},{7,5},{8,10},{9,11},{10,... | collective-permute-start | bytes 393224 | tf_op jit(solution)/shard_map/ppermute | solution.py:54
  70.5 6.3 %collective-permute-start.6 = (bf16[512,128]{1,0:T(8,128)(2,1)S(1)}, bf16[512,128]{1,0:T(8,128)(2,1)S(1)}, u32[]{:S(2)}, u32[]{:S(2)}) collective-permute-start(bf16[512,128]{1,0:T(8,128)(2,1)S(1)} %slice_bitcast_fusion.1), channel_id=1, source_target_pairs={{0,1},{1,0},{2,3},{3,2},{4,5},{5,4},{6,7},{7,6},{8,9},{9,8},{10,11... | collective-permute-start | bytes 393224 | tf_op jit(solution)/shard_map/ppermute | solution.py:54
  78.6 2.5 %collective-permute-start.15 = (f32[128,256]{1,0:T(8,128)S(1)}, f32[128,256]{1,0:T(8,128)S(1)}, u32[]{:S(2)}, u32[]{:S(2)}) collective-permute-start(f32[128,256]{1,0:T(8,128)S(1)} %convolution_multiply_fusion), channel_id=1, source_target_pairs={{0,1},{1,0},{2,3},{3,2},{4,5},{5,4},{6,7},{7,6},{8,9},{9,8},{10,11... | collective-permute-start | bytes 393224 | tf_op jit(solution)/shard_map/ppermute | solution.py:54
  79.0 6.5 %collective-permute-start.23 = (bf16[512,128]{1,0:T(8,128)(2,1)S(1)}, bf16[512,128]{1,0:T(8,128)(2,1)S(1)}, u32[]{:S(2)}, u32[]{:S(2)}) collective-permute-start(bf16[512,128]{1,0:T(8,128)(2,1)S(1)} %convolution_convert_fusion), channel_id=1, source_target_pairs={{0,2},{1,3},{2,0},{3,1},{4,6},{5,7},{6,4},{7,5},{8,10},{9,11},{10,... | collective-permute-start | bytes 393224 | tf_op jit(solution)/shard_map/ppermute | solution.py:54
  80.6 2.1 %collective-permute-start.13 = (bf16[512,128]{1,0:T(8,128)(2,1)S(1)}, bf16[512,128]{1,0:T(8,128)(2,1)S(1)}, u32[]{:S(2)}, u32[]{:S(2)}) collective-permute-start(bf16[512,128]{1,0:T(8,128)(2,1)S(1)} %convolution_convert_fusion), channel_id=1, source_target_pairs={{0,1},{1,0},{2,3},{3,2},{4,5},{5,4},{6,7},{7,6},{8,9},{9,8},{10,11... | collective-permute-start | bytes 393224 | tf_op jit(solution)/shard_map/ppermute | solution.py:54
  81.1 5.9 %collective-permute-start.16 = (f32[64,256]{1,0:T(8,128)S(1)}, f32[64,256]{1,0:T(8,128)S(1)}, u32[]{:S(2)}, u32[]{:S(2)}) collective-permute-start(f32[64,256]{1,0:T(8,128)S(1)} %constant_dynamic-slice_fusion.2), channel_id=1, source_target_pairs={{0,128},{1,129},{2,130},{3,131},{4,132},{5,133},{6,134},{7,135},{8... | collective-permute-start | bytes 196616 | tf_op jit(solution)/shard_map/ppermute | solution.py:54
  82.7 5.8 %collective-permute-start.14 = (bf16[1024,128]{1,0:T(8,128)(2,1)S(1)}, bf16[1024,128]{1,0:T(8,128)(2,1)S(1)}, u32[]{:S(2)}, u32[]{:S(2)}) collective-permute-start(bf16[1024,128]{1,0:T(8,128)(2,1)S(1)} %constant_dynamic-update-slice_fusion), channel_id=1, source_target_pairs={{0,4},{1,29},{2,6},{3,31},{4,8},{5,1},{6,10},{7,3},{8,12},{9,5},{1... | collective-permute-start | bytes 786440 | tf_op jit(solution)/shard_map/ppermute | solution.py:54
  85.5 2.5 %collective-permute-start.24 = (bf16[512,128]{1,0:T(8,128)(2,1)S(1)}, bf16[512,128]{1,0:T(8,128)(2,1)S(1)}, u32[]{:S(2)}, u32[]{:S(2)}) collective-permute-start(bf16[512,128]{1,0:T(8,128)(2,1)S(1)} %collective-permute-done.23), channel_id=1, source_target_pairs={{0,1},{1,0},{2,3},{3,2},{4,5},{5,4},{6,7},{7,6},{8,9},{9,8},{10,11... | collective-permute-start | bytes 393224 | tf_op jit(solution)/shard_map/ppermute | solution.py:54
  88.0 5.8 %collective-permute-start.25 = (bf16[1024,128]{1,0:T(8,128)(2,1)S(1)}, bf16[1024,128]{1,0:T(8,128)(2,1)S(1)}, u32[]{:S(2)}, u32[]{:S(2)}) collective-permute-start(bf16[1024,128]{1,0:T(8,128)(2,1)S(1)} %constant_dynamic-update-slice_fusion.2), channel_id=1, source_target_pairs={{0,4},{1,29},{2,6},{3,31},{4,8},{5,1},{6,10},{7,3},{8,12},{9,5},{1... | collective-permute-start | bytes 786440 | tf_op jit(solution)/shard_map/ppermute | solution.py:54
  88.5 8.0 %collective-permute-start.17 = (bf16[1024,128]{1,0:T(8,128)(2,1)S(1)}, bf16[1024,128]{1,0:T(8,128)(2,1)S(1)}, u32[]{:S(2)}, u32[]{:S(2)}) collective-permute-start(bf16[1024,128]{1,0:T(8,128)(2,1)S(1)} %collective-permute-done.14), channel_id=1, source_target_pairs={{0,4},{1,29},{2,6},{3,31},{4,8},{5,1},{6,10},{7,3},{8,12},{9,5},{1... | collective-permute-start | bytes 786440 | tf_op jit(solution)/shard_map/ppermute | solution.py:54
  89.6 4.3 %collective-permute-start.18 = (f32[32,256]{1,0:T(8,128)S(1)}, f32[32,256]{1,0:T(8,128)S(1)}, u32[]{:S(2)}, u32[]{:S(2)}) collective-permute-start(f32[32,256]{1,0:T(8,128)S(1)} %constant_dynamic-slice_fusion.1), channel_id=1, source_target_pairs={{0,64},{1,65},{2,66},{3,67},{4,68},{5,69},{6,70},{7,71},{8,72},{9,... | collective-permute-start | bytes 98312 | tf_op jit(solution)/shard_map/ppermute | solution.py:54
  93.8 6.3 %collective-permute-start.26 = (bf16[1024,128]{1,0:T(8,128)(2,1)S(1)}, bf16[1024,128]{1,0:T(8,128)(2,1)S(1)}, u32[]{:S(2)}, u32[]{:S(2)}) collective-permute-start(bf16[1024,128]{1,0:T(8,128)(2,1)S(1)} %collective-permute-done.25), channel_id=1, source_target_pairs={{0,4},{1,29},{2,6},{3,31},{4,8},{5,1},{6,10},{7,3},{8,12},{9,5},{1... | collective-permute-start | bytes 786440 | tf_op jit(solution)/shard_map/ppermute | solution.py:54
  96.4 5.4 %collective-permute-start.20 = (f32[16,256]{1,0:T(8,128)S(1)}, f32[16,256]{1,0:T(8,128)S(1)}, u32[]{:S(2)}, u32[]{:S(2)}) collective-permute-start(f32[16,256]{1,0:T(8,128)S(1)} %constant_dynamic-slice_fusion), channel_id=1, source_target_pairs={{0,32},{1,33},{2,34},{3,35},{4,36},{5,37},{6,38},{7,39},{8,40},{9,... | collective-permute-start | bytes 49160 | tf_op jit(solution)/shard_map/ppermute | solution.py:54
  96.5 23.1 %collective-permute-start.29 = (bf16[2048,128]{1,0:T(8,128)(2,1)S(1)}, bf16[2048,128]{1,0:T(8,128)(2,1)S(1)}, u32[]{:S(2)}, u32[]{:S(2)}) collective-permute-start(bf16[2048,128]{1,0:T(8,128)(2,1)S(1)} %pad_maximum_fusion), channel_id=1, source_target_pairs={{0,1},{1,0},{2,3},{3,2},{4,5},{5,4},{6,7},{7,6},{8,9},{9,8},{10,11... | collective-permute-start | bytes 1572872 | tf_op jit(solution)/shard_map/ppermute | solution.py:54
  99.3 5.5 %collective-permute-start.19 = (bf16[1024,128]{1,0:T(8,128)(2,1)S(1)}, bf16[1024,128]{1,0:T(8,128)(2,1)S(1)}, u32[]{:S(2)}, u32[]{:S(2)}) collective-permute-start(bf16[1024,128]{1,0:T(8,128)(2,1)S(1)} %collective-permute-done.17), channel_id=1, source_target_pairs={{0,4},{1,29},{2,6},{3,31},{4,8},{5,1},{6,10},{7,3},{8,12},{9,5},{1... | collective-permute-start | bytes 786440 | tf_op jit(solution)/shard_map/ppermute | solution.py:54
  100.1 7.2 %collective-permute-start.27 = (bf16[1024,128]{1,0:T(8,128)(2,1)S(1)}, bf16[1024,128]{1,0:T(8,128)(2,1)S(1)}, u32[]{:S(2)}, u32[]{:S(2)}) collective-permute-start(bf16[1024,128]{1,0:T(8,128)(2,1)S(1)} %collective-permute-done.26), channel_id=1, source_target_pairs={{0,4},{1,29},{2,6},{3,31},{4,8},{5,1},{6,10},{7,3},{8,12},{9,5},{1... | collective-permute-start | bytes 786440 | tf_op jit(solution)/shard_map/ppermute | solution.py:54
  101.8 17.7 %collective-permute-start.30 = (bf16[2048,128]{1,0:T(8,128)(2,1)S(1)}, bf16[2048,128]{1,0:T(8,128)(2,1)S(1)}, u32[]{:S(2)}, u32[]{:S(2)}) collective-permute-start(bf16[2048,128]{1,0:T(8,128)(2,1)S(1)} %pad_maximum_fusion.1), channel_id=1, source_target_pairs={{0,1},{1,0},{2,3},{3,2},{4,5},{5,4},{6,7},{7,6},{8,9},{9,8},{10,11... | collective-permute-start | bytes 1572872 | tf_op jit(solution)/shard_map/ppermute | solution.py:54
  104.8 7.5 %collective-permute-start.22 = (f32[16,256]{1,0:T(8,128)S(1)}, f32[16,256]{1,0:T(8,128)S(1)}, u32[]{:S(2)}, u32[]{:S(2)}) collective-permute-start(f32[16,256]{1,0:T(8,128)S(1)} %dynamic-slice_add_fusion.2), channel_id=1, source_target_pairs={{0,2},{1,3},{2,0},{3,1},{4,6},{5,7},{6,4},{7,5},{8,10},{9,11},{10,... | collective-permute-start | bytes 49160 | tf_op jit(solution)/shard_map/ppermute | solution.py:54
  107.4 13.3 %collective-permute-start.31 = (bf16[2048,128]{1,0:T(8,128)(2,1)S(1)}, bf16[2048,128]{1,0:T(8,128)(2,1)S(1)}, u32[]{:S(2)}, u32[]{:S(2)}) collective-permute-start(bf16[2048,128]{1,0:T(8,128)(2,1)S(1)} %pad_maximum_fusion.2), channel_id=1, source_target_pairs={{0,1},{1,0},{2,3},{3,2},{4,5},{5,4},{6,7},{7,6},{8,9},{9,8},{10,11... | collective-permute-start | bytes 1572872 | tf_op jit(solution)/shard_map/ppermute | solution.py:54
  111.5 4.1 %collective-permute-start.21 = (bf16[512,128]{1,0:T(8,128)(2,1)S(1)}, bf16[512,128]{1,0:T(8,128)(2,1)S(1)}, u32[]{:S(2)}, u32[]{:S(2)}) collective-permute-start(bf16[512,128]{1,0:T(8,128)(2,1)S(1)} %slice.87), channel_id=1, source_target_pairs={{0,4},{1,29},{2,6},{3,31},{4,8},{5,1},{6,10},{7,3},{8,12},{9,5},{1... | collective-permute-start | bytes 393224 | tf_op jit(solution)/shard_map/ppermute | solution.py:54
  112.4 5.0 %collective-permute-start.28 = (bf16[512,128]{1,0:T(8,128)(2,1)S(1)}, bf16[512,128]{1,0:T(8,128)(2,1)S(1)}, u32[]{:S(2)}, u32[]{:S(2)}) collective-permute-start(bf16[512,128]{1,0:T(8,128)(2,1)S(1)} %slice.99), channel_id=1, source_target_pairs={{0,4},{1,29},{2,6},{3,31},{4,8},{5,1},{6,10},{7,3},{8,12},{9,5},{1... | collective-permute-start | bytes 393224 | tf_op jit(solution)/shard_map/ppermute | solution.py:54
  117.3 3.3 %collective-permute-start.32 = (bf16[1024,128]{1,0:T(8,128)(2,1)S(1)}, bf16[1024,128]{1,0:T(8,128)(2,1)S(1)}, u32[]{:S(2)}, u32[]{:S(2)}) collective-permute-start(bf16[1024,128]{1,0:T(8,128)(2,1)S(1)} %pad_maximum_fusion.5), channel_id=1, source_target_pairs={{0,1},{1,0},{2,3},{3,2},{4,5},{5,4},{6,7},{7,6},{8,9},{9,8},{10,11... | collective-permute-start | bytes 786440 | tf_op jit(solution)/shard_map/ppermute | solution.py:54
  126.5 19.0 %all-to-all-start.1 = ((bf16[8,512,128]{2,1,0:T(8,128)(2,1)}), bf16[8,512,128]{2,1,0:T(8,128)(2,1)S(1)}, u32[]{:S(2)}, u32[]{:S(2)}) async-start(bf16[8,512,128]{2,1,0:T(8,128)(2,1)} %bitcast.23), calls=%async_computation.1 | async-start | bytes 2097152 | tf_op jit(solution)/shard_map/all_to_all | solution.py:311
  130.5 2.6 %collective-permute-start.33 = (f32[16,256]{1,0:T(8,128)S(1)}, f32[16,256]{1,0:T(8,128)S(1)}, u32[]{:S(2)}, u32[]{:S(2)}) collective-permute-start(f32[16,256]{1,0:T(8,128)S(1)} %add.205), channel_id=1, source_target_pairs={{0,4},{1,5},{2,6},{3,7},{4,0},{5,1},{6,2},{7,3},{8,12},{9,13},{10,... | collective-permute-start | bytes 49160 | tf_op jit(solution)/shard_map/ppermute | solution.py:54
  133.1 4.7 %collective-permute-start.34 = (f32[16,256]{1,0:T(8,128)S(1)}, f32[16,256]{1,0:T(8,128)S(1)}, u32[]{:S(2)}, u32[]{:S(2)}) collective-permute-start(f32[16,256]{1,0:T(8,128)S(1)} %add.207), channel_id=1, source_target_pairs={{0,12},{1,13},{2,14},{3,15},{4,8},{5,9},{6,10},{7,11},{8,4},{9,5},... | collective-permute-start | bytes 49160 | tf_op jit(solution)/shard_map/ppermute | solution.py:54
  137.8 4.1 %collective-permute-start.35 = (f32[16,256]{1,0:T(8,128)S(1)}, f32[16,256]{1,0:T(8,128)S(1)}, u32[]{:S(2)}, u32[]{:S(2)}) collective-permute-start(f32[16,256]{1,0:T(8,128)S(1)} %add.208), channel_id=1, source_target_pairs={{0,28},{1,29},{2,30},{3,31},{4,24},{5,25},{6,26},{7,27},{8,20},{9,... | collective-permute-start | bytes 49160 | tf_op jit(solution)/shard_map/ppermute | solution.py:54

commit v5 on v4

--- a/solution.py
+++ b/solution.py
@@ -43,7 +43,7 @@
 Z_RING = _pairs(lambda xl, y, z, xh, c: (xl, y, (z + 1 - 2 * c) % 8, xh, c))
 REP_SWAPS = (
     _pairs(lambda xl, y, z, xh, c: (1 - xl, y, z, xh, c)),
-    _pairs(lambda xl, y, z, xh, c: (xl, y ^ 2, z, xh, c)),
+    _pairs(lambda xl, y, z, xh, c: (xl, y ^ 3, z, xh, c)),
     _pairs(lambda xl, y, z, xh, c: (xl, y ^ 1, z, xh, c)),
 )
 CORE_SWAP = _pairs(lambda xl, y, z, xh, c: (xl, y, z, xh, 1 - c))
@@ -309,7 +309,7 @@
     columns = backward_products(land_bwd, cols, count, grads, tiles)
     columns, weight_sum = tied(columns, weight_sum)
     parts = lax.all_to_all(columns.reshape(8, 512, BS), REP, 0, 0)
-    for k in (1, 3, 7):
+    for k in (1, 2, 6):
         weight_sum = weight_sum + send(weight_sum, z_flip(k))
     feature_grad = (
         jnp.sum(parts.astype(jnp.float32), 0) + scale * row_grad.astype(jnp.float32)

time: 147 us -> 147 us (level)
  starting transfers between devices: 75.5 us -> 71.4 us
  waiting for transfers between devices: 50.9 us -> 53.5 us
  Pallas kernels: 11.4 us -> 13.2 us
    ppermute x36, starting transfers between devices: 65.5 us -> 61.8 us  [send(): return lax.ppermute(value, AXES, pairs)]
    ppermute x36, waiting for transfers between devices: 35.1 us -> 37.7 us  [send(): return lax.ppermute(value, AXES, pairs)]
  transfers between devices with their start and end apart: 38 -> 38, of which waited for: 21 -> 22; matrix products, arithmetic and copies ran while one was open for 2% -> 2% of each run, Pallas kernels for 0% -> 0%
where the time goes in v5:
time: 147 us
  starting transfers between devices  71.4 us (49%)
  waiting for transfers between devices  53.5 us (36%)
  Pallas kernels  13.2 us (9%)
  other arithmetic  4.56 us (3%)
  between operations  1.74 us (1%)
  matrix products  1.53 us (1%)
    ppermute x36, starting transfers between devices, send(): return lax.ppermute(value, AXES, pairs)  61.8 us
    ppermute x36, waiting for transfers between devices, send(): return lax.ppermute(value, AXES, pairs)  37.7 us
    all_to_all x1, waiting for transfers between devices, on_device(): panel = lax.all_to_all(spread(features[0], 8), REP, 0, 0)  12.8 us
    pallas_call x1, Pallas kernels, backward_products(): pl.pallas_call(backward_kernel, out_shape=jax.ShapeDtypeStruct((32, BS, B...  6 us
    all_to_all x1, starting transfers between devices, on_device(): panel = lax.all_to_all(spread(features[0], 8), REP, 0, 0)  5.96 us
    pallas_call x1, Pallas kernels, forward_products(): pl.pallas_call(forward_kernel, out_shape=(kept, away, away), in_specs=[sm...  5.21 us
    all_to_all x1, starting transfers between devices, on_device(): parts = lax.all_to_all(columns.reshape(8, 512, BS), REP, 0, 0)  3.66 us
    all_to_all x1, waiting for transfers between devices, on_device(): parts = lax.all_to_all(columns.reshape(8, 512, BS), REP, 0, 0)  2.96 us
  transfers between devices with their start and end apart: 38, of which 22 were waited for; matrix products, arithmetic and copies ran while one was open for 2% of the time, Pallas kernels for 0%

profile of v5, /device:TPU:1, one launch (start us, length us, event | category | flops | bytes accessed | tf_op | source)
XLA Modules:
  0.0 146.7 jit_solution(2742927858480047318)
XLA Ops:
  0.6 2.0 %spread.1 = bf16[8,512,128]{2,1,0:T(8,128)(2,1)} custom-call(bf16[512,128]{1,0:T(8,128)(2,1)} %bitcast.73), custom_call_target="tpu_custom_call" | custom-call | tf_op jit(solution)/shard_map/spread/pallas_call | solution.py:97
  2.6 6.0 %all-to-all-start = ((bf16[8,512,128]{2,1,0:T(8,128)(2,1)}), bf16[8,512,128]{2,1,0:T(8,128)(2,1)S(1)}, u32[]{:S(2)}, u32[]{:S(2)}) async-start(bf16[8,512,128]{2,1,0:T(8,128)(2,1)} %spread.1), calls=%async_computation | async-start | bytes 2097152 | tf_op jit(solution)/shard_map/all_to_all | solution.py:254
  9.3 0.7 reduce
  10.0 0.7 reduce.1.cols_ref
  10.7 12.8 %all-to-all-done = bf16[8,512,128]{2,1,0:T(8,128)(2,1)S(1)} async-done(((bf16[8,512,128]{2,1,0:T(8,128)(2,1)}), bf16[8,512,128]{2,1,0:T(8,128)(2,1)S(1)}, u32[]{:S(2)}, u32[]{:S(2)}) %all-to-all-start) | async-done | bytes 1048608 | tf_op jit(solution)/shard_map/all_to_all | solution.py:254
  23.5 5.2 %forward_products.1 = (bf16[64,128,128]{2,1,0:T(8,128)(2,1)S(1)}, bf16[32,128,128]{2,1,0:T(8,128)(2,1)S(1)}, bf16[32,128,128]{2,1,0:T(8,128)(2,1)S(1)}) custom-call(s32[384]{0:T(512)S(1)} %fusion.26.land_ref, s32[384]{0:T(512)S(1)} %reduce.1.cols_ref, s32[1]{0:T(128)} %bitcast.60.count_ref, bf16[32,128,128]{2,1,0:T(8,128)(2,1)S(1)} %bitcast.63, ...), custom_call_target="tpu_custom_call" | custom-call | flops 1610612736 | bytes 18874368 | tf_op jit(solution)/shard_map/forward_products/pallas_call | solution.py:128
  28.8 2.6 %collective-permute-done = bf16[32,128,128]{2,1,0:T(8,128)(2,1)S(1)} collective-permute-done((bf16[32,128,128]{2,1,0:T(8,128)(2,1)S(1)}, bf16[32,128,128]{2,1,0:T(8,128)(2,1)S(1)}, u32[]{:S(2)}, u32[]{:S(2)}) %collective-permute-start) | collective-permute-done | bytes 1048608 | tf_op jit(solution)/shard_map/ppermute | solution.py:54
  31.5 0.4 add_convert_fusion.1
  32.1 6.4 %collective-permute-start.7 = (bf16[512,128]{1,0:T(8,128)(2,1)S(1)}, bf16[512,128]{1,0:T(8,128)(2,1)S(1)}, u32[]{:S(2)}, u32[]{:S(2)}) collective-permute-start(bf16[512,128]{1,0:T(8,128)(2,1)S(1)} %get-tuple-element.73), channel_id=1, source_target_pairs={{0,4},{1,29},{2,6},{3,31},{4,8},{5,1},{6,10},{7,3},{8,12},{9,5},{1... | collective-permute-start | bytes 393224 | tf_op jit(solution)/shard_map/ppermute | solution.py:54
  38.5 1.9 %collective-permute-done.7 = bf16[512,128]{1,0:T(8,128)(2,1)S(1)} collective-permute-done((bf16[512,128]{1,0:T(8,128)(2,1)S(1)}, bf16[512,128]{1,0:T(8,128)(2,1)S(1)}, u32[]{:S(2)}, u32[]{:S(2)}) %collective-permute-start.7) | collective-permute-done | bytes 131104 | tf_op jit(solution)/shard_map/ppermute | solution.py:54
  40.5 3.2 %collective-permute-start.8 = (bf16[2,512,128]{2,1,0:T(8,128)(2,1)S(1)}, bf16[2,512,128]{2,1,0:T(8,128)(2,1)S(1)}, u32[]{:S(2)}, u32[]{:S(2)}) collective-permute-start(bf16[2,512,128]{2,1,0:T(8,128)(2,1)S(1)} %pad_maximum_fusion.4), channel_id=1, source_target_pairs={{0,4},{1,29},{2,6},{3,31},{4,8},{5,1},{6,10},{7,3},{8,12},{9,5},{1... | collective-permute-start | bytes 786440 | tf_op jit(solution)/shard_map/ppermute | solution.py:54
  43.7 0.4 add_convert_fusion
  44.2 2.8 %collective-permute-done.8 = bf16[2,512,128]{2,1,0:T(8,128)(2,1)S(1)} collective-permute-done((bf16[2,512,128]{2,1,0:T(8,128)(2,1)S(1)}, bf16[2,512,128]{2,1,0:T(8,128)(2,1)S(1)}, u32[]{:S(2)}, u32[]{:S(2)}) %collective-permute-start.8) | collective-permute-done | bytes 262176 | tf_op jit(solution)/shard_map/ppermute | solution.py:54
  47.0 3.2 %collective-permute-start.9 = (bf16[2,512,128]{2,1,0:T(8,128)(2,1)S(1)}, bf16[2,512,128]{2,1,0:T(8,128)(2,1)S(1)}, u32[]{:S(2)}, u32[]{:S(2)}) collective-permute-start(bf16[2,512,128]{2,1,0:T(8,128)(2,1)S(1)} %add_convert_fusion.3), channel_id=1, source_target_pairs={{0,4},{1,29},{2,6},{3,31},{4,8},{5,1},{6,10},{7,3},{8,12},{9,5},{1... | collective-permute-start | bytes 786440 | tf_op jit(solution)/shard_map/ppermute | solution.py:54
  50.3 1.3 collective-permute-start.3
  51.7 1.9 %collective-permute-done.9 = bf16[2,512,128]{2,1,0:T(8,128)(2,1)S(1)} collective-permute-done((bf16[2,512,128]{2,1,0:T(8,128)(2,1)S(1)}, bf16[2,512,128]{2,1,0:T(8,128)(2,1)S(1)}, u32[]{:S(2)}, u32[]{:S(2)}) %collective-permute-start.9) | collective-permute-done | bytes 262176 | tf_op jit(solution)/shard_map/ppermute | solution.py:54
  53.6 3.2 %collective-permute-start.10 = (bf16[2,512,128]{2,1,0:T(8,128)(2,1)S(1)}, bf16[2,512,128]{2,1,0:T(8,128)(2,1)S(1)}, u32[]{:S(2)}, u32[]{:S(2)}) collective-permute-start(bf16[2,512,128]{2,1,0:T(8,128)(2,1)S(1)} %add_convert_fusion.2), channel_id=1, source_target_pairs={{0,4},{1,29},{2,6},{3,31},{4,8},{5,1},{6,10},{7,3},{8,12},{9,5},{1... | collective-permute-start | bytes 786440 | tf_op jit(solution)/shard_map/ppermute | solution.py:54
  57.0 2.7 %collective-permute-start.4 = (bf16[2,512,128]{2,1,0:T(8,128)(2,1)S(1)}, bf16[2,512,128]{2,1,0:T(8,128)(2,1)S(1)}, u32[]{:S(2)}, u32[]{:S(2)}) collective-permute-start(bf16[2,512,128]{2,1,0:T(8,128)(2,1)S(1)} %fusion.1), channel_id=1, source_target_pairs={{0,4},{1,29},{2,6},{3,31},{4,8},{5,1},{6,10},{7,3},{8,12},{9,5},{1... | collective-permute-start | bytes 786440 | tf_op jit(solution)/shard_map/ppermute | solution.py:54
  59.6 0.5 collective-permute-done.10
  60.2 5.0 %collective-permute-start.11 = (bf16[512,128]{1,0:T(8,128)(2,1)S(1)}, bf16[512,128]{1,0:T(8,128)(2,1)S(1)}, u32[]{:S(2)}, u32[]{:S(2)}) collective-permute-start(bf16[512,128]{1,0:T(8,128)(2,1)S(1)} %slice_bitcast_fusion), channel_id=1, source_target_pairs={{0,1},{1,0},{2,3},{3,2},{4,5},{5,4},{6,7},{7,6},{8,9},{9,8},{10,11... | collective-permute-start | bytes 393224 | tf_op jit(solution)/shard_map/ppermute | solution.py:54
  65.2 1.0 collective-permute-start.5
  66.3 1.6 %collective-permute-start.12 = (bf16[512,128]{1,0:T(8,128)(2,1)S(1)}, bf16[512,128]{1,0:T(8,128)(2,1)S(1)}, u32[]{:S(2)}, u32[]{:S(2)}) collective-permute-start(bf16[512,128]{1,0:T(8,128)(2,1)S(1)} %fusion.8), channel_id=1, source_target_pairs={{0,2},{1,3},{2,0},{3,1},{4,6},{5,7},{6,4},{7,5},{8,10},{9,11},{10,... | collective-permute-start | bytes 393224 | tf_op jit(solution)/shard_map/ppermute | solution.py:54
  67.9 2.6 %collective-permute-done.5 = bf16[2,512,128]{2,1,0:T(8,128)(2,1)S(1)} collective-permute-done((bf16[2,512,128]{2,1,0:T(8,128)(2,1)S(1)}, bf16[2,512,128]{2,1,0:T(8,128)(2,1)S(1)}, u32[]{:S(2)}, u32[]{:S(2)}) %collective-permute-start.5) | collective-permute-done | bytes 262176 | tf_op jit(solution)/shard_map/ppermute | solution.py:54
  70.5 5.3 %collective-permute-start.6 = (bf16[512,128]{1,0:T(8,128)(2,1)S(1)}, bf16[512,128]{1,0:T(8,128)(2,1)S(1)}, u32[]{:S(2)}, u32[]{:S(2)}) collective-permute-start(bf16[512,128]{1,0:T(8,128)(2,1)S(1)} %slice_bitcast_fusion.1), channel_id=1, source_target_pairs={{0,1},{1,0},{2,3},{3,2},{4,5},{5,4},{6,7},{7,6},{8,9},{9,8},{10,11... | collective-permute-start | bytes 393224 | tf_op jit(solution)/shard_map/ppermute | solution.py:54
  75.9 1.0 collective-permute-done.6
  77.0 1.1 fusion
  78.1 0.2 convolution_multiply_fusion
  78.6 0.4 collective-permute-start.15
  79.0 1.6 %collective-permute-start.23 = (bf16[512,128]{1,0:T(8,128)(2,1)S(1)}, bf16[512,128]{1,0:T(8,128)(2,1)S(1)}, u32[]{:S(2)}, u32[]{:S(2)}) collective-permute-start(bf16[512,128]{1,0:T(8,128)(2,1)S(1)} %convolution_convert_fusion), channel_id=1, source_target_pairs={{0,2},{1,3},{2,0},{3,1},{4,6},{5,7},{6,4},{7,5},{8,10},{9,11},{10,... | collective-permute-start | bytes 393224 | tf_op jit(solution)/shard_map/ppermute | solution.py:54
  80.6 0.4 collective-permute-start.13
  81.1 1.6 %collective-permute-start.16 = (f32[64,256]{1,0:T(8,128)S(1)}, f32[64,256]{1,0:T(8,128)S(1)}, u32[]{:S(2)}, u32[]{:S(2)}) collective-permute-start(f32[64,256]{1,0:T(8,128)S(1)} %constant_dynamic-slice_fusion.2), channel_id=1, source_target_pairs={{0,128},{1,129},{2,130},{3,131},{4,132},{5,133},{6,134},{7,135},{8... | collective-permute-start | bytes 196616 | tf_op jit(solution)/shard_map/ppermute | solution.py:54
  82.7 0.5 collective-permute-start.14
  83.1 2.3 %collective-permute-done.23 = bf16[512,128]{1,0:T(8,128)(2,1)S(1)} collective-permute-done((bf16[512,128]{1,0:T(8,128)(2,1)S(1)}, bf16[512,128]{1,0:T(8,128)(2,1)S(1)}, u32[]{:S(2)}, u32[]{:S(2)}) %collective-permute-start.23) | collective-permute-done | bytes 131104 | tf_op jit(solution)/shard_map/ppermute | solution.py:54
  85.5 1.3 collective-permute-start.24
  86.9 0.8 collective-permute-done.24
  87.8 0.5 collective-permute-start.25
  88.3 1.3 collective-permute-start.17
  89.6 1.5 collective-permute-start.18
  91.0 2.8 %collective-permute-done.18 = f32[32,256]{1,0:T(8,128)S(1)} collective-permute-done((f32[32,256]{1,0:T(8,128)S(1)}, f32[32,256]{1,0:T(8,128)S(1)}, u32[]{:S(2)}, u32[]{:S(2)}) %collective-permute-start.18) | collective-permute-done | bytes 32800 | tf_op jit(solution)/shard_map/ppermute | solution.py:54
  93.8 0.8 collective-permute-start.26
  94.7 1.5 %collective-permute-done.17 = bf16[1024,128]{1,0:T(8,128)(2,1)S(1)} collective-permute-done((bf16[1024,128]{1,0:T(8,128)(2,1)S(1)}, bf16[1024,128]{1,0:T(8,128)(2,1)S(1)}, u32[]{:S(2)}, u32[]{:S(2)}) %collective-permute-start.17) | collective-permute-done | bytes 262176 | tf_op jit(solution)/shard_map/ppermute | solution.py:54
  96.2 0.6 collective-permute-start.20
  96.8 2.8 %collective-permute-start.29 = (bf16[2048,128]{1,0:T(8,128)(2,1)S(1)}, bf16[2048,128]{1,0:T(8,128)(2,1)S(1)}, u32[]{:S(2)}, u32[]{:S(2)}) collective-permute-start(bf16[2048,128]{1,0:T(8,128)(2,1)S(1)} %pad_maximum_fusion), channel_id=1, source_target_pairs={{0,1},{1,0},{2,3},{3,2},{4,5},{5,4},{6,7},{7,6},{8,9},{9,8},{10,11... | collective-permute-start | bytes 1572872 | tf_op jit(solution)/shard_map/ppermute | solution.py:54
  99.8 1.4 collective-permute-start.27
  101.2 2.5 %collective-permute-start.30 = (bf16[2048,128]{1,0:T(8,128)(2,1)S(1)}, bf16[2048,128]{1,0:T(8,128)(2,1)S(1)}, u32[]{:S(2)}, u32[]{:S(2)}) collective-permute-start(bf16[2048,128]{1,0:T(8,128)(2,1)S(1)} %pad_maximum_fusion.1), channel_id=1, source_target_pairs={{0,1},{1,0},{2,3},{3,2},{4,5},{5,4},{6,7},{7,6},{8,9},{9,8},{10,11... | collective-permute-start | bytes 1572872 | tf_op jit(solution)/shard_map/ppermute | solution.py:54
  103.6 1.5 %collective-permute-done.19 = bf16[1024,128]{1,0:T(8,128)(2,1)S(1)} collective-permute-done((bf16[1024,128]{1,0:T(8,128)(2,1)S(1)}, bf16[1024,128]{1,0:T(8,128)(2,1)S(1)}, u32[]{:S(2)}, u32[]{:S(2)}) %collective-permute-start.19) | collective-permute-done | bytes 262176 | tf_op jit(solution)/shard_map/ppermute | solution.py:54
  105.1 1.8 %collective-permute-start.22 = (f32[16,256]{1,0:T(8,128)S(1)}, f32[16,256]{1,0:T(8,128)S(1)}, u32[]{:S(2)}, u32[]{:S(2)}) collective-permute-start(f32[16,256]{1,0:T(8,128)S(1)} %dynamic-slice_add_fusion.2), channel_id=1, source_target_pairs={{0,2},{1,3},{2,0},{3,1},{4,6},{5,7},{6,4},{7,5},{8,10},{9,11},{10,... | collective-permute-start | bytes 49160 | tf_op jit(solution)/shard_map/ppermute | solution.py:54
  106.9 1.0 collective-permute-done.27
  108.0 3.2 %collective-permute-start.31 = (bf16[2048,128]{1,0:T(8,128)(2,1)S(1)}, bf16[2048,128]{1,0:T(8,128)(2,1)S(1)}, u32[]{:S(2)}, u32[]{:S(2)}) collective-permute-start(bf16[2048,128]{1,0:T(8,128)(2,1)S(1)} %pad_maximum_fusion.2), channel_id=1, source_target_pairs={{0,1},{1,0},{2,3},{3,2},{4,5},{5,4},{6,7},{7,6},{8,9},{9,8},{10,11... | collective-permute-start | bytes 1572872 | tf_op jit(solution)/shard_map/ppermute | solution.py:54
  111.2 0.8 collective-permute-start.21
  112.2 3.2 %collective-permute-done.21 = bf16[512,128]{1,0:T(8,128)(2,1)S(1)} collective-permute-done((bf16[512,128]{1,0:T(8,128)(2,1)S(1)}, bf16[512,128]{1,0:T(8,128)(2,1)S(1)}, u32[]{:S(2)}, u32[]{:S(2)}) %collective-permute-start.21) | collective-permute-done | bytes 131104 | tf_op jit(solution)/shard_map/ppermute | solution.py:54
  115.3 1.7 %collective-permute-done.28 = bf16[512,128]{1,0:T(8,128)(2,1)S(1)} collective-permute-done((bf16[512,128]{1,0:T(8,128)(2,1)S(1)}, bf16[512,128]{1,0:T(8,128)(2,1)S(1)}, u32[]{:S(2)}, u32[]{:S(2)}) %collective-permute-start.28) | collective-permute-done | bytes 131104 | tf_op jit(solution)/shard_map/ppermute | solution.py:54
  117.0 2.2 %collective-permute-start.32 = (bf16[1024,128]{1,0:T(8,128)(2,1)S(1)}, bf16[1024,128]{1,0:T(8,128)(2,1)S(1)}, u32[]{:S(2)}, u32[]{:S(2)}) collective-permute-start(bf16[1024,128]{1,0:T(8,128)(2,1)S(1)} %pad_maximum_fusion.5), channel_id=1, source_target_pairs={{0,1},{1,0},{2,3},{3,2},{4,5},{5,4},{6,7},{7,6},{8,9},{9,8},{10,11... | collective-permute-start | bytes 786440 | tf_op jit(solution)/shard_map/ppermute | solution.py:54
  119.2 1.2 collective-permute-done.32
  121.1 6.0 %backward_products.1 = bf16[32,128,128]{2,1,0:T(8,128)(2,1)} custom-call(s32[384]{0:T(512)S(1)} %get-tuple-element.65.land_ref, s32[384]{0:T(512)S(1)} %reduce.1.cols_ref, s32[1]{0:T(128)} %bitcast.61.count_ref, bf16[128,128,128]{2,1,0:T(8,128)(2,1)S(1)} %bitcast.62, bf16[384,128,128]{2,1,0:T(8,128)(2,1)} %bitcast.65), custom_call_target="tpu_custom_call" | custom-call | flops 1610612736 | bytes 18874368 | tf_op jit(solution)/shard_map/backward_products/pallas_call | solution.py:166
  127.1 3.7 %all-to-all-start.1 = ((bf16[8,512,128]{2,1,0:T(8,128)(2,1)}), bf16[8,512,128]{2,1,0:T(8,128)(2,1)S(1)}, u32[]{:S(2)}, u32[]{:S(2)}) async-start(bf16[8,512,128]{2,1,0:T(8,128)(2,1)} %bitcast.23), calls=%async_computation.1 | async-start | bytes 2097152 | tf_op jit(solution)/shard_map/all_to_all | solution.py:311
  130.8 2.6 %collective-permute-done.33 = f32[16,256]{1,0:T(8,128)S(1)} collective-permute-done((f32[16,256]{1,0:T(8,128)S(1)}, f32[16,256]{1,0:T(8,128)S(1)}, u32[]{:S(2)}, u32[]{:S(2)}) %collective-permute-start.33) | collective-permute-done | bytes 16416 | tf_op jit(solution)/shard_map/ppermute | solution.py:54
  133.4 1.7 %collective-permute-start.34 = (f32[16,256]{1,0:T(8,128)S(1)}, f32[16,256]{1,0:T(8,128)S(1)}, u32[]{:S(2)}, u32[]{:S(2)}) collective-permute-start(f32[16,256]{1,0:T(8,128)S(1)} %add.207), channel_id=1, source_target_pairs={{0,8},{1,9},{2,10},{3,11},{4,12},{5,13},{6,14},{7,15},{8,0},{9,1},... | collective-permute-start | bytes 49160 | tf_op jit(solution)/shard_map/ppermute | solution.py:54
  135.1 2.1 %collective-permute-done.34 = f32[16,256]{1,0:T(8,128)S(1)} collective-permute-done((f32[16,256]{1,0:T(8,128)S(1)}, f32[16,256]{1,0:T(8,128)S(1)}, u32[]{:S(2)}, u32[]{:S(2)}) %collective-permute-start.34) | collective-permute-done | bytes 16416 | tf_op jit(solution)/shard_map/ppermute | solution.py:54
  137.2 1.5 %collective-permute-start.35 = (f32[16,256]{1,0:T(8,128)S(1)}, f32[16,256]{1,0:T(8,128)S(1)}, u32[]{:S(2)}, u32[]{:S(2)}) collective-permute-start(f32[16,256]{1,0:T(8,128)S(1)} %add.208), channel_id=1, source_target_pairs={{0,24},{1,25},{2,26},{3,27},{4,28},{5,29},{6,30},{7,31},{8,16},{9,... | collective-permute-start | bytes 49160 | tf_op jit(solution)/shard_map/ppermute | solution.py:54
  138.7 3.5 %collective-permute-done.35 = f32[16,256]{1,0:T(8,128)S(1)} collective-permute-done((f32[16,256]{1,0:T(8,128)S(1)}, f32[16,256]{1,0:T(8,128)S(1)}, u32[]{:S(2)}, u32[]{:S(2)}) %collective-permute-start.35) | collective-permute-done | bytes 16416 | tf_op jit(solution)/shard_map/ppermute | solution.py:54
  142.2 0.6 add.209
  142.8 3.0 %all-to-all-done.1 = bf16[8,512,128]{2,1,0:T(8,128)(2,1)S(1)} async-done(((bf16[8,512,128]{2,1,0:T(8,128)(2,1)}), bf16[8,512,128]{2,1,0:T(8,128)(2,1)S(1)}, u32[]{:S(2)}, u32[]{:S(2)}) %all-to-all-start.1) | async-done | bytes 1048608 | tf_op jit(solution)/shard_map/all_to_all | solution.py:311
  145.9 0.8 fusion.10
  (88 shorter events, 2.9 us)
Async XLA Ops:
  0.6 76.4 %copy-start = (bf16[128,256]{1,0:T(8,128)(2,1)S(1)}, bf16[128,256]{1,0:T(8,128)(2,1)}, u32[]{:S(2)}) copy-start(bf16[128,256]{1,0:T(8,128)(2,1)} %param.9) | copy-start | bytes 196612
  2.6 20.9 %all-to-all-start = ((bf16[8,512,128]{2,1,0:T(8,128)(2,1)}), bf16[8,512,128]{2,1,0:T(8,128)(2,1)S(1)}, u32[]{:S(2)}, u32[]{:S(2)}) async-start(bf16[8,512,128]{2,1,0:T(8,128)(2,1)} %spread.1), calls=%async_computation | async-start | bytes 2097152 | tf_op jit(solution)/shard_map/all_to_all | solution.py:254
  28.7 2.7 %collective-permute-start = (bf16[32,128,128]{2,1,0:T(8,128)(2,1)S(1)}, bf16[32,128,128]{2,1,0:T(8,128)(2,1)S(1)}, u32[]{:S(2)}, u32[]{:S(2)}) collective-permute-start(bf16[32,128,128]{2,1,0:T(8,128)(2,1)S(1)} %get-tuple-element.36), channel_id=1, source_target_pairs={{0,1},{1,0},{2,3},{3,2},{4,5},{5,4},{6,7},{7,6},{8,9},{9,8},{10,11... | collective-permute-start | bytes 3145736 | tf_op jit(solution)/shard_map/ppermute | solution.py:54
  31.9 11.8 %collective-permute-start.1 = (bf16[32,128,128]{2,1,0:T(8,128)(2,1)S(1)}, bf16[32,128,128]{2,1,0:T(8,128)(2,1)S(1)}, u32[]{:S(2)}, u32[]{:S(2)}) collective-permute-start(bf16[32,128,128]{2,1,0:T(8,128)(2,1)S(1)} %get-tuple-element.37), channel_id=1, source_target_pairs={{0,1},{1,0},{2,3},{3,2},{4,5},{5,4},{6,7},{7,6},{8,9},{9,8},{10,11... | collective-permute-start | bytes 3145736 | tf_op jit(solution)/shard_map/ppermute | solution.py:54
  32.1 8.3 %collective-permute-start.7 = (bf16[512,128]{1,0:T(8,128)(2,1)S(1)}, bf16[512,128]{1,0:T(8,128)(2,1)S(1)}, u32[]{:S(2)}, u32[]{:S(2)}) collective-permute-start(bf16[512,128]{1,0:T(8,128)(2,1)S(1)} %get-tuple-element.73), channel_id=1, source_target_pairs={{0,4},{1,29},{2,6},{3,31},{4,8},{5,1},{6,10},{7,3},{8,12},{9,5},{1... | collective-permute-start | bytes 393224 | tf_op jit(solution)/shard_map/ppermute | solution.py:54
  40.5 6.5 %collective-permute-start.8 = (bf16[2,512,128]{2,1,0:T(8,128)(2,1)S(1)}, bf16[2,512,128]{2,1,0:T(8,128)(2,1)S(1)}, u32[]{:S(2)}, u32[]{:S(2)}) collective-permute-start(bf16[2,512,128]{2,1,0:T(8,128)(2,1)S(1)} %pad_maximum_fusion.4), channel_id=1, source_target_pairs={{0,4},{1,29},{2,6},{3,31},{4,8},{5,1},{6,10},{7,3},{8,12},{9,5},{1... | collective-permute-start | bytes 786440 | tf_op jit(solution)/shard_map/ppermute | solution.py:54
  44.0 32.8 %copy-start.1 = (bf16[1,512,128]{2,1,0:T(8,128)(2,1)S(1)}, bf16[1,512,128]{2,1,0:T(8,128)(2,1)}, u32[]{:S(2)}) copy-start(bf16[1,512,128]{2,1,0:T(8,128)(2,1)} %param.8) | copy-start | bytes 393220
  44.0 32.8 %copy-start.2 = (f32[1,512]{1,0:T(1,128)S(1)}, f32[1,512]{1,0:T(1,128)}, u32[]{:S(2)}) copy-start(f32[1,512]{1,0:T(1,128)} %param.11) | copy-start | bytes 6148
  44.1 33.0 %copy-start.3 = (bf16[1,512,256]{2,1,0:T(8,128)(2,1)S(1)}, bf16[1,512,256]{2,1,0:T(8,128)(2,1)}, u32[]{:S(2)}) copy-start(bf16[1,512,256]{2,1,0:T(8,128)(2,1)} %param.10) | copy-start | bytes 786436
  44.1 6.1 %collective-permute-start.2 = (bf16[512,128]{1,0:T(8,128)(2,1)S(1)}, bf16[512,128]{1,0:T(8,128)(2,1)S(1)}, u32[]{:S(2)}, u32[]{:S(2)}) collective-permute-start(bf16[512,128]{1,0:T(8,128)(2,1)S(1)} %bitcast.75), channel_id=1, source_target_pairs={{0,4},{1,29},{2,6},{3,31},{4,8},{5,1},{6,10},{7,3},{8,12},{9,5},{1... | collective-permute-start | bytes 393224 | tf_op jit(solution)/shard_map/ppermute | solution.py:54
  47.0 6.5 %collective-permute-start.9 = (bf16[2,512,128]{2,1,0:T(8,128)(2,1)S(1)}, bf16[2,512,128]{2,1,0:T(8,128)(2,1)S(1)}, u32[]{:S(2)}, u32[]{:S(2)}) collective-permute-start(bf16[2,512,128]{2,1,0:T(8,128)(2,1)S(1)} %add_convert_fusion.3), channel_id=1, source_target_pairs={{0,4},{1,29},{2,6},{3,31},{4,8},{5,1},{6,10},{7,3},{8,12},{9,5},{1... | collective-permute-start | bytes 786440 | tf_op jit(solution)/shard_map/ppermute | solution.py:54
  50.3 6.5 %collective-permute-start.3 = (bf16[2,512,128]{2,1,0:T(8,128)(2,1)S(1)}, bf16[2,512,128]{2,1,0:T(8,128)(2,1)S(1)}, u32[]{:S(2)}, u32[]{:S(2)}) collective-permute-start(bf16[2,512,128]{2,1,0:T(8,128)(2,1)S(1)} %pad_maximum_fusion.3), channel_id=1, source_target_pairs={{0,4},{1,29},{2,6},{3,31},{4,8},{5,1},{6,10},{7,3},{8,12},{9,5},{1... | collective-permute-start | bytes 786440 | tf_op jit(solution)/shard_map/ppermute | solution.py:54
  53.6 6.5 %collective-permute-start.10 = (bf16[2,512,128]{2,1,0:T(8,128)(2,1)S(1)}, bf16[2,512,128]{2,1,0:T(8,128)(2,1)S(1)}, u32[]{:S(2)}, u32[]{:S(2)}) collective-permute-start(bf16[2,512,128]{2,1,0:T(8,128)(2,1)S(1)} %add_convert_fusion.2), channel_id=1, source_target_pairs={{0,4},{1,29},{2,6},{3,31},{4,8},{5,1},{6,10},{7,3},{8,12},{9,5},{1... | collective-permute-start | bytes 786440 | tf_op jit(solution)/shard_map/ppermute | solution.py:54
  57.0 8.2 %collective-permute-start.4 = (bf16[2,512,128]{2,1,0:T(8,128)(2,1)S(1)}, bf16[2,512,128]{2,1,0:T(8,128)(2,1)S(1)}, u32[]{:S(2)}, u32[]{:S(2)}) collective-permute-start(bf16[2,512,128]{2,1,0:T(8,128)(2,1)S(1)} %fusion.1), channel_id=1, source_target_pairs={{0,4},{1,29},{2,6},{3,31},{4,8},{5,1},{6,10},{7,3},{8,12},{9,5},{1... | collective-permute-start | bytes 786440 | tf_op jit(solution)/shard_map/ppermute | solution.py:54
  60.2 6.1 %collective-permute-start.11 = (bf16[512,128]{1,0:T(8,128)(2,1)S(1)}, bf16[512,128]{1,0:T(8,128)(2,1)S(1)}, u32[]{:S(2)}, u32[]{:S(2)}) collective-permute-start(bf16[512,128]{1,0:T(8,128)(2,1)S(1)} %slice_bitcast_fusion), channel_id=1, source_target_pairs={{0,1},{1,0},{2,3},{3,2},{4,5},{5,4},{6,7},{7,6},{8,9},{9,8},{10,11... | collective-permute-start | bytes 393224 | tf_op jit(solution)/shard_map/ppermute | solution.py:54
  65.2 5.3 %collective-permute-start.5 = (bf16[2,512,128]{2,1,0:T(8,128)(2,1)S(1)}, bf16[2,512,128]{2,1,0:T(8,128)(2,1)S(1)}, u32[]{:S(2)}, u32[]{:S(2)}) collective-permute-start(bf16[2,512,128]{2,1,0:T(8,128)(2,1)S(1)} %fusion.2), channel_id=1, source_target_pairs={{0,4},{1,29},{2,6},{3,31},{4,8},{5,1},{6,10},{7,3},{8,12},{9,5},{1... | collective-permute-start | bytes 786440 | tf_op jit(solution)/shard_map/ppermute | solution.py:54
  66.3 9.6 %collective-permute-start.12 = (bf16[512,128]{1,0:T(8,128)(2,1)S(1)}, bf16[512,128]{1,0:T(8,128)(2,1)S(1)}, u32[]{:S(2)}, u32[]{:S(2)}) collective-permute-start(bf16[512,128]{1,0:T(8,128)(2,1)S(1)} %fusion.8), channel_id=1, source_target_pairs={{0,2},{1,3},{2,0},{3,1},{4,6},{5,7},{6,4},{7,5},{8,10},{9,11},{10,... | collective-permute-start | bytes 393224 | tf_op jit(solution)/shard_map/ppermute | solution.py:54
  70.5 6.3 %collective-permute-start.6 = (bf16[512,128]{1,0:T(8,128)(2,1)S(1)}, bf16[512,128]{1,0:T(8,128)(2,1)S(1)}, u32[]{:S(2)}, u32[]{:S(2)}) collective-permute-start(bf16[512,128]{1,0:T(8,128)(2,1)S(1)} %slice_bitcast_fusion.1), channel_id=1, source_target_pairs={{0,1},{1,0},{2,3},{3,2},{4,5},{5,4},{6,7},{7,6},{8,9},{9,8},{10,11... | collective-permute-start | bytes 393224 | tf_op jit(solution)/shard_map/ppermute | solution.py:54
  78.6 2.5 %collective-permute-start.15 = (f32[128,256]{1,0:T(8,128)S(1)}, f32[128,256]{1,0:T(8,128)S(1)}, u32[]{:S(2)}, u32[]{:S(2)}) collective-permute-start(f32[128,256]{1,0:T(8,128)S(1)} %convolution_multiply_fusion), channel_id=1, source_target_pairs={{0,1},{1,0},{2,3},{3,2},{4,5},{5,4},{6,7},{7,6},{8,9},{9,8},{10,11... | collective-permute-start | bytes 393224 | tf_op jit(solution)/shard_map/ppermute | solution.py:54
  79.0 6.5 %collective-permute-start.23 = (bf16[512,128]{1,0:T(8,128)(2,1)S(1)}, bf16[512,128]{1,0:T(8,128)(2,1)S(1)}, u32[]{:S(2)}, u32[]{:S(2)}) collective-permute-start(bf16[512,128]{1,0:T(8,128)(2,1)S(1)} %convolution_convert_fusion), channel_id=1, source_target_pairs={{0,2},{1,3},{2,0},{3,1},{4,6},{5,7},{6,4},{7,5},{8,10},{9,11},{10,... | collective-permute-start | bytes 393224 | tf_op jit(solution)/shard_map/ppermute | solution.py:54
  80.6 2.1 %collective-permute-start.13 = (bf16[512,128]{1,0:T(8,128)(2,1)S(1)}, bf16[512,128]{1,0:T(8,128)(2,1)S(1)}, u32[]{:S(2)}, u32[]{:S(2)}) collective-permute-start(bf16[512,128]{1,0:T(8,128)(2,1)S(1)} %convolution_convert_fusion), channel_id=1, source_target_pairs={{0,1},{1,0},{2,3},{3,2},{4,5},{5,4},{6,7},{7,6},{8,9},{9,8},{10,11... | collective-permute-start | bytes 393224 | tf_op jit(solution)/shard_map/ppermute | solution.py:54
  81.1 5.8 %collective-permute-start.16 = (f32[64,256]{1,0:T(8,128)S(1)}, f32[64,256]{1,0:T(8,128)S(1)}, u32[]{:S(2)}, u32[]{:S(2)}) collective-permute-start(f32[64,256]{1,0:T(8,128)S(1)} %constant_dynamic-slice_fusion.2), channel_id=1, source_target_pairs={{0,128},{1,129},{2,130},{3,131},{4,132},{5,133},{6,134},{7,135},{8... | collective-permute-start | bytes 196616 | tf_op jit(solution)/shard_map/ppermute | solution.py:54
  82.7 5.6 %collective-permute-start.14 = (bf16[1024,128]{1,0:T(8,128)(2,1)S(1)}, bf16[1024,128]{1,0:T(8,128)(2,1)S(1)}, u32[]{:S(2)}, u32[]{:S(2)}) collective-permute-start(bf16[1024,128]{1,0:T(8,128)(2,1)S(1)} %constant_dynamic-update-slice_fusion), channel_id=1, source_target_pairs={{0,4},{1,29},{2,6},{3,31},{4,8},{5,1},{6,10},{7,3},{8,12},{9,5},{1... | collective-permute-start | bytes 786440 | tf_op jit(solution)/shard_map/ppermute | solution.py:54
  85.5 2.3 %collective-permute-start.24 = (bf16[512,128]{1,0:T(8,128)(2,1)S(1)}, bf16[512,128]{1,0:T(8,128)(2,1)S(1)}, u32[]{:S(2)}, u32[]{:S(2)}) collective-permute-start(bf16[512,128]{1,0:T(8,128)(2,1)S(1)} %collective-permute-done.23), channel_id=1, source_target_pairs={{0,1},{1,0},{2,3},{3,2},{4,5},{5,4},{6,7},{7,6},{8,9},{9,8},{10,11... | collective-permute-start | bytes 393224 | tf_op jit(solution)/shard_map/ppermute | solution.py:54
  87.8 6.0 %collective-permute-start.25 = (bf16[1024,128]{1,0:T(8,128)(2,1)S(1)}, bf16[1024,128]{1,0:T(8,128)(2,1)S(1)}, u32[]{:S(2)}, u32[]{:S(2)}) collective-permute-start(bf16[1024,128]{1,0:T(8,128)(2,1)S(1)} %constant_dynamic-update-slice_fusion.2), channel_id=1, source_target_pairs={{0,4},{1,29},{2,6},{3,31},{4,8},{5,1},{6,10},{7,3},{8,12},{9,5},{1... | collective-permute-start | bytes 786440 | tf_op jit(solution)/shard_map/ppermute | solution.py:54
  88.3 7.9 %collective-permute-start.17 = (bf16[1024,128]{1,0:T(8,128)(2,1)S(1)}, bf16[1024,128]{1,0:T(8,128)(2,1)S(1)}, u32[]{:S(2)}, u32[]{:S(2)}) collective-permute-start(bf16[1024,128]{1,0:T(8,128)(2,1)S(1)} %collective-permute-done.14), channel_id=1, source_target_pairs={{0,4},{1,29},{2,6},{3,31},{4,8},{5,1},{6,10},{7,3},{8,12},{9,5},{1... | collective-permute-start | bytes 786440 | tf_op jit(solution)/shard_map/ppermute | solution.py:54
  89.6 4.3 %collective-permute-start.18 = (f32[32,256]{1,0:T(8,128)S(1)}, f32[32,256]{1,0:T(8,128)S(1)}, u32[]{:S(2)}, u32[]{:S(2)}) collective-permute-start(f32[32,256]{1,0:T(8,128)S(1)} %constant_dynamic-slice_fusion.1), channel_id=1, source_target_pairs={{0,96},{1,97},{2,98},{3,99},{4,100},{5,101},{6,102},{7,103},{8,104... | collective-permute-start | bytes 98312 | tf_op jit(solution)/shard_map/ppermute | solution.py:54
  93.8 5.9 %collective-permute-start.26 = (bf16[1024,128]{1,0:T(8,128)(2,1)S(1)}, bf16[1024,128]{1,0:T(8,128)(2,1)S(1)}, u32[]{:S(2)}, u32[]{:S(2)}) collective-permute-start(bf16[1024,128]{1,0:T(8,128)(2,1)S(1)} %collective-permute-done.25), channel_id=1, source_target_pairs={{0,4},{1,29},{2,6},{3,31},{4,8},{5,1},{6,10},{7,3},{8,12},{9,5},{1... | collective-permute-start | bytes 786440 | tf_op jit(solution)/shard_map/ppermute | solution.py:54
  96.2 4.9 %collective-permute-start.20 = (f32[16,256]{1,0:T(8,128)S(1)}, f32[16,256]{1,0:T(8,128)S(1)}, u32[]{:S(2)}, u32[]{:S(2)}) collective-permute-start(f32[16,256]{1,0:T(8,128)S(1)} %constant_dynamic-slice_fusion), channel_id=1, source_target_pairs={{0,32},{1,33},{2,34},{3,35},{4,36},{5,37},{6,38},{7,39},{8,40},{9,... | collective-permute-start | bytes 49160 | tf_op jit(solution)/shard_map/ppermute | solution.py:54
  96.8 22.4 %collective-permute-start.29 = (bf16[2048,128]{1,0:T(8,128)(2,1)S(1)}, bf16[2048,128]{1,0:T(8,128)(2,1)S(1)}, u32[]{:S(2)}, u32[]{:S(2)}) collective-permute-start(bf16[2048,128]{1,0:T(8,128)(2,1)S(1)} %pad_maximum_fusion), channel_id=1, source_target_pairs={{0,1},{1,0},{2,3},{3,2},{4,5},{5,4},{6,7},{7,6},{8,9},{9,8},{10,11... | collective-permute-start | bytes 1572872 | tf_op jit(solution)/shard_map/ppermute | solution.py:54
  99.6 5.5 %collective-permute-start.19 = (bf16[1024,128]{1,0:T(8,128)(2,1)S(1)}, bf16[1024,128]{1,0:T(8,128)(2,1)S(1)}, u32[]{:S(2)}, u32[]{:S(2)}) collective-permute-start(bf16[1024,128]{1,0:T(8,128)(2,1)S(1)} %collective-permute-done.17), channel_id=1, source_target_pairs={{0,4},{1,29},{2,6},{3,31},{4,8},{5,1},{6,10},{7,3},{8,12},{9,5},{1... | collective-permute-start | bytes 786440 | tf_op jit(solution)/shard_map/ppermute | solution.py:54
  99.8 8.2 %collective-permute-start.27 = (bf16[1024,128]{1,0:T(8,128)(2,1)S(1)}, bf16[1024,128]{1,0:T(8,128)(2,1)S(1)}, u32[]{:S(2)}, u32[]{:S(2)}) collective-permute-start(bf16[1024,128]{1,0:T(8,128)(2,1)S(1)} %collective-permute-done.26), channel_id=1, source_target_pairs={{0,4},{1,29},{2,6},{3,31},{4,8},{5,1},{6,10},{7,3},{8,12},{9,5},{1... | collective-permute-start | bytes 786440 | tf_op jit(solution)/shard_map/ppermute | solution.py:54
  101.2 18.1 %collective-permute-start.30 = (bf16[2048,128]{1,0:T(8,128)(2,1)S(1)}, bf16[2048,128]{1,0:T(8,128)(2,1)S(1)}, u32[]{:S(2)}, u32[]{:S(2)}) collective-permute-start(bf16[2048,128]{1,0:T(8,128)(2,1)S(1)} %pad_maximum_fusion.1), channel_id=1, source_target_pairs={{0,1},{1,0},{2,3},{3,2},{4,5},{5,4},{6,7},{7,6},{8,9},{9,8},{10,11... | collective-permute-start | bytes 1572872 | tf_op jit(solution)/shard_map/ppermute | solution.py:54
  105.1 6.9 %collective-permute-start.22 = (f32[16,256]{1,0:T(8,128)S(1)}, f32[16,256]{1,0:T(8,128)S(1)}, u32[]{:S(2)}, u32[]{:S(2)}) collective-permute-start(f32[16,256]{1,0:T(8,128)S(1)} %dynamic-slice_add_fusion.2), channel_id=1, source_target_pairs={{0,2},{1,3},{2,0},{3,1},{4,6},{5,7},{6,4},{7,5},{8,10},{9,11},{10,... | collective-permute-start | bytes 49160 | tf_op jit(solution)/shard_map/ppermute | solution.py:54
  108.0 12.4 %collective-permute-start.31 = (bf16[2048,128]{1,0:T(8,128)(2,1)S(1)}, bf16[2048,128]{1,0:T(8,128)(2,1)S(1)}, u32[]{:S(2)}, u32[]{:S(2)}) collective-permute-start(bf16[2048,128]{1,0:T(8,128)(2,1)S(1)} %pad_maximum_fusion.2), channel_id=1, source_target_pairs={{0,1},{1,0},{2,3},{3,2},{4,5},{5,4},{6,7},{7,6},{8,9},{9,8},{10,11... | collective-permute-start | bytes 1572872 | tf_op jit(solution)/shard_map/ppermute | solution.py:54
  111.2 4.1 %collective-permute-start.21 = (bf16[512,128]{1,0:T(8,128)(2,1)S(1)}, bf16[512,128]{1,0:T(8,128)(2,1)S(1)}, u32[]{:S(2)}, u32[]{:S(2)}) collective-permute-start(bf16[512,128]{1,0:T(8,128)(2,1)S(1)} %slice.87), channel_id=1, source_target_pairs={{0,4},{1,29},{2,6},{3,31},{4,8},{5,1},{6,10},{7,3},{8,12},{9,5},{1... | collective-permute-start | bytes 393224 | tf_op jit(solution)/shard_map/ppermute | solution.py:54
  112.1 5.0 %collective-permute-start.28 = (bf16[512,128]{1,0:T(8,128)(2,1)S(1)}, bf16[512,128]{1,0:T(8,128)(2,1)S(1)}, u32[]{:S(2)}, u32[]{:S(2)}) collective-permute-start(bf16[512,128]{1,0:T(8,128)(2,1)S(1)} %slice.99), channel_id=1, source_target_pairs={{0,4},{1,29},{2,6},{3,31},{4,8},{5,1},{6,10},{7,3},{8,12},{9,5},{1... | collective-permute-start | bytes 393224 | tf_op jit(solution)/shard_map/ppermute | solution.py:54
  117.0 3.3 %collective-permute-start.32 = (bf16[1024,128]{1,0:T(8,128)(2,1)S(1)}, bf16[1024,128]{1,0:T(8,128)(2,1)S(1)}, u32[]{:S(2)}, u32[]{:S(2)}) collective-permute-start(bf16[1024,128]{1,0:T(8,128)(2,1)S(1)} %pad_maximum_fusion.5), channel_id=1, source_target_pairs={{0,1},{1,0},{2,3},{3,2},{4,5},{5,4},{6,7},{7,6},{8,9},{9,8},{10,11... | collective-permute-start | bytes 786440 | tf_op jit(solution)/shard_map/ppermute | solution.py:54
  127.1 18.7 %all-to-all-start.1 = ((bf16[8,512,128]{2,1,0:T(8,128)(2,1)}), bf16[8,512,128]{2,1,0:T(8,128)(2,1)S(1)}, u32[]{:S(2)}, u32[]{:S(2)}) async-start(bf16[8,512,128]{2,1,0:T(8,128)(2,1)} %bitcast.23), calls=%async_computation.1 | async-start | bytes 2097152 | tf_op jit(solution)/shard_map/all_to_all | solution.py:311
  130.8 2.6 %collective-permute-start.33 = (f32[16,256]{1,0:T(8,128)S(1)}, f32[16,256]{1,0:T(8,128)S(1)}, u32[]{:S(2)}, u32[]{:S(2)}) collective-permute-start(f32[16,256]{1,0:T(8,128)S(1)} %add.205), channel_id=1, source_target_pairs={{0,4},{1,5},{2,6},{3,7},{4,0},{5,1},{6,2},{7,3},{8,12},{9,13},{10,... | collective-permute-start | bytes 49160 | tf_op jit(solution)/shard_map/ppermute | solution.py:54
  133.4 3.8 %collective-permute-start.34 = (f32[16,256]{1,0:T(8,128)S(1)}, f32[16,256]{1,0:T(8,128)S(1)}, u32[]{:S(2)}, u32[]{:S(2)}) collective-permute-start(f32[16,256]{1,0:T(8,128)S(1)} %add.207), channel_id=1, source_target_pairs={{0,8},{1,9},{2,10},{3,11},{4,12},{5,13},{6,14},{7,15},{8,0},{9,1},... | collective-permute-start | bytes 49160 | tf_op jit(solution)/shard_map/ppermute | solution.py:54
  137.2 5.0 %collective-permute-start.35 = (f32[16,256]{1,0:T(8,128)S(1)}, f32[16,256]{1,0:T(8,128)S(1)}, u32[]{:S(2)}, u32[]{:S(2)}) collective-permute-start(f32[16,256]{1,0:T(8,128)S(1)} %add.208), channel_id=1, source_target_pairs={{0,24},{1,25},{2,26},{3,27},{4,28},{5,29},{6,30},{7,31},{8,16},{9,... | collective-permute-start | bytes 49160 | tf_op jit(solution)/shard_map/ppermute | solution.py:54
